TPU v7x, 32 devices: a whole 2x2x4 slice. The times are simulated.
32 devices in a mesh: dp: 8 (over z, x), ctx: 4 (over y, core).
Axes of the slice: x: 2, y: 2, z: 4, core: 2. Of those that a mesh axis runs over, the one named last changes fastest.
Arguments:
- inputs: bfloat16 [2, 8, 1024, 1024], P(None, 'dp', 'ctx'), may hold values from -6 to 6
- cotangent: bfloat16 [2, 8, 1024, 1024], P(None, 'dp', 'ctx'), may hold values from -6 to 6
- image_lengths: int32 [2, 8, 16], P(None, 'dp'), may hold values from 0 to 1024, as said below
- norm1_gain: bfloat16 [1024], replicated, may hold values from 0.25 to 1.75
- norm1_bias: bfloat16 [1024], replicated, may hold values from -1 to 1
- qkv_weight: bfloat16 [1024, 3072], replicated, may hold values from -0.1875 to 0.1875
- qv_bias: bfloat16 [2, 1024], replicated, may hold values from -1.5 to 1.5
- out_weight: bfloat16 [1024, 1024], replicated, may hold values from -0.75 to 0.75
- out_bias: bfloat16 [1024], replicated, may hold values from -1 to 1
- norm2_gain: bfloat16 [1024], replicated, may hold values from 0.25 to 1.75
- norm2_bias: bfloat16 [1024], replicated, may hold values from -1 to 1
- up_weight: bfloat16 [1024, 4096], replicated, may hold values from -0.1875 to 0.1875
- up_bias: bfloat16 [4096], replicated, may hold values from -1.5 to 1.5
- down_weight: bfloat16 [4096, 1024], replicated, may hold values from -0.09375 to 0.09375
- down_bias: bfloat16 [1024], replicated, may hold values from -1 to 1
Outputs:
- block_output: bfloat16 [2, 8, 1024, 1024], P(None, 'dp', 'ctx')
- input_grad: bfloat16 [2, 8, 1024, 1024], P(None, 'dp', 'ctx')
- grad_norm1_gain: float32 [1024], P(('dp', 'ctx'))
- grad_norm1_bias: float32 [1024], P(('dp', 'ctx'))
- grad_qkv_weight: float32 [1024, 3072], P(('dp', 'ctx'))
- grad_qv_bias: float32 [2, 1024], P(None, ('dp', 'ctx'))
- grad_out_weight: float32 [1024, 1024], P(('dp', 'ctx'))
- grad_out_bias: float32 [1024], P(('dp', 'ctx'))
- grad_norm2_gain: float32 [1024], P(('dp', 'ctx'))
- grad_norm2_bias: float32 [1024], P(('dp', 'ctx'))
- grad_up_weight: float32 [1024, 4096], P(('dp', 'ctx'))
- grad_up_bias: float32 [4096], P(('dp', 'ctx'))
- grad_down_weight: float32 [4096, 1024], P(('dp', 'ctx'))
- grad_down_bias: float32 [1024], P(('dp', 'ctx'))
Inputs may be any that keep to these rules, and one draw needn't show every extreme that they name: `image_lengths`: in each row the lengths are positive up to the row's last image and zero after it; they sum to 1024 or less, and the rest of the sequence is padding.
All inputs are finite; a program needn't handle non-finite values.
Results may differ from a plain program's by a relative error of at most 0.015.
Values may be sent and summed in bfloat16 or wider, within the bound.
No kernel may reach another device: no remote copies, remote signals or barrier semaphores. Data moves between devices by JAX's collectives and lax.ppermute only.
A program may use at most 256 MiB of HBM per device.

v0:
```python
import functools

import jax
import jax.numpy as jnp
from jax import lax
from jax.experimental import pallas as pl
from jax.experimental.pallas import tpu as pltpu
from jax.sharding import PartitionSpec as P

HEADS = 16
HEAD_DIM = 64
PAIR = 2 * HEAD_DIM
NEG = -1e30
EPS = 1e-06
LOG2E = 1.4426950408889634
SCALE = HEAD_DIM ** (-0.5)
BF16 = jnp.bfloat16
F32 = jnp.float32
VMEM = 60 * 1024 * 1024
LESS_VMEM = 32 * 1024 * 1024
DH_PIECES = 4

NT = (((1,), (1,)), ((), ()))
NN = (((1,), (0,)), ((), ()))
TN = (((0,), (0,)), ((), ()))


def dot(left, right, dims=NN):
    return lax.dot_general(left, right, dims, preferred_element_type=F32)


def call(kernel, name, place, args, grid, in_specs, outs, scratch=(), after=(), fill=(), vmem=LESS_VMEM):
    known = len(args)
    skipped = len(after) + len(fill)
    stays = [len(out) > 3 and bool(out[3]) for out in outs]

    def settled(array):
        pinned = any(array is other for other in place.pinned)
        return pltpu.with_memory_space_constraint(array, pltpu.VMEM if pinned else pltpu.HBM)

    def inner(place_ref, *refs):
        kernel(place_ref, *refs[:known], *refs[known + skipped :])

    anywhere = pl.BlockSpec(memory_space=pl.ANY)
    first = 1 + known + len(after)
    results = pl.pallas_call(
        inner,
        grid_spec=pltpu.PrefetchScalarGridSpec(
            num_scalar_prefetch=1,
            grid=grid,
            in_specs=list(in_specs) + [anywhere] * skipped,
            out_specs=[out[2] for out in outs],
            scratch_shapes=list(scratch),
        ),
        out_shape=[(pltpu.VMEM if stay else pltpu.HBM)(out[0], out[1]) for out, stay in zip(outs, stays)],
        input_output_aliases={first + index: index for index in range(len(fill))},
        compiler_params=pltpu.CompilerParams(vmem_limit_bytes=vmem),
        cost_estimate=pl.CostEstimate(flops=int(2*1.15e9) if name=="step" else 0, bytes_accessed=0, transcendentals=0),
        name=name,
    )(place.numbers, *[settled(array) for array in (*args, *after, *fill)])
    place.pinned += [array for array, stay in zip(results, stays) if stay]
    return results


class Place:
    def __init__(self, numbers):
        self.numbers = numbers
        self.pinned = []


def without_bit(number, spot):
    return ((number >> (spot + 1)) << spot) | (number & ((1 << spot) - 1))


def deal(stage_ref, me, pieces):
    for relative in range(stage_ref.shape[0]):
        rows = stage_ref[jnp.bitwise_xor(jnp.int32(relative), me)]
        for keep_ref, send_ref, bit, columns in pieces:
            target = send_ref if (relative >> bit) & 1 else keep_ref
            target[without_bit(relative, bit)] = rows[:, columns]


def norm_parts(values):
    centred = values - jnp.mean(values, axis=-1, keepdims=True)
    inverse = lax.rsqrt(jnp.mean(centred * centred, axis=-1, keepdims=True) + EPS)
    return centred * inverse, inverse


def norm_back(grad, normal, inverse, gain):
    scaled = grad * gain
    inner = (
        scaled
        - jnp.mean(scaled, axis=-1, keepdims=True)
        - normal * jnp.mean(scaled * normal, axis=-1, keepdims=True)
    )
    return inverse * inner


def step_kernel(jobs, place, *refs):
    ins = sum(len(layout) for _, layout in jobs) * 2
    sources = refs[:ins]
    targets = refs[ins:]
    for job, (spot, layout) in enumerate(jobs):
        keep_ref, send_ref = targets[2 * job : 2 * job + 2]
        columns = keep_ref.shape[2]
        base = 0
        for rows, width in layout:
            old_ref, came_ref = sources[:2]
            sources = sources[2:]
            for number in range(old_ref.shape[0]):
                value = (old_ref[number].astype(F32) + came_ref[number].astype(F32)).astype(keep_ref.dtype)
                target = send_ref if (number >> spot) & 1 else keep_ref
                spare = without_bit(number, spot)
                for part in range(width // columns):
                    start = base + part * rows
                    target[spare, start : start + rows] = value[:, part * columns : (part + 1) * columns]
            base += rows * (width // columns)


def step_call(place, jobs, after=()):
    ins = []
    outs = []
    layouts = []
    for arrays, spot in jobs:
        columns = min(array.shape[2] for array in arrays)
        layout = [array.shape[1:] for array in arrays[::2]]
        rows = sum(rows * (width // columns) for rows, width in layout)
        shape = (arrays[0].shape[0] // 2, rows, columns)
        layouts.append((spot, layout))
        ins += arrays
        outs += [(shape, arrays[0].dtype, pl.BlockSpec(shape, lambda i, s: (0, 0, 0)))] * 2
    return call(
        functools.partial(step_kernel, layouts),
        "step",
        place,
        tuple(ins),
        (1,),
        [pl.BlockSpec(array.shape, lambda i, s: (0, 0, 0)) for array in ins],
        outs,
        after=after,
    )


def hand_out(stage_ref, member, value, out_refs, start=0):
    group = len(out_refs)
    rows = stage_ref.shape[1]
    stage_ref[...] = value.reshape(stage_ref.shape)
    for steps, out_ref in enumerate(out_refs):
        for block in range(stage_ref.shape[0] // group):
            out_ref[start + block * rows : start + (block + 1) * rows] = stage_ref[
                block * group + (member + steps) % group
            ]


def project_kernel(group, copies, place, *refs):
    part_refs = refs[:group]
    vec_ref, wq_ref, wk_ref, wv_ref, qvb_ref = refs[group : group + 5]
    refs = refs[group + 5 :]
    if copies:
        refs[-2][...] = refs[0][...].reshape(refs[-2].shape)
        refs[-1][...] = refs[1][...].reshape(refs[-1].shape)
        refs = refs[2:-2]
    x_ref, ht_ref, q_ref, k_ref, v_ref = refs
    gain = vec_ref[0:1]
    shift = vec_ref[1:2]
    qvb = qvb_ref[...].astype(F32)
    rows = part_refs[0].shape[0]
    for steps, part_ref in enumerate(part_refs):
        base = ((place[0] + group - steps) % group) * rows
        spot = pl.ds(pl.multiple_of(base, rows), rows)
        values = part_ref[...]
        x_ref[spot] = values
        normal, _ = norm_parts(values.astype(F32))
        hidden = (normal * gain + shift).astype(BF16)
        ht_ref[:, spot] = hidden.T
        q_ref[spot] = (dot(hidden, wq_ref[...]) + qvb[0:1]).astype(BF16)
        k_ref[spot] = dot(hidden, wk_ref[...]).astype(BF16)
        v_ref[spot] = (dot(hidden, wv_ref[...]) + qvb[1:2]).astype(BF16)


def project(place, parts, first_row, length, vectors, qkv_weight, qv_bias, fill, copied=None):
    group = len(parts)
    rows, width = parts[0].shape
    own = width // group
    rows = rows * group
    index = first_row // rows
    extra = ()
    extra_in = []
    extra_out = []
    if copied is not None:
        shape = copied.shape[2:]
        extra = (copied, copied)
        extra_in = [
            pl.BlockSpec((1, 1) + shape, lambda i, s: (s[1] % 2, 0, 0, 0)),
            pl.BlockSpec((1, 1) + shape, lambda i, s: (1 - s[1] % 2, 0, 0, 0)),
        ]
        extra_out = [(shape, BF16, pl.BlockSpec(shape, lambda i, s: (0, 0)))] * 2
    vector = pl.BlockSpec((8, width), lambda i, s: (0, 0))
    part = pl.BlockSpec((rows // group, width), lambda i, s: (0, 0))
    row = pl.BlockSpec((rows, own), lambda i, s: (index, 0))
    weights = [
        pl.BlockSpec((width, own), functools.partial(lambda t, i, s: (0, t * group + s[0]), t))
        for t in range(3)
    ]
    return call(
        functools.partial(project_kernel, group, copied is not None),
        "project",
        place,
        tuple(parts) + (vectors, qkv_weight, qkv_weight, qkv_weight, qv_bias) + extra,
        (1,),
        [part] * group
        + [vector]
        + weights
        + [pl.BlockSpec((2, own), lambda i, s: (0, s[0]))]
        + extra_in,
        [
            ((length, width), BF16, pl.BlockSpec((rows, width), lambda i, s: (index, 0))),
            ((width, length), BF16, pl.BlockSpec((width, rows), lambda i, s: (0, index))),
        ]
        + [((length, own), BF16, row)] * 3
        + extra_out,
        fill=fill,
    )


def attend_kernel(limit, sub, place, q_ref, k_ref, v_ref, segc_ref, segr_ref, mixed_ref, lse_ref):
    keys = k_ref[...]
    keys = jnp.concatenate([keys, keys], axis=1)
    values = v_ref[...]
    values = jnp.concatenate([values, jnp.ones(values.shape, BF16)], axis=1)
    lane = lax.broadcasted_iota(jnp.int32, (sub, PAIR), 1)
    zero = jnp.zeros((), BF16)
    segr = segr_ref[...]
    for start in range(0, q_ref.shape[0], sub):
        part = pl.ds(start, sub)
        scaled = q_ref[part].astype(F32) * (SCALE * LOG2E)
        high = scaled.astype(BF16)
        low = (scaled - high.astype(F32)).astype(BF16)
        segc = segc_ref[part]
        valid = segc < limit
        bias = jnp.where(jnp.where(valid, segc, -1)[:, :1] == segr, 0.0, NEG)
        mixed = []
        logs = []
        for head in range(2):
            own = (lane < HEAD_DIM) == (head == 0)
            query = jnp.concatenate([jnp.where(own, high, zero), jnp.where(own, low, zero)], axis=1)
            scores = dot(query, keys, NT) + bias
            largest = jnp.max(scores, axis=1, keepdims=True)
            weights = jnp.exp2(scores - largest).astype(BF16)
            summed = dot(weights, values)
            total = summed[:, PAIR:]
            mixed.append(summed[:, :PAIR] / total)
            logs.append(largest + jnp.log2(total))
        first = lane < HEAD_DIM
        mixed_ref[part] = jnp.where(valid, jnp.where(first, mixed[0], mixed[1]), 0.0).astype(BF16)
        lse_ref[part] = jnp.where(valid, jnp.where(first, logs[0], logs[1]), 0.0)


def attend(place, first, count, query, keys, values, seg_cols, seg_row, limit, after=()):
    length = query.shape[0]
    width = count * PAIR
    block = min(1024, length)
    tile = pl.BlockSpec((block, PAIR), lambda p, j, s: (j, first + p))
    whole = pl.BlockSpec((length, PAIR), lambda p, j, s: (0, first + p))
    out_tile = pl.BlockSpec((block, PAIR), lambda p, j, s: (j, p))
    return call(
        functools.partial(attend_kernel, limit, min(256, block)),
        "attend",
        place,
        (query, keys, values, seg_cols, seg_row),
        (width // PAIR, length // block),
        [
            tile,
            whole,
            whole,
            pl.BlockSpec((block, PAIR), lambda p, j, s: (j, 0)),
            pl.BlockSpec((1, length), lambda p, j, s: (0, 0)),
        ],
        [((length, width), BF16, out_tile), ((length, width), F32, out_tile)],
        after=after,
        vmem=LESS_VMEM if length <= 1024 else VMEM,
    )


def attend_back_kernel(
    limit,
    sub,
    place,
    q_ref,
    k_ref,
    v_ref,
    do_ref,
    mixed_ref,
    lse_ref,
    segc_ref,
    segr_ref,
    dq_ref,
    dk_ref,
    dv_ref,
    kt_ref,
    dk_sum,
    dv_sum,
):
    step = pl.program_id(1)
    steps = pl.num_programs(1)
    length = k_ref.shape[0]
    keys = k_ref[...]
    kt_ref[...] = keys.T
    zero = jnp.zeros((), BF16)
    minus = -jnp.ones((), BF16)
    values = v_ref[...]
    key_lane = lax.broadcasted_iota(jnp.int32, (length, PAIR), 1)
    lane = lax.broadcasted_iota(jnp.int32, (sub, PAIR), 1)
    spot = lane & (HEAD_DIM - 1)
    ones = jnp.where((key_lane & (HEAD_DIM - 1)) < 3, minus, zero)
    key_sides = []
    value_sides = []
    for head in range(2):
        own = (key_lane < HEAD_DIM) == (head == 0)
        key_sides.append(jnp.concatenate([jnp.where(own, keys, ones), keys], axis=1))
        value_sides.append(jnp.where(own, values, ones))
    segc = segc_ref[...]
    segc = jnp.where(segc < limit, segc, -1)[:, :1]

    def in_three(value):
        high = value.astype(BF16)
        rest = value - high.astype(F32)
        middle = rest.astype(BF16)
        low = (rest - middle.astype(F32)).astype(BF16)
        return jnp.where(spot == 0, high, jnp.where(spot == 1, middle, jnp.where(spot == 2, low, zero)))

    dk_all = dv_all = None
    for start in range(0, q_ref.shape[0], sub):
        part = pl.ds(start, sub)
        query = q_ref[part]
        scaled = query.astype(F32) * (SCALE * LOG2E)
        high = scaled.astype(BF16)
        low = (scaled - high.astype(F32)).astype(BF16)
        grad = do_ref[part]
        product = grad.astype(F32) * mixed_ref[part].astype(F32)
        logs = lse_ref[part]
        same = segc == segr_ref[:, part]
        dq_rows = []
        for head in range(2):
            own = (lane < HEAD_DIM) == (head == 0)
            log = jnp.broadcast_to(logs[:, head * HEAD_DIM : head * HEAD_DIM + 1], logs.shape)
            delta = jnp.sum(jnp.where(own, product, 0.0), axis=1, keepdims=True)
            delta = jnp.broadcast_to(delta, logs.shape)
            query_side = jnp.concatenate(
                [jnp.where(own, high, in_three(log)), jnp.where(own, low, zero)], axis=1
            )
            grad_side = jnp.where(own, grad, in_three(delta))
            scores = dot(key_sides[head], query_side, NT)
            probs = jnp.where(same, jnp.exp2(scores), 0.0).astype(BF16)
            d_probs = dot(value_sides[head], grad_side, NT)
            d_scores = probs * d_probs.astype(BF16)
            dv_part = dot(probs, jnp.where(own, grad, zero))
            dk_part = dot(d_scores, jnp.where(own, query, zero))
            dv_all = dv_part if dv_all is None else dv_all + dv_part
            dk_all = dk_part if dk_all is None else dk_all + dk_part
            dq_rows.append(dot(kt_ref[head * HEAD_DIM : (head + 1) * HEAD_DIM], d_scores))
        dq_ref[part] = (jnp.concatenate(dq_rows, axis=0).T * SCALE).astype(BF16)
    dk_all = dk_all * SCALE

    @pl.when(step == 0)
    def _():
        dk_sum[...] = dk_all
        dv_sum[...] = dv_all

    @pl.when(step > 0)
    def _():
        dk_sum[...] += dk_all
        dv_sum[...] += dv_all

    @pl.when(step == steps - 1)
    def _():
        dk_ref[...] = dk_sum[...].astype(BF16)
        dv_ref[...] = dv_sum[...].astype(BF16)


def attend_back(
    place, first, query, keys, values, d_mixed, mixed, logs, seg_cols, seg_row, limit, after=()
):
    length, width = mixed.shape
    block = min(1024, length)
    tile = pl.BlockSpec((block, PAIR), lambda p, j, s: (j, first + p))
    whole = pl.BlockSpec((length, PAIR), lambda p, j, s: (0, first + p))
    out_tile = pl.BlockSpec((block, PAIR), lambda p, j, s: (j, p))
    out_whole = pl.BlockSpec((length, PAIR), lambda p, j, s: (0, p))
    return call(
        functools.partial(attend_back_kernel, limit, min(256, block)),
        "attend_back",
        place,
        (query, keys, values, d_mixed, mixed, logs, seg_cols, seg_row),
        (width // PAIR, length // block),
        [
            tile,
            whole,
            whole,
            tile,
            out_tile,
            out_tile,
            pl.BlockSpec((length, PAIR), lambda p, j, s: (0, 0)),
            pl.BlockSpec((1, block), lambda p, j, s: (0, j)),
        ],
        [
            ((length, width), BF16, out_tile),
            ((length, width), BF16, out_whole),
            ((length, width), BF16, out_whole),
        ],
        [pltpu.VMEM((PAIR, length), BF16), pltpu.VMEM((length, PAIR), F32), pltpu.VMEM((length, PAIR), F32)],
        after=after,
        vmem=LESS_VMEM if length <= 1024 else VMEM,
    )


def collect_kernel(group, place, *refs):
    part_refs = refs[:-2]
    rows_ref, sums_ref = refs[-2:]
    count = part_refs[0].shape[0]
    total = None
    for index, part_ref in enumerate(part_refs):
        block, steps = index // group, index % group
        values = part_ref[...]
        spot = block * group + (place[0] + group - steps) % group
        rows_ref[pl.ds(pl.multiple_of(spot * count, count), count)] = values
        part = jnp.sum(values.astype(F32), axis=0, keepdims=True)
        total = part if total is None else total + part
    sums_ref[...] = jnp.concatenate([total, jnp.zeros((7, total.shape[1]), F32)], axis=0)


def collect(place, parts, group, after=()):
    rows, width = parts[0].shape
    length = rows * len(parts)
    whole = pl.BlockSpec((rows, width), lambda i, s: (0, 0))
    return call(
        functools.partial(collect_kernel, group),
        "collect",
        place,
        tuple(parts),
        (1,),
        [whole] * len(parts),
        [
            ((length, width), BF16, pl.BlockSpec((length, width), lambda i, s: (0, 0))),
            ((8, width), F32, pl.BlockSpec((8, width), lambda i, s: (0, 0))),
        ],
        after=after,
        vmem=LESS_VMEM if length <= 1024 else VMEM,
    )


def close_kernel(number, place, x_ref, vec_ref, *refs):
    mixed_refs = refs[:number]
    weight_refs = refs[number : 2 * number]
    middle_ref, own_ref, hidden_ref, ht_ref = refs[2 * number :]
    gain = vec_ref[2:3]
    shift = vec_ref[3:4]
    bias = vec_ref[4:5]
    sub = 256
    for start in range(0, x_ref.shape[0], sub):
        part = pl.ds(start, sub)
        middle = x_ref[part].astype(F32) + bias
        for mixed_ref, weight_ref in zip(mixed_refs, weight_refs):
            middle = middle + dot(mixed_ref[part], weight_ref[...])
        middle_ref[part] = middle
        normal, _ = norm_parts(middle)
        hidden = (normal * gain + shift).astype(BF16)
        hidden_ref[part] = hidden
        ht_ref[:, part] = hidden.T
    count = own_ref.shape[0]
    own_ref[...] = middle_ref[pl.ds(pl.multiple_of(place[0] * count, count), count)]


def close(place, x_rows, mixed_parts, group, out_weight, vectors, slice_rows, after=()):
    length, width = x_rows.shape
    calls = len(mixed_parts)
    number = calls * group
    own = width // number
    rows = slice_rows * group
    vector = pl.BlockSpec((8, width), lambda i, s: (0, 0))
    row = pl.BlockSpec((rows, width), lambda i, s: (i, 0))
    arrays = []
    weights = []
    for j in range(calls):
        for steps in range(group):
            arrays.append(mixed_parts[j][steps])
            weights.append(
                pl.BlockSpec(
                    (own, width),
                    functools.partial(lambda j, t, i, s: (((s[0] + group - t) % group) * calls + j, 0), j, steps),
                )
            )
    return call(
        functools.partial(close_kernel, number),
        "close",
        place,
        (x_rows, vectors)
        + tuple(arrays)
        + (out_weight,) * number,
        (length // rows,),
        [row, vector] + [pl.BlockSpec((rows, own), lambda i, s: (i, 0))] * number + weights,
        [
            ((length, width), F32, row),
            ((length // group, width), F32, pl.BlockSpec((slice_rows, width), lambda i, s: (i, 0))),
            ((length, width), BF16, row, length <= 1024),
            ((width, length), BF16, pl.BlockSpec((width, rows), lambda i, s: (0, i)), length <= 1024),
        ],
        after=after,
    )


def up_specs(width, tile, block, group, number):
    return [
        pl.BlockSpec((width, block), functools.partial(lambda n, t, s: (0, (t * number + n) * group + s[0]), n))
        for n in range(number)
    ]


def feed_up_kernel(number, group, cut, place, h_ref, cot_ref, upb_ref, *refs):
    up_refs = refs[:number]
    active_refs = refs[number : number + group]
    slope_ref, ka_ref, sa_ref, kb_ref, sb_ref, stage_ref, rows_ref = refs[number + group :]
    up = jnp.concatenate([ref[...] for ref in up_refs], axis=1) if number > 1 else up_refs[0][...]
    upper = dot(h_ref[...], up) + upb_ref[...].astype(F32)
    half = 0.5 + 0.5 * lax.erf(upper * 0.7071067811865476)
    bell = jnp.exp2(upper * upper * (-0.5 * LOG2E)) * 0.3989422804014327
    active = (upper * half).astype(BF16)
    hand_out(rows_ref, place[0], active, active_refs)
    slope_ref[...] = (half + upper * bell).astype(BF16)
    stage_ref[...] = dot(active, cot_ref[...], TN).astype(BF16).reshape(stage_ref.shape)
    deal(
        stage_ref,
        place[1] % stage_ref.shape[0],
        [(ka_ref, sa_ref, 1, slice(0, cut)), (kb_ref, sb_ref, 0, slice(cut, None))],
    )


def feed_up(place, hidden, cotangent, up_arrays, up_blocks, upb_own, group, chips, cut, rows, after=()):
    length, width = hidden.shape
    ff = upb_own.shape[1]
    chunk = ff // chips
    tile = min(512 if length <= 1024 else 128, ff)
    parts = tile // chunk
    whole = pl.BlockSpec((length, width), lambda t, s: (0, 0), pipeline_mode=pl.Buffered(1))
    tiled = pl.BlockSpec((length, tile), lambda t, s: (0, t))
    number, specs = up_blocks(tile)

    def piece(columns):
        spec = pl.BlockSpec(
            (parts // 2, chunk, columns), lambda t, s: (jnp.bitwise_xor(t, s[1] // parts), 0, 0)
        )
        return ((chips // 2, chunk, columns), BF16, spec)

    return call(
        functools.partial(feed_up_kernel, number, group, cut),
        "feed_up",
        place,
        (hidden, cotangent, upb_own) + (up_arrays,) * number,
        (ff // tile,),
        [whole, whole, pl.BlockSpec((1, tile), lambda t, s: (0, t))] + specs,
        [
            (
                (length // group, ff),
                BF16,
                pl.BlockSpec((length // group, tile), lambda t, s: (0, t)),
            )
        ]
        * group
        + [((length, ff), BF16, tiled, length <= 1024)]
        + [piece(cut)] * 2
        + [piece(width - cut)] * 2,
        [pltpu.VMEM((parts, chunk, width), BF16), pltpu.VMEM((length // rows, rows, tile), BF16)],
        after=after,
        vmem=LESS_VMEM if length <= 1024 else VMEM,
    )


def feed_back_kernel(number, chips, split, place, ht_ref, cot_ref, slope_ref, down_ref, *refs):
    up_refs = refs[:number]
    dh_refs = refs[number : number + DH_PIECES]
    dub_ref, ka_ref, sa_ref, kb_ref, sb_ref, dh_sum, stage_ref = refs[number + DH_PIECES :]
    step = pl.program_id(0)
    up = jnp.concatenate([ref[...] for ref in up_refs], axis=1) if number > 1 else up_refs[0][...]
    down = down_ref[...]
    down = down.reshape(down.shape[0] * down.shape[2], down.shape[3])
    d_upper = (dot(cot_ref[...], down, NT) * slope_ref[...].astype(F32)).astype(BF16)
    dub_ref[...] = jnp.sum(d_upper.astype(F32), axis=0, keepdims=True)
    length = d_upper.shape[0]
    rows = min(1024, length)

    def add(start):
        part = dot(d_upper[start : start + rows], up, NT)

        @pl.when(step == 0)
        def _():
            dh_sum[start : start + rows] = part

        @pl.when(step > 0)
        def _():
            dh_sum[start : start + rows] += part

    for start in range(0, length, rows):
        add(start)

    rows = ht_ref.shape[0] // chips
    many = max(1, 256 // rows)
    for start in range(0, chips, many):
        grad = dot(ht_ref[start * rows : (start + many) * rows], d_upper).astype(BF16)
        stage_ref[start : start + many] = grad.reshape(many, rows, grad.shape[1])

    @pl.when(step < split)
    def _():
        deal(stage_ref, place[1], [(ka_ref, sa_ref, 1, slice(None))])

    @pl.when(step >= split)
    def _():
        deal(stage_ref, place[1], [(kb_ref, sb_ref, 0, slice(None))])

    @pl.when(step == pl.num_programs(0) - 1)
    def _():
        piece_rows = dh_refs[0].shape[0]
        for index, dh_ref in enumerate(dh_refs):
            dh_ref[...] = dh_sum[index * piece_rows : (index + 1) * piece_rows].astype(BF16)


def feed_back(
    place, hidden_t, cotangent, slope, down_weight, up_arrays, up_blocks, group, chips, share, after=()
):
    width, length = hidden_t.shape
    ff = slope.shape[1]
    chunk = ff // chips
    tile = min(512 if length <= 1024 else 128, ff)
    parts = tile // chunk
    number, specs = up_blocks(tile)
    tiles = ff // tile
    split = max(1, min(tiles - 1, round(tiles * share)))
    some = width // chips

    def piece(first, last):
        spec = pl.BlockSpec(
            (chips // 2, some, tile), lambda t, s: (0, 0, jnp.clip(t, first, last - 1) - first)
        )
        return ((chips // 2, some, (last - first) * tile), BF16, spec)

    return call(
        functools.partial(feed_back_kernel, number, chips, split),
        "feed_back",
        place,
        (hidden_t, cotangent, slope, down_weight.reshape(chips, group, chunk, width)) + (up_arrays,) * number,
        (ff // tile,),
        [
            pl.BlockSpec((width, length), lambda t, s: (0, 0), pipeline_mode=pl.Buffered(1)),
            pl.BlockSpec((length, width), lambda t, s: (0, 0), pipeline_mode=pl.Buffered(1)),
            pl.BlockSpec((length, tile), lambda t, s: (0, t)),
            pl.BlockSpec((parts, 1, chunk, width), lambda t, s: (t, s[0], 0, 0)),
        ]
        + specs,
        [
            ((length // DH_PIECES, width), BF16, pl.BlockSpec((length // DH_PIECES, width), lambda t, s: (0, 0)))
        ]
        * DH_PIECES
        + [((1, ff), F32, pl.BlockSpec((1, tile), lambda t, s: (0, t)))]
        + [piece(0, split)] * 2
        + [piece(split, tiles)] * 2,
        [pltpu.VMEM((length, width), F32), pltpu.VMEM((chips, some, tile), BF16)],
        after=after,
        vmem=LESS_VMEM if length <= 1024 else VMEM,
    )


def feed_down_kernel(group, place, down_ref, middle_ref, vec_ref, *refs):
    active_refs = refs[:group]
    near_ref, far_ref, sum_ref = refs[group:]
    step = pl.program_id(0)
    total = None
    for steps, active_ref in enumerate(active_refs):
        down = down_ref[:, pl.ds((place[0] + group - steps) % group, 1)]
        part = dot(active_ref[...], down.reshape(-1, down.shape[3]))
        total = part if total is None else total + part

    @pl.when(step == 0)
    def _():
        sum_ref[...] = total

    @pl.when(step > 0)
    def _():
        sum_ref[...] += total

    @pl.when(step == pl.num_programs(0) - 1)
    def _():
        half = near_ref.shape[0]
        for start, out_ref in ((0, near_ref), (half, far_ref)):
            part = pl.ds(start, half)
            out_ref[...] = (middle_ref[part] + sum_ref[part] + vec_ref[5:6]).astype(BF16)


def feed_down(place, active_parts, down_weight, middle, vectors, chips, after=()):
    group = len(active_parts)
    rows, ff = active_parts[0].shape
    width = down_weight.shape[1]
    chunk = ff // chips
    tile = min(512, ff)
    out = ((rows // 2, width), BF16, pl.BlockSpec((rows // 2, width), lambda i, s: (0, 0)))
    return call(
        functools.partial(feed_down_kernel, group),
        "feed_down",
        place,
        (down_weight.reshape(chips, group, chunk, width), middle, vectors) + tuple(active_parts),
        (ff // tile,),
        [
            pl.BlockSpec((tile // chunk, group, chunk, width), lambda i, s: (i, 0, 0, 0)),
            pl.BlockSpec((rows, width), lambda i, s: (0, 0)),
            pl.BlockSpec((8, width), lambda i, s: (0, 0)),
        ]
        + [pl.BlockSpec((rows, tile), lambda i, s: (0, i))] * group,
        [out, out],
        [pltpu.VMEM((rows, width), F32)],
        after=after,
    )


def middle_back_kernel(group, span, turn, place, middle_ref, cot_ref, vec_ref, weight_ref, *refs):
    part_refs = refs[: group * DH_PIECES]
    branch_ref, d_middle_ref, d_mixed_ref, sums_ref, sum_ref = refs[group * DH_PIECES :]
    step = pl.program_id(0)

    def gather(piece):
        @pl.when(step // span == piece)
        def _():
            total = part_refs[piece * group][...].astype(F32)
            for ref in part_refs[piece * group + 1 : (piece + 1) * group]:
                total = total + ref[...].astype(F32)
            sum_ref[...] = total

    for piece in range(DH_PIECES):
        gather(piece)
    d_hidden = sum_ref[...]
    normal, inverse = norm_parts(middle_ref[...])
    d_middle = cot_ref[...].astype(F32) + norm_back(d_hidden, normal, inverse, vec_ref[2:3])
    branch = d_middle.astype(BF16)
    branch_ref[...] = branch

    @pl.when(step // turn % group == place[0])
    def _():
        d_middle_ref[...] = d_middle

    d_mixed_ref[...] = dot(branch, weight_ref[...], NT).astype(BF16)
    sums = jnp.concatenate(
        [
            jnp.sum(d_hidden * normal, axis=0, keepdims=True),
            jnp.sum(d_hidden, axis=0, keepdims=True),
            jnp.sum(branch.astype(F32), axis=0, keepdims=True),
            jnp.zeros((5, branch.shape[1]), F32),
        ],
        axis=0,
    )

    @pl.when(step == 0)
    def _():
        sums_ref[...] = sums

    @pl.when(step > 0)
    def _():
        sums_ref[...] += sums


def middle_back(place, middle, cotangent, vectors, out_weight, parts, slice_rows, after=()):
    length, width = middle.shape
    group = len(parts[0])
    own = width // group
    rows = min(256, length // DH_PIECES, slice_rows)
    turn = slice_rows // rows
    span = length // DH_PIECES // rows
    row = pl.BlockSpec((rows, width), lambda i, s: (i, 0))
    specs = [
        pl.BlockSpec(
            (rows, width), functools.partial(lambda k, i, s: (jnp.clip(i - k * span, 0, span - 1), 0), piece)
        )
        for piece in range(DH_PIECES)
        for _ in range(group)
    ]
    return call(
        functools.partial(middle_back_kernel, group, span, turn),
        "middle_back",
        place,
        (middle, cotangent, vectors, out_weight) + tuple(array for piece in parts for array in piece),
        (length // rows,),
        [
            row,
            row,
            pl.BlockSpec((8, width), lambda i, s: (0, 0)),
            pl.BlockSpec((own, width), lambda i, s: (s[0], 0)),
        ]
        + specs,
        [
            ((length, width), BF16, row),
            (
                (length // group, width),
                F32,
                pl.BlockSpec((rows, width), lambda i, s: (i // (turn * group) * turn + i % turn, 0)),
            ),
            ((length, own), BF16, pl.BlockSpec((rows, own), lambda i, s: (i, 0))),
            ((8, width), F32, pl.BlockSpec((8, width), lambda i, s: (0, 0))),
        ],
        [pltpu.VMEM((rows, width), F32)],
        after=after,
        vmem=LESS_VMEM if length <= 1024 else VMEM,
    )


def attention_grad_kernel(group, calls, chips, cut, place, *refs):
    ht_ref, dq_ref, dk_ref, dv_ref = refs[:4]
    mixed_refs = refs[5 : 5 + group * calls]
    side_refs = refs[-6 - group : -6]
    ka_ref, sa_ref, kb_ref, sb_ref, stage_ref, rows_ref = refs[-6:]
    offset = 0
    if calls:
        branch = refs[4][...]
        offset = branch.shape[1]
        share = chips // (group * calls)
        for index, mixed_ref in enumerate(mixed_refs):
            owner = ((place[0] + group - index % group) % group) * calls + index // group
            grad = dot(mixed_ref[...], branch, TN).astype(BF16)
            rows = grad.shape[0] // share
            stage_ref[pl.ds(owner * share, share), :, :offset] = grad.reshape(share, rows, offset)
    side = jnp.concatenate([dq_ref[...], dk_ref[...], dv_ref[...]], axis=1)
    hand_out(rows_ref, place[0], side, side_refs)
    rows = ht_ref.shape[0] // chips
    many = max(1, 256 // rows)
    for start in range(0, chips, many):
        grad = dot(ht_ref[start * rows : (start + many) * rows], side).astype(BF16)
        stage_ref[start : start + many, :, offset:] = grad.reshape(many, rows, grad.shape[1])
    for relative in range(chips):
        values = stage_ref[jnp.bitwise_xor(jnp.int32(relative), place[1])]
        (sa_ref if relative & 2 else ka_ref)[without_bit(relative, 1)] = values[:, :cut]
        (sb_ref if relative & 1 else kb_ref)[without_bit(relative, 0)] = values[:, cut:]


def attention_grad(place, hidden_t, triple, group, chips, slice_rows, branch=None, mixed_parts=(), after=()):
    width, length = hidden_t.shape
    own = triple[0].shape[1]
    some = width // chips
    calls = len(mixed_parts)
    columns = 3 * own + (width // group if calls else 0)
    cut = columns // 2
    args = [hidden_t, *triple]
    specs = [pl.BlockSpec((width, length), lambda i, s: (0, 0))]
    specs += [pl.BlockSpec((length, own), lambda i, s: (0, 0))] * 3
    if calls:
        arrays = [mixed_parts[j][s] for j in range(calls) for s in range(group)]
        args += [branch, *arrays]
        specs.append(pl.BlockSpec((length, width // group), lambda i, s: (0, s[0])))
        specs += [pl.BlockSpec(array.shape, lambda i, s: (0, 0)) for array in arrays]
    sides = (length // group, 3 * own)

    def piece(rows, columns):
        shape = (chips // 2, rows, columns)
        return (shape, BF16, pl.BlockSpec(shape, lambda i, s: (0, 0, 0)))

    return call(
        functools.partial(attention_grad_kernel, group, calls, chips, cut),
        "attention_grad",
        place,
        tuple(args),
        (1,),
        specs,
        [(sides, BF16, pl.BlockSpec(sides, lambda i, s: (0, 0)))] * group
        + [piece(some, cut)] * 2
        + [piece(some, columns - cut)] * 2,
        [
            pltpu.VMEM((chips, some, columns), BF16),
            pltpu.VMEM((length // slice_rows, slice_rows, 3 * own), BF16),
        ],
        after=after,
        vmem=LESS_VMEM if length <= 1024 else VMEM,
    )


def hidden_back_kernel(group, calls, place, x_ref, base_ref, vec_ref, *refs):
    number = group * calls
    side_refs = refs[:number]
    weight_refs = refs[number : 4 * number]
    near_ref, far_ref, sums_ref = refs[4 * number :]
    total = None
    for index, side_ref in enumerate(side_refs):
        side = side_ref[...]
        each = side.shape[1] // 3
        row_sums = jnp.sum(side.astype(F32), axis=0, keepdims=True)
        spot = ((place[0] + group - index % group) % group) * calls + index // group
        spot = pl.ds(pl.multiple_of(spot * each, each), each)
        sums_ref[2:3, spot] = row_sums[:, :each]
        sums_ref[3:4, spot] = row_sums[:, 2 * each :]
        for third in range(3):
            part = dot(side[:, third * each : (third + 1) * each], weight_refs[3 * index + third][...], NT)
            total = part if total is None else total + part
    normal, inverse = norm_parts(x_ref[...].reshape(total.shape).astype(F32))
    sums_ref[0:1] = jnp.sum(total * normal, axis=0, keepdims=True)
    sums_ref[1:2] = jnp.sum(total, axis=0, keepdims=True)
    sums_ref[4:8] = jnp.zeros((4, total.shape[1]), F32)
    result = (base_ref[...] + norm_back(total, normal, inverse, vec_ref[0:1])).astype(BF16)
    half = near_ref.shape[0]
    near_ref[...] = result[:half]
    far_ref[...] = result[half:]


def hidden_back(place, x_rows, d_middle, vectors, side_parts, qkv_weight, slice_rows, after=()):
    calls = len(side_parts)
    group = len(side_parts[0])
    rows, columns = side_parts[0][0].shape
    each = columns // 3
    length, width = x_rows.shape
    slices = length // group // slice_rows
    whole = pl.BlockSpec((rows, width), lambda i, s: (0, 0))
    arrays = []
    weights = []
    for j in range(calls):
        for steps in range(group):
            arrays.append(side_parts[j][steps])
            for third in range(3):
                weights.append(
                    pl.BlockSpec(
                        (width, each),
                        functools.partial(
                            lambda j, t, third, i, s: (
                                0,
                                third * group * calls + ((s[0] + group - t) % group) * calls + j,
                            ),
                            j,
                            steps,
                            third,
                        ),
                    )
                )
    out = ((rows // 2, width), BF16, pl.BlockSpec((rows // 2, width), lambda i, s: (0, 0)))
    return call(
        functools.partial(hidden_back_kernel, group, calls),
        "hidden_back",
        place,
        (x_rows.reshape(slices, group, slice_rows, width), d_middle, vectors)
        + tuple(arrays)
        + (qkv_weight,) * len(weights),
        (1,),
        [
            pl.BlockSpec((slices, 1, slice_rows, width), lambda i, s: (0, s[0], 0, 0)),
            whole,
            pl.BlockSpec((8, width), lambda i, s: (0, 0)),
        ]
        + [pl.BlockSpec((rows, columns), lambda i, s: (0, 0))] * len(arrays)
        + weights,
        [out, out, ((8, width), F32, pl.BlockSpec((8, width), lambda i, s: (0, 0)))],
        after=after,
        vmem=LESS_VMEM if length <= 1024 else VMEM,
    )


def part_kernel(takes, whole, place, *refs):
    arrays = (len(refs) - 2 - bool(whole)) // 2
    own_ref, send_ref = refs[2 * arrays : 2 * arrays + 2]
    rows = own_ref.shape[0]
    mine = place[0] == 0
    start = 0

    def total(index, first, count):
        part = pl.ds(first, count)
        return refs[2 * index][0, part].astype(F32) + refs[2 * index + 1][0, part].astype(F32)

    for index, first in takes:
        both = total(index, first, 2 * rows)
        columns = both.shape[1]
        own_ref[:, start : start + columns] = jnp.where(mine, both[:rows], both[rows:])
        send_ref[:, start : start + columns] = jnp.where(mine, both[rows:], both[:rows]).astype(BF16)
        start += columns
    if whole:
        out_ref = refs[-1]
        start = 0
        for index, first in whole:
            value = total(index, first, out_ref.shape[0])
            out_ref[:, start : start + value.shape[1]] = value
            start += value.shape[1]


def part_rows(place, arrays, takes, rows, whole=(), whole_rows=0, after=()):
    columns = sum(arrays[2 * index].shape[2] for index, _ in takes)
    out = pl.BlockSpec((rows, columns), lambda i, s: (0, 0))
    outs = [((rows, columns), F32, out), ((rows, columns), BF16, out)]
    if whole:
        shape = (whole_rows, sum(arrays[2 * index].shape[2] for index, _ in whole))
        outs.append((shape, F32, pl.BlockSpec(shape, lambda i, s: (0, 0))))
    return call(
        functools.partial(part_kernel, takes, whole),
        "part_rows",
        place,
        tuple(arrays),
        (1,),
        [pl.BlockSpec(array.shape, lambda i, s: (0, 0, 0)) for array in arrays],
        outs,
        after=after,
    )


def emit_kernel(moves, place, own_ref, came_ref, *out_refs):
    member = place[0]
    for source, size, out, column, stride in moves:
        for ref, who in ((own_ref, member), (came_ref, 1 - member)):
            spot = pl.ds(pl.multiple_of(column + who * stride, 128), size)
            out_refs[out][:, spot] = ref[:, source : source + size].astype(F32)


def emit(place, own, came, moves, widths, after=()):
    rows, columns = own.shape
    block = pl.BlockSpec((rows, columns), lambda i, s: (0, 0))
    return call(
        functools.partial(emit_kernel, moves),
        "emit",
        place,
        (own, came),
        (1,),
        [block, block],
        [((rows, width), F32, pl.BlockSpec((rows, width), lambda i, s: (0, 0))) for width in widths],
        after=after,
    )


def body(
    inputs,
    cotangent,
    image_lengths,
    norm1_gain,
    norm1_bias,
    qkv_weight,
    qv_bias,
    out_weight,
    out_bias,
    norm2_gain,
    norm2_bias,
    up_weight,
    up_bias,
    down_weight,
    down_bias,
):
    rows, width = inputs.shape[2:]
    limit = image_lengths.shape[-1]
    ff = up_weight.shape[1]
    dp_size = lax.axis_size("dp")
    ctx_size = lax.axis_size("ctx")
    group = ctx_size // 2
    dp_index = lax.axis_index("dp")
    ctx_index = lax.axis_index("ctx")
    half = ctx_index // group
    member = ctx_index % group
    length = rows * ctx_size
    chips = dp_size * 2
    dp_bits = dp_size.bit_length() - 1
    own_width = width // group
    own_ff = ff // group
    chunk = own_ff // chips
    place = Place(jnp.stack([member, dp_index * 2 + half]).astype(jnp.int32))

    def across(value):
        pairs = [(i, (i + group) % ctx_size) for i in range(ctx_size)]
        return lax.ppermute(value, "ctx", pairs)

    def around(value, steps):
        pairs = [
            (h * group + g, h * group + (g + steps) % group) for h in range(2) for g in range(group)
        ]
        return lax.ppermute(value, "ctx", pairs)

    def all_around(value):
        return [value] + [around(value, steps) for steps in range(1, group)]

    def in_order(parts, axis=0):
        if group == 2:
            first = member == 0
            return jnp.stack(
                [jnp.where(first, parts[0], parts[1]), jnp.where(first, parts[1], parts[0])], axis=axis
            )
        return jnp.roll(jnp.stack(parts[::-1], axis=axis), member + 1, axis=axis)

    def gather(value):
        return in_order(all_around(value))

    def pick(value, index, axis):
        return lax.dynamic_index_in_dim(value, index, axis, keepdims=False)

    def group_sum_scatter(value, axis):
        total = pick(value, member, axis).astype(F32)
        for steps in range(1, group):
            total = total + around(pick(value, (member + steps) % group, axis), steps).astype(F32)
        return total

    def swap_bit(value, bit):
        if bit < 0:
            return across(value)
        return lax.ppermute(value, "dp", [(i, i ^ (1 << bit)) for i in range(dp_size)])

    all_bits = list(range(dp_bits - 1, -1, -1)) + [-1]
    rest_bits = list(range(1, dp_bits))

    class Halving:
        def __init__(self, keep, send, bits, order):
            self.order = list(order)
            self.left = list(bits)
            self.keep = keep
            self.came = swap_bit(send, self.order[0])
            self.order.pop(0)

    def pair(pieces):
        first = [bit for bit in all_bits if bit != 0]
        second = [bit for bit in all_bits if bit != -1]
        return [
            Halving(*pieces[:2], first, [0, -1] + rest_bits),
            Halving(*pieces[2:], second, [-1, 0] + rest_bits),
        ]

    def step(after, *jobs):
        asked = []
        for halvings in jobs:
            first = halvings[0]
            bit = first.order[0]
            arrays = [array for halving in halvings for array in (halving.keep, halving.came)]
            asked.append((arrays, len(first.left) - 1 - first.left.index(bit)))
        sums = step_call(place, asked, after)
        results = []
        for index, halvings in enumerate(jobs):
            first = halvings[0]
            left = [bit for bit in first.left if bit != first.order[0]]
            results.append(Halving(sums[2 * index], sums[2 * index + 1], left, first.order))
        return list(sums[:1]), results

    slices = 2 if group > 2 else 1
    slice_rows = rows // slices

    def sliced(value):
        return [value[c * slice_rows : (c + 1) * slice_rows] for c in range(slices)]

    own_inputs = pick(inputs, half, 0)[0]
    far_inputs = across(pick(inputs, 1 - half, 0)[0])
    vectors = jnp.stack([norm1_gain, norm1_bias, norm2_gain, norm2_bias, out_bias, down_bias, out_bias, out_bias])
    vectors = vectors.astype(F32)
    filled = ()
    for side, both_of in enumerate((own_inputs, far_inputs)):
        for c, part in enumerate(sliced(both_of)):
            start = (side * slices + c) * (length // (2 * slices))
            copied = cotangent if not filled else None
            filled = project(
                place, all_around(part), start, length, vectors, qkv_weight, qv_bias, filled, copied
            )
            if copied is not None:
                *filled, own_cot, far_cot = filled
    x_rows, hidden1_t, query, keys, values = filled
    cot_parts = [part for value in sliced(own_cot) for part in all_around(value)]
    far_cot = across(far_cot)
    cot_parts += [part for value in sliced(far_cot) for part in all_around(value)]

    spots = jnp.arange(length, dtype=jnp.int32).reshape(2, group, slices, rows // slices)
    spots = jnp.swapaxes(spots, 1, 2)
    positions = jnp.where(half == 0, spots, spots[::-1]).reshape(length)
    ends = jnp.cumsum(pick(image_lengths, half, 0)[0])
    segment = jnp.sum((positions[:, None] >= ends[None, :]).astype(jnp.int32), axis=1)
    seg_row = segment.reshape(1, length)
    seg_cols = jnp.broadcast_to(segment[:, None], (length, PAIR))

    if chunk % 128 == 0:
        up_arrays = up_weight

        def up_blocks(tile):
            return tile // chunk, up_specs(width, tile, chunk, group, tile // chunk)

    else:
        up_arrays = pick(up_weight.reshape(width, chips, group, chunk), member, 2).reshape(width, own_ff)

        def up_blocks(tile):
            return 1, [pl.BlockSpec((width, tile), lambda t, s: (0, t))]

    upb_own = pick(up_bias.reshape(chips, group, chunk), member, 1).reshape(1, own_ff)

    pairs = own_width // PAIR
    calls = min(2, pairs)
    each = pairs // calls
    mixed = []
    logs = []
    mixed_parts = []
    ready = []
    for j in range(calls):
        mixed_j, logs_j = attend(
            place, j * each, each, query, keys, values, seg_cols, seg_row, limit, after=ready
        )
        mixed.append(mixed_j)
        logs.append(logs_j)
        mixed_parts.append(all_around(mixed_j))
        ready = [mixed_j]
    cot_rows, cot_sums = collect(place, cot_parts, group, after=ready)
    middle, middle_own, hidden2, hidden2_t = close(
        place, x_rows, mixed_parts, group, out_weight, vectors, slice_rows, after=[cot_rows]
    )
    up_out = feed_up(
        place,
        hidden2,
        cot_rows,
        up_arrays,
        up_blocks,
        upb_own,
        group,
        chips,
        width // 2,
        slice_rows,
    )
    active_parts = up_out[:group]
    slope, *down_pieces = up_out[group:]
    active_parts = [active_parts[0]] + [around(active_parts[steps], steps) for steps in range(1, group)]
    down = pair(down_pieces)
    back = feed_back(
        place,
        hidden2_t,
        cot_rows,
        slope,
        down_weight,
        up_arrays,
        up_blocks,
        group,
        chips,
        0.5,
        after=down_pieces[:1],
    )
    dh_pieces = back[:DH_PIECES]
    upb_grad, *up_pieces = back[DH_PIECES:]
    dh_parts = [all_around(piece) for piece in dh_pieces]
    up = pair(up_pieces)

    ready, down = step(dh_pieces[:1], [down[0]], [down[1]])
    branch, d_middle, d_mixed, sums = middle_back(
        place, middle, cot_rows, vectors, out_weight, dh_parts, slice_rows, after=ready
    )

    def back_of(j, after):
        return attend_back(
            place, j * each, query, keys, values, d_mixed, mixed[j], logs[j], seg_cols, seg_row, limit, after=after
        )

    def grad_of(j, triple, after):
        results = attention_grad(
            place,
            hidden1_t,
            triple,
            group,
            chips,
            slice_rows,
            branch if j == 0 else None,
            mixed_parts if j == 0 else (),
            after=after,
        )
        sides = results[:group]
        sides = [sides[0]] + [around(sides[steps], steps) for steps in range(1, group)]
        return pair(results[group:]), sides, list(results[:1])

    triple = back_of(0, [branch])
    early, sides, ready = grad_of(0, triple, triple[:1])
    sides_of = [sides]
    ready, (down,) = step(ready, down)
    if calls > 1:
        ready, up = step(ready, [up[0]], [up[1]])
        triple = back_of(1, ready)
        late, sides, ready = grad_of(1, triple, triple[:1])
        sides_of.append(sides)
        ready, (up, down, *early) = step(ready, up, [down], [early[0]], [early[1]])
    else:
        ready, (*up, down) = step(ready, [up[0]], [up[1]], [down])
        ready, (up, *early) = step(ready, up, [early[0]], [early[1]])
    input_near, input_far, own_sums = hidden_back(
        place, x_rows, d_middle, vectors, sides_of, qkv_weight, slice_rows, after=ready
    )

    own = width // (chips * group)
    both = 1.0 / group
    member_is = (jnp.arange(group, dtype=jnp.int32) == member).astype(F32)
    sums_of = jnp.concatenate([own_sums[:4], sums[2:3] * both, sums[:2] * both, cot_sums[:1] * both])
    small = jnp.transpose(sums_of.reshape(8, chips * group, own), (1, 0, 2)).reshape(chips * group, 8 * own)
    upb_full = (upb_grad.reshape(chips, 1, chunk) * member_is[None, :, None]).reshape(chips * group, chunk)
    small = jnp.concatenate([small, upb_full], axis=1)
    small = lax.all_to_all(small, ("dp", "ctx"), 0, 0, tiled=True)
    small = jnp.sum(small, axis=0)
    small_rows = small[: 8 * own].reshape(8, own)
    upb_out = small[8 * own :]

    ready = [input_near]
    if calls > 1:
        ready, (*late, up, early) = step(ready, [late[0]], [late[1]], [up], early)
    else:
        ready, (early,) = step(ready, early)
    out_near, out_far = feed_down(place, active_parts, down_weight, middle_own, vectors, chips, after=ready)
    ready = [out_near]
    if calls > 1:
        ready, (late, early) = step(ready, late, [early])
        tails = [down, up, early, late]
    else:
        tails = [down, up, early]
    while any(tail.order for tail in tails):
        active = [tail for tail in tails if tail.order]
        ready, stepped = step(ready, *[[tail] for tail in active])
        for tail, new in zip(active, stepped):
            tails[tails.index(tail)] = new

    def hand_back(near, far):
        came = across(far)
        first = half == 0
        return jnp.stack([jnp.where(first, near, came), jnp.where(first, came, near)])[:, None]

    block_output = hand_back(out_near, out_far)
    input_grad = hand_back(input_near, input_far)

    some = width // chips

    def exchange(value):
        value = value.reshape(group, own, value.shape[1])
        parts = [pick(value, member, 0)] + [
            around(pick(value, (member + steps) % group, 0).astype(BF16), steps).astype(F32)
            for steps in range(1, group)
        ]
        return in_order(parts, 1)

    def sums_in(tail):
        return tail.keep[0].astype(F32) + tail.came[0].astype(F32)

    down, up, *rest = tails
    if group == 2 and own % 16 == 0:
        columns = up.keep.shape[2]
        up_own, up_send, down_out = part_rows(
            place,
            [down.keep, down.came, up.keep, up.came],
            [(1, k * some) for k in range(own_ff // columns)],
            own,
            [(0, k * chunk) for k in range(2)],
            chunk,
            ready,
        )
        moves = [(k * chunk, chunk, 0, k * 2 * chunk, chunk) for k in range(chips)]
        (up_out,) = emit(place, up_own, around(up_send, 1), moves, [ff])
        rest_own, rest_send = part_rows(
            place,
            [array for tail in rest for array in (tail.keep, tail.came)],
            [(index, first) for index in range(calls) for first in (0, some)],
            own,
            after=[up_out],
        )
        moves = [(0, own_width, 0, 0, own_width)] + [
            (own_width + (j * 3 + t) * each * PAIR, each * PAIR, 1, t * width + j * each * PAIR, own_width)
            for j in range(calls)
            for t in range(3)
        ]
        out_out, qkv_out = emit(place, rest_own, around(rest_send, 1), moves, [width, 3 * width])
    else:

        def blocks_of(tail, rows):
            value = sums_in(tail)
            return [value[start : start + rows] for start in range(0, value.shape[0], rows)]

        down_out = jnp.concatenate(blocks_of(down, chunk), axis=1)
        up_out = exchange(jnp.concatenate(blocks_of(up, some), axis=1)).reshape(own, group, chips, chunk)
        up_out = jnp.swapaxes(up_out, 1, 2).reshape(own, ff)
        parts = [part for tail in rest for part in blocks_of(tail, some)]
        rest = exchange(jnp.concatenate(parts, axis=1))
        out_out = rest[:, :, :own_width].reshape(own, width)
        qkv_out = rest[:, :, own_width:].reshape(own, group, calls, 3, each * PAIR)
        qkv_out = jnp.transpose(qkv_out, (0, 3, 1, 2, 4)).reshape(own, 3 * width)
    return (
        block_output,
        input_grad,
        small_rows[0],
        small_rows[1],
        qkv_out,
        small_rows[2:4],
        out_out,
        small_rows[4],
        small_rows[5],
        small_rows[6],
        up_out,
        upb_out,
        down_out,
        small_rows[7],
    )


def solution(mesh):
    split = P(None, "dp", "ctx", None)
    both = ("dp", "ctx")
    return jax.shard_map(
        body,
        mesh=mesh,
        in_specs=(split, split, P(None, "dp", None)) + (P(),) * 12,
        out_specs=(
            split,
            split,
            P(both),
            P(both),
            P(both, None),
            P(None, both),
            P(both, None),
            P(both),
            P(both),
            P(both),
            P(both, None),
            P(both),
            P(both, None),
            P(both),
        ),
        check_vma=False,
    )
```

profile of v0, /device:TPU:0, one launch (start us, length us, event | category | flops | bytes accessed | tf_op | source)
XLA Modules:
  0.0 286.4 jit_solution(12213197875746512636)
XLA Ops:
  0.8 1.3 dynamic-slice_bitcast_fusion
  2.6 2.6 collective-permute-start
  6.8 7.3 %project.2 = (bf16[1024,1024]{1,0:T(8,128)(2,1)}, bf16[1024,1024]{1,0:T(8,128)(2,1)}, bf16[1024,512]{1,0:T(8,128)(2,1)}, bf16[1024,512]{1,0:T(8,128)(2,1)}, bf16...) custom-call(s32[2]{0:T(128)S(1)} %pad_add_fusion.place_ref, ...), custom_call_target="tpu_custom_call" | custom-call | tf_op jit(solution)/shard_map/project/pallas_call | solution.py:46
  15.1 2.8 collective-permute-done.refs_0_
  20.6 6.3 %project.3 = (bf16[1024,1024]{1,0:T(8,128)(2,1)}, bf16[1024,1024]{1,0:T(8,128)(2,1)}, bf16[1024,512]{1,0:T(8,128)(2,1)}, bf16[1024,512]{1,0:T(8,128)(2,1)}, bf16[1024,512]{1,0:T(8,128)(2,1)}) custom-call(s32[2]{0:T(128)S(1)} %pad_add_fusion.place_ref, ...), custom_call_target="tpu_custom_call", output_to_operand_aliasing={{0}: (8, {}), {1}: (9, {}), {2}: (10, {}), {3}: (11, {}), {... | custom-call | tf_op jit(solution)/shard_map/project/pallas_call | solution.py:46
  27.9 9.5 %attend.2 = (bf16[1024,256]{1,0:T(8,128)(2,1)}, f32[1024,256]{1,0:T(8,128)}) custom-call(s32[2]{0:T(128)S(1)} %pad_add_fusion.place_ref, bf16[1024,512]{1,0:T(8,128)(2,1)} %get-tuple-element.124.refs_0_, bf16[1024,512]{1,0:T(8,128)(2,1)} %get-tuple-element.125.refs_1_, bf16[1024,512]{1,0:T(8,128)(2,1)} %get-tuple-element.126.refs_2_, ...), custom_call_target="tpu_custom_call" | custom-call | tf_op jit(solution)/shard_map/attend/pallas_call | solution.py:46
  38.0 9.4 %attend.3 = (bf16[1024,256]{1,0:T(8,128)(2,1)}, f32[1024,256]{1,0:T(8,128)}) custom-call(s32[2]{0:T(128)S(1)} %pad_add_fusion.place_ref, bf16[1024,512]{1,0:T(8,128)(2,1)} %get-tuple-element.124.refs_0_, bf16[1024,512]{1,0:T(8,128)(2,1)} %get-tuple-element.125.refs_1_, bf16[1024,512]{1,0:T(8,128)(2,1)} %get-tuple-element.126.refs_2_, ...), custom_call_target="tpu_custom_call" | custom-call | tf_op jit(solution)/shard_map/attend/pallas_call | solution.py:46
  49.8 3.7 %collect.1 = (bf16[1024,1024]{1,0:T(8,128)(2,1)}, f32[8,1024]{1,0:T(8,128)}) custom-call(s32[2]{0:T(128)S(1)} %pad_add_fusion.place_ref, bf16[256,1024]{1,0:T(8,128)(2,1)} %get-tuple-element.129.refs_0_, bf16[256,1024]{1,0:T(8,128)(2,1)} %copy-done.17, bf16[256,1024]{1,0:T(8,128)(2,1)} %copy-done.16, bf16[256,1024]{1,0:T(8,128)(2,1)} %copy-done.18, ...), custom_call_target="tpu_custom_call" | custom-call | tf_op jit(solution)/shard_map/collect/pallas_call | solution.py:46
  54.5 7.9 %close.1 = (f32[1024,1024]{1,0:T(8,128)}, f32[512,1024]{1,0:T(8,128)}, bf16[1024,1024]{1,0:T(8,128)(2,1)S(1)}, bf16[1024,1024]{1,0:T(8,128)(2,1)S(1)}) custom-call(s32[2]{0:T(128)S(1)} %pad_add_fusion.place_ref, bf16[1024,1024]{1,0:T(8,128)(2,1)} %get-tuple-element.123.refs_0_, f32[8,1024]{1,0:T(8,128)} %convert_element_type.13.refs_2_.refs_1_, ...), custom_call_target="tpu_custom_call" | custom-call | tf_op jit(solution)/shard_map/close/pallas_call | solution.py:46
  62.5 17.1 %feed_up.1 = (bf16[512,2048]{1,0:T(8,128)(2,1)}, bf16[512,2048]{1,0:T(8,128)(2,1)}, bf16[1024,2048]{1,0:T(8,128)(2,1)S(1)}, bf16[8,128,512]{2,1,0:T(8,128)(2,1)}...) custom-call(s32[2]{0:T(128)S(1)} %pad_add_fusion.place_ref, ...), custom_call_target="tpu_custom_call" | custom-call | tf_op jit(solution)/shard_map/feed_up/pallas_call | solution.py:46
  79.6 2.0 collective-permute-start.13
  81.6 1.5 collective-permute-start.14
  83.1 22.5 %feed_back.1 = (bf16[256,1024]{1,0:T(8,128)(2,1)}, bf16[256,1024]{1,0:T(8,128)(2,1)}, bf16[256,1024]{1,0:T(8,128)(2,1)}, bf16[256,1024]{1,0:T(8,128)(2,1)}, f32[...) custom-call(s32[2]{0:T(128)S(1)} %pad_add_fusion.place_ref, ...), custom_call_target="tpu_custom_call" | custom-call | tf_op jit(solution)/shard_map/feed_back/pallas_call | solution.py:46
  106.2 1.5 collective-permute-done.10.refs_7_
  109.5 4.1 %step.7 = (bf16[4,128,512]{2,1,0:T(8,128)(2,1)}, bf16[4,128,512]{2,1,0:T(8,128)(2,1)}, bf16[4,128,512]{2,1,0:T(8,128)(2,1)}, bf16[4,128,512]{2,1,0:T(8,128)(2,1)}) custom-call(s32[2]{0:T(128)S(1)} %pad_add_fusion.place_ref, bf16[8,128,512]{2,1,0:T(8,128)(2,1)} %get-tuple-element.140.refs_8_.refs_0_, bf16[8,128,512]{2,1,0:T(8,128)(2,1)} %copy-done.36, ...), custom_call_target="tpu_custom_call" | custom-call | flops 2300000000 | tf_op jit(solution)/shard_map/step/pallas_call | solution.py:46
  114.7 1.5 collective-permute-start.18
  117.0 11.5 %middle_back.1 = (bf16[1024,1024]{1,0:T(8,128)(2,1)}, f32[512,1024]{1,0:T(8,128)}, bf16[1024,512]{1,0:T(8,128)(2,1)}, f32[8,1024]{1,0:T(8,128)}) custom-call(s32[2]{0:T(128)S(1)} %pad_add_fusion.place_ref, f32[1024,1024]{1,0:T(8,128)} %get-tuple-element.137.refs_0_, bf16[1024,1024]{1,0:T(8,128)(2,1)} %get-tuple-element.131.refs_10_.refs_1_, ...), custom_call_target="tpu_custom_call" | custom-call | tf_op jit(solution)/shard_map/middle_back/pallas_call | solution.py:46
  128.6 15.3 %attend_back.2 = (bf16[1024,256]{1,0:T(8,128)(2,1)}, bf16[1024,256]{1,0:T(8,128)(2,1)}, bf16[1024,256]{1,0:T(8,128)(2,1)}) custom-call(s32[2]{0:T(128)S(1)} %pad_add_fusion.place_ref, bf16[1024,512]{1,0:T(8,128)(2,1)} %get-tuple-element.124.refs_0_, bf16[1024,512]{1,0:T(8,128)(2,1)} %get-tuple-element.125.refs_1_, ...), custom_call_target="tpu_custom_call" | custom-call | tf_op jit(solution)/shard_map/attend_back/pallas_call | solution.py:46
  143.9 8.0 %attention_grad.2 = (bf16[512,768]{1,0:T(8,128)(2,1)}, bf16[512,768]{1,0:T(8,128)(2,1)}, bf16[8,64,640]{2,1,0:T(8,128)(2,1)}, bf16[8,64,640]{2,1,0:T(8,128)(2,1)...) custom-call(s32[2]{0:T(128)S(1)} %pad_add_fusion.place_ref, bf16[1024,1024]{1,0:T(8,128)(2,1)} %get-tuple-element.136.refs_0_, ...), custom_call_target="tpu_custom_call" | custom-call | tf_op jit(solution)/shard_map/attention_grad/pallas_call | solution.py:46
  154.3 3.2 %step.8 = (bf16[2,256,512]{2,1,0:T(8,128)(2,1)}, bf16[2,256,512]{2,1,0:T(8,128)(2,1)}) custom-call(s32[2]{0:T(128)S(1)} %pad_add_fusion.place_ref, bf16[4,128,512]{2,1,0:T(8,128)(2,1)} %get-tuple-element.148.refs_12_.refs_0_, bf16[4,128,512]{2,1,0:T(8,128)(2,1)} %copy-done.43, bf16[4,128,512]{2,1,0:T(8,128)(2,1)} %get-tuple-element.156.refs_2_, ...), custom_call_target="tpu_custom_call" | custom-call | flops 2300000000 | tf_op jit(solution)/shard_map/step/pallas_call | solution.py:46
  157.5 1.6 collective-permute-start.23
  160.4 4.2 %step.9 = (bf16[4,64,1024]{2,1,0:T(8,128)(2,1)}, bf16[4,64,1024]{2,1,0:T(8,128)(2,1)}, bf16[4,64,1024]{2,1,0:T(8,128)(2,1)}, bf16[4,64,1024]{2,1,0:T(8,128)(2,1)}) custom-call(s32[2]{0:T(128)S(1)} %pad_add_fusion.place_ref, bf16[8,64,1024]{2,1,0:T(8,128)(2,1)} %get-tuple-element.151.refs_0_, bf16[8,64,1024]{2,1,0:T(8,128)(2,1)} %copy-done.34, ...), custom_call_target="tpu_custom_call" | custom-call | flops 2300000000 | tf_op jit(solution)/shard_map/step/pallas_call | solution.py:46
  164.6 3.5 %collective-permute-done.24.refs_7_ = bf16[8,64,640]{2,1,0:T(8,128)(2,1)S(1)} collective-permute-done((bf16[8,64,640]{2,1,0:T(8,128)(2,1)}, bf16[8,64,640]{2,1,0:T(8,128)(2,1)S(1)}, u32[]{:S(2)}, u32[]{:S(2)}) %collective-permute-start.24) | collective-permute-done | bytes 655392 | tf_op jit(solution)/shard_map/ppermute | solution.py:1095
  168.1 1.2 collective-permute-start.21
  170.2 14.9 %attend_back.3 = (bf16[1024,256]{1,0:T(8,128)(2,1)}, bf16[1024,256]{1,0:T(8,128)(2,1)}, bf16[1024,256]{1,0:T(8,128)(2,1)}) custom-call(s32[2]{0:T(128)S(1)} %pad_add_fusion.place_ref, bf16[1024,512]{1,0:T(8,128)(2,1)} %get-tuple-element.124.refs_0_, bf16[1024,512]{1,0:T(8,128)(2,1)} %get-tuple-element.125.refs_1_, ...), custom_call_target="tpu_custom_call" | custom-call | tf_op jit(solution)/shard_map/attend_back/pallas_call | solution.py:46
  185.2 5.7 %attention_grad.3 = (bf16[512,768]{1,0:T(8,128)(2,1)}, bf16[512,768]{1,0:T(8,128)(2,1)}, bf16[8,64,384]{2,1,0:T(8,128)(2,1)}, bf16[8,64,384]{2,1,0:T(8,128)(2,1)...) custom-call(s32[2]{0:T(128)S(1)} %pad_add_fusion.place_ref, bf16[1024,1024]{1,0:T(8,128)(2,1)} %get-tuple-element.136.refs_0_, ...), custom_call_target="tpu_custom_call" | custom-call | tf_op jit(solution)/shard_map/attention_grad/pallas_call | solution.py:46
  191.8 1.2 collective-permute-start.19
  193.8 4.9 %step.10 = (bf16[2,128,1024]{2,1,0:T(8,128)(2,1)}, bf16[2,128,1024]{2,1,0:T(8,128)(2,1)}, bf16[1,256,512]{2,1,0:T(8,128)(2,1)}, bf16[1,256,512]{2,1,0:T(8,128)(2...) custom-call(s32[2]{0:T(128)S(1)} %pad_add_fusion.place_ref, ...), custom_call_target="tpu_custom_call" | custom-call | flops 2300000000 | tf_op jit(solution)/shard_map/step/pallas_call | solution.py:46
  198.7 1.7 collective-permute-start.26
  201.1 2.4 collective-permute-done.19.refs_1_
  206.3 10.7 %hidden_back.1 = (bf16[256,1024]{1,0:T(8,128)(2,1)}, bf16[256,1024]{1,0:T(8,128)(2,1)}, f32[8,1024]{1,0:T(8,128)}) custom-call(s32[2]{0:T(128)S(1)} %pad_add_fusion.place_ref, bf16[2,2,256,1024]{3,2,1,0:T(8,128)(2,1)} %bitcast.43, f32[512,1024]{1,0:T(8,128)} %get-tuple-element.188.refs_1_, f32[8,1024]{1,0:T(8,128)} %convert_element_type.13.refs_2_.refs_1_, ...), custom_call_target="tpu_custom_call" | custom-call | tf_op jit(solution)/shard_map/hidden_back/pallas_call | solution.py:46
  219.0 3.9 %step.11 = (bf16[4,64,384]{2,1,0:T(8,128)(2,1)}, bf16[4,64,384]{2,1,0:T(8,128)(2,1)}, bf16[4,64,384]{2,1,0:T(8,128)(2,1)}, bf16[4,64,384]{2,1,0:T(8,128)(2,1)}, ...) custom-call(s32[2]{0:T(128)S(1)} %pad_add_fusion.place_ref, ...), custom_call_target="tpu_custom_call" | custom-call | flops 2300000000 | tf_op jit(solution)/shard_map/step/pallas_call | solution.py:46
  222.9 1.6 collective-permute-start.35
  225.2 3.8 %all-to-all-start = ((f32[32,1,384]{2,1,0:T(1,128)}), f32[32,1,384]{2,1,0:T(1,128)S(1)}, u32[]{:S(2)}, u32[]{:S(2)}) async-start(f32[32,1,384]{2,1,0:T(1,128)} %copy.48), calls=%async_computation | async-start | bytes 98304 | tf_op jit(solution)/shard_map/all_to_all | solution.py:1281
  229.0 1.8 collective-permute-start.32
  230.9 5.6 %all-to-all-done = f32[32,1,384]{2,1,0:T(1,128)S(1)} async-done(((f32[32,1,384]{2,1,0:T(1,128)}), f32[32,1,384]{2,1,0:T(1,128)S(1)}, u32[]{:S(2)}, u32[]{:S(2)}) %all-to-all-start) | async-done | bytes 49184 | tf_op jit(solution)/shard_map/all_to_all | solution.py:1281
  240.8 10.7 %feed_down.1 = (bf16[256,1024]{1,0:T(8,128)(2,1)}, bf16[256,1024]{1,0:T(8,128)(2,1)}) custom-call(s32[2]{0:T(128)S(1)} %pad_add_fusion.place_ref, bf16[16,2,128,1024]{3,2,1,0:T(8,128)(2,1)} %bitcast.42, f32[512,1024]{1,0:T(8,128)} %get-tuple-element.132.refs_1_, f32[8,1024]{1,0:T(8,128)} %convert_element_type.13.refs_2_.refs_1_, ...), custom_call_target="tpu_custom_call" | custom-call | tf_op jit(solution)/shard_map/feed_down/pallas_call | solution.py:46
  251.5 1.8 collective-permute-start.40
  253.3 1.4 collective-permute-start.31
  254.7 2.9 %step.12 = (bf16[2,128,384]{2,1,0:T(8,128)(2,1)}, bf16[2,128,384]{2,1,0:T(8,128)(2,1)}, bf16[1,128,640]{2,1,0:T(8,128)(2,1)}, bf16[1,128,640]{2,1,0:T(8,128)(2,1)}) custom-call(s32[2]{0:T(128)S(1)} %pad_add_fusion.place_ref, bf16[4,64,384]{2,1,0:T(8,128)(2,1)} %get-tuple-element.192.refs_5_.refs_0_, bf16[4,64,384]{2,1,0:T(8,128)(2,1)} %copy-done.48, ...), custom_call_target="tpu_custom_call" | custom-call | flops 2300000000 | tf_op jit(solution)/shard_map/step/pallas_call | solution.py:46
  259.4 1.5 collective-permute-start.36
  260.8 6.7 %collective-permute-done.37.refs_1_ = bf16[2,128,384]{2,1,0:T(8,128)(2,1)S(1)} collective-permute-done((bf16[2,128,384]{2,1,0:T(8,128)(2,1)}, bf16[2,128,384]{2,1,0:T(8,128)(2,1)S(1)}, u32[]{:S(2)}, u32[]{:S(2)}) %collective-permute-start.37) | collective-permute-done | bytes 196640 | tf_op jit(solution)/shard_map/ppermute | solution.py:1095
  268.2 2.3 step.13
  271.2 2.7 part_rows.2
  274.0 1.5 collective-permute-done.41.refs_1_
  276.2 2.4 emit.2.refs_4_
  279.2 2.5 part_rows.3
  283.9 2.4 emit.3
  (216 shorter events, 38.5 us)
Async XLA Ops:
  0.6 46.9 %copy-start = (bf16[4096]{0:T(1024)(128)(2,1)S(1)}, bf16[4096]{0:T(1024)(128)(2,1)}, u32[]{:S(2)}) copy-start(bf16[4096]{0:T(1024)(128)(2,1)} %param.27) | copy-start | bytes 24580
  2.0 4.0 %collective-permute-start.2 = (bf16[256,1024]{1,0:T(8,128)(2,1)S(1)}, bf16[256,1024]{1,0:T(8,128)(2,1)S(1)}, u32[]{:S(2)}, u32[]{:S(2)}) collective-permute-start(bf16[256,1024]{1,0:T(8,128)(2,1)S(1)} %get-tuple-element.282.refs_0_), channel_id=1, source_target_pairs={{0,1},{1,0},{2,3},{3,2},{4,5},{5,4},{6,7},{7,6},{8,9},{9,8},{10,11... | collective-permute-start | bytes 1572872 | tf_op jit(solution)/shard_map/ppermute | solution.py:1067
  2.6 15.4 %collective-permute-start = (bf16[256,1024]{1,0:T(8,128)(2,1)S(1)}, bf16[256,1024]{1,0:T(8,128)(2,1)S(1)}, u32[]{:S(2)}, u32[]{:S(2)}) collective-permute-start(bf16[256,1024]{1,0:T(8,128)(2,1)S(1)} %get-tuple-element.283), channel_id=1, source_target_pairs={{0,2},{1,3},{2,0},{3,1},{4,6},{5,7},{6,4},{7,5},{8,10},{9,11},{10,... | collective-permute-start | bytes 1572872 | tf_op jit(solution)/shard_map/ppermute | solution.py:1061
  6.0 11.9 %copy-start.52 = (s32[2,1,16]{2,1,0:T(1,128)S(1)}, s32[2,1,16]{2,1,0:T(1,128)}, u32[]{:S(2)}) copy-start(s32[2,1,16]{2,1,0:T(1,128)} %param.17) | copy-start | bytes 388
  14.1 23.5 %collective-permute-start.6 = (bf16[256,1024]{1,0:T(8,128)(2,1)}, bf16[256,1024]{1,0:T(8,128)(2,1)S(1)}, u32[]{:S(2)}, u32[]{:S(2)}) collective-permute-start(bf16[256,1024]{1,0:T(8,128)(2,1)} %get-tuple-element.130), channel_id=1, source_target_pairs={{0,2},{1,3},{2,0},{3,1},{4,6},{5,7},{6,4},{7,5},{8,10},{9,11},{10,... | collective-permute-start | bytes 1572872 | tf_op jit(solution)/shard_map/ppermute | solution.py:1061
  17.9 1.9 collective-permute-start.1
  18.3 29.9 %collective-permute-start.5 = (bf16[256,1024]{1,0:T(8,128)(2,1)}, bf16[256,1024]{1,0:T(8,128)(2,1)S(1)}, u32[]{:S(2)}, u32[]{:S(2)}) collective-permute-start(bf16[256,1024]{1,0:T(8,128)(2,1)} %get-tuple-element.129.refs_0_), channel_id=1, source_target_pairs={{0,1},{1,0},{2,3},{3,2},{4,5},{5,4},{6,7},{7,6},{8,9},{9,8},{10,11... | collective-permute-start | bytes 1572872 | tf_op jit(solution)/shard_map/ppermute | solution.py:1067
  37.5 16.1 %collective-permute-start.3 = (bf16[1024,256]{1,0:T(8,128)(2,1)}, bf16[1024,256]{1,0:T(8,128)(2,1)S(1)}, u32[]{:S(2)}, u32[]{:S(2)}) collective-permute-start(bf16[1024,256]{1,0:T(8,128)(2,1)} %get-tuple-element.127.refs_5_.refs_2_.refs_4_), channel_id=1, source_target_pairs={{0,1},{1,0},{2,3},{3,2},{4,5},{5,4},{6,7},{7,6},{8,9},{9,8},{10,11... | collective-permute-start | bytes 1572872 | tf_op jit(solution)/shard_map/ppermute | solution.py:1067
  37.6 10.6 %collective-permute-start.7 = (bf16[256,1024]{1,0:T(8,128)(2,1)S(1)}, bf16[256,1024]{1,0:T(8,128)(2,1)S(1)}, u32[]{:S(2)}, u32[]{:S(2)}) collective-permute-start(bf16[256,1024]{1,0:T(8,128)(2,1)S(1)} %collective-permute-done.6.refs_2_), channel_id=1, source_target_pairs={{0,1},{1,0},{2,3},{3,2},{4,5},{5,4},{6,7},{7,6},{8,9},{9,8},{10,11... | collective-permute-start | bytes 1572872 | tf_op jit(solution)/shard_map/ppermute | solution.py:1067
  47.4 6.2 %collective-permute-start.4 = (bf16[1024,256]{1,0:T(8,128)(2,1)}, bf16[1024,256]{1,0:T(8,128)(2,1)S(1)}, u32[]{:S(2)}, u32[]{:S(2)}) collective-permute-start(bf16[1024,256]{1,0:T(8,128)(2,1)} %get-tuple-element.128.refs_4_.refs_7_), channel_id=1, source_target_pairs={{0,1},{1,0},{2,3},{3,2},{4,5},{5,4},{6,7},{7,6},{8,9},{9,8},{10,11... | collective-permute-start | bytes 1572872 | tf_op jit(solution)/shard_map/ppermute | solution.py:1067
  79.6 28.3 %collective-permute-start.13 = (bf16[8,128,512]{2,1,0:T(8,128)(2,1)}, bf16[8,128,512]{2,1,0:T(8,128)(2,1)S(1)}, u32[]{:S(2)}, u32[]{:S(2)}) collective-permute-start(bf16[8,128,512]{2,1,0:T(8,128)(2,1)} %get-tuple-element.145), channel_id=1, source_target_pairs={{0,4},{4,0},{8,12},{12,8},{16,20},{20,16},{24,28},{28,24},{1,5},{5... | collective-permute-start | bytes 3145736 | tf_op jit(solution)/shard_map/ppermute | solution.py:1095
  81.6 26.9 %collective-permute-start.14 = (bf16[8,128,512]{2,1,0:T(8,128)(2,1)}, bf16[8,128,512]{2,1,0:T(8,128)(2,1)S(1)}, u32[]{:S(2)}, u32[]{:S(2)}) collective-permute-start(bf16[8,128,512]{2,1,0:T(8,128)(2,1)} %get-tuple-element.147), channel_id=1, source_target_pairs={{0,2},{1,3},{2,0},{3,1},{4,6},{5,7},{6,4},{7,5},{8,10},{9,11},{10,... | collective-permute-start | bytes 3145736 | tf_op jit(solution)/shard_map/ppermute | solution.py:1061
  105.6 2.2 collective-permute-start.10
  105.7 7.9 %collective-permute-start.11 = (bf16[256,1024]{1,0:T(8,128)(2,1)}, bf16[256,1024]{1,0:T(8,128)(2,1)S(1)}, u32[]{:S(2)}, u32[]{:S(2)}) collective-permute-start(bf16[256,1024]{1,0:T(8,128)(2,1)} %get-tuple-element.143.refs_8_), channel_id=1, source_target_pairs={{0,1},{1,0},{2,3},{3,2},{4,5},{5,4},{6,7},{7,6},{8,9},{9,8},{10,11... | collective-permute-start | bytes 1572872 | tf_op jit(solution)/shard_map/ppermute | solution.py:1067
  106.2 8.6 %collective-permute-start.12 = (bf16[256,1024]{1,0:T(8,128)(2,1)}, bf16[256,1024]{1,0:T(8,128)(2,1)S(1)}, u32[]{:S(2)}, u32[]{:S(2)}) collective-permute-start(bf16[256,1024]{1,0:T(8,128)(2,1)} %get-tuple-element.144.refs_10_), channel_id=1, source_target_pairs={{0,1},{1,0},{2,3},{3,2},{4,5},{5,4},{6,7},{7,6},{8,9},{9,8},{10,11... | collective-permute-start | bytes 1572872 | tf_op jit(solution)/shard_map/ppermute | solution.py:1067
  107.8 8.4 %collective-permute-start.9 = (bf16[256,1024]{1,0:T(8,128)(2,1)}, bf16[256,1024]{1,0:T(8,128)(2,1)S(1)}, u32[]{:S(2)}, u32[]{:S(2)}) collective-permute-start(bf16[256,1024]{1,0:T(8,128)(2,1)} %get-tuple-element.141.refs_4_), channel_id=1, source_target_pairs={{0,1},{1,0},{2,3},{3,2},{4,5},{5,4},{6,7},{7,6},{8,9},{9,8},{10,11... | collective-permute-start | bytes 1572872 | tf_op jit(solution)/shard_map/ppermute | solution.py:1067
  107.9 51.2 %collective-permute-start.15 = (bf16[8,64,1024]{2,1,0:T(8,128)(2,1)}, bf16[8,64,1024]{2,1,0:T(8,128)(2,1)S(1)}, u32[]{:S(2)}, u32[]{:S(2)}) collective-permute-start(bf16[8,64,1024]{2,1,0:T(8,128)(2,1)} %get-tuple-element.152), channel_id=1, source_target_pairs={{0,4},{4,0},{8,12},{12,8},{16,20},{20,16},{24,28},{28,24},{1,5},{5... | collective-permute-start | bytes 3145736 | tf_op jit(solution)/shard_map/ppermute | solution.py:1095
  108.5 50.6 %collective-permute-start.16 = (bf16[8,64,1024]{2,1,0:T(8,128)(2,1)}, bf16[8,64,1024]{2,1,0:T(8,128)(2,1)S(1)}, u32[]{:S(2)}, u32[]{:S(2)}) collective-permute-start(bf16[8,64,1024]{2,1,0:T(8,128)(2,1)} %get-tuple-element.154), channel_id=1, source_target_pairs={{0,2},{1,3},{2,0},{3,1},{4,6},{5,7},{6,4},{7,5},{8,10},{9,11},{10,... | collective-permute-start | bytes 3145736 | tf_op jit(solution)/shard_map/ppermute | solution.py:1061
  113.6 38.9 %collective-permute-start.17 = (bf16[4,128,512]{2,1,0:T(8,128)(2,1)}, bf16[4,128,512]{2,1,0:T(8,128)(2,1)S(1)}, u32[]{:S(2)}, u32[]{:S(2)}) collective-permute-start(bf16[4,128,512]{2,1,0:T(8,128)(2,1)} %get-tuple-element.155), channel_id=1, source_target_pairs={{0,2},{1,3},{2,0},{3,1},{4,6},{5,7},{6,4},{7,5},{8,10},{9,11},{10,... | collective-permute-start | bytes 1572872 | tf_op jit(solution)/shard_map/ppermute | solution.py:1061
  114.7 38.7 %collective-permute-start.18 = (bf16[4,128,512]{2,1,0:T(8,128)(2,1)}, bf16[4,128,512]{2,1,0:T(8,128)(2,1)S(1)}, u32[]{:S(2)}, u32[]{:S(2)}) collective-permute-start(bf16[4,128,512]{2,1,0:T(8,128)(2,1)} %get-tuple-element.157), channel_id=1, source_target_pairs={{0,4},{4,0},{8,12},{12,8},{16,20},{20,16},{24,28},{28,24},{1,5},{5... | collective-permute-start | bytes 1572872 | tf_op jit(solution)/shard_map/ppermute | solution.py:1095
  151.9 16.1 %collective-permute-start.24 = (bf16[8,64,640]{2,1,0:T(8,128)(2,1)}, bf16[8,64,640]{2,1,0:T(8,128)(2,1)S(1)}, u32[]{:S(2)}, u32[]{:S(2)}) collective-permute-start(bf16[8,64,640]{2,1,0:T(8,128)(2,1)} %get-tuple-element.178), channel_id=1, source_target_pairs={{0,4},{4,0},{8,12},{12,8},{16,20},{20,16},{24,28},{28,24},{1,5},{5... | collective-permute-start | bytes 1966088 | tf_op jit(solution)/shard_map/ppermute | solution.py:1095
  152.5 16.8 %collective-permute-start.25 = (bf16[8,64,640]{2,1,0:T(8,128)(2,1)}, bf16[8,64,640]{2,1,0:T(8,128)(2,1)S(1)}, u32[]{:S(2)}, u32[]{:S(2)}) collective-permute-start(bf16[8,64,640]{2,1,0:T(8,128)(2,1)} %get-tuple-element.180), channel_id=1, source_target_pairs={{0,2},{1,3},{2,0},{3,1},{4,6},{5,7},{6,4},{7,5},{8,10},{9,11},{10,... | collective-permute-start | bytes 1966088 | tf_op jit(solution)/shard_map/ppermute | solution.py:1061
  157.5 33.3 %collective-permute-start.23 = (bf16[2,256,512]{2,1,0:T(8,128)(2,1)}, bf16[2,256,512]{2,1,0:T(8,128)(2,1)S(1)}, u32[]{:S(2)}, u32[]{:S(2)}) collective-permute-start(bf16[2,256,512]{2,1,0:T(8,128)(2,1)} %get-tuple-element.176), channel_id=1, source_target_pairs={{0,8},{4,12},{8,0},{12,4},{16,24},{20,28},{24,16},{28,20},{1,9},{5... | collective-permute-start | bytes 1572872 | tf_op jit(solution)/shard_map/ppermute | solution.py:1095
  159.1 80.4 %collective-permute-start.8 = (bf16[512,2048]{1,0:T(8,128)(2,1)}, bf16[512,2048]{1,0:T(8,128)(2,1)S(1)}, u32[]{:S(2)}, u32[]{:S(2)}) collective-permute-start(bf16[512,2048]{1,0:T(8,128)(2,1)} %get-tuple-element.135), channel_id=1, source_target_pairs={{0,1},{1,0},{2,3},{3,2},{4,5},{5,4},{6,7},{7,6},{8,9},{9,8},{10,11... | collective-permute-start | bytes 6291464 | tf_op jit(solution)/shard_map/ppermute | solution.py:1067
  159.1 39.6 %collective-permute-start.29 = (bf16[512,768]{1,0:T(8,128)(2,1)}, bf16[512,768]{1,0:T(8,128)(2,1)S(1)}, u32[]{:S(2)}, u32[]{:S(2)}) collective-permute-start(bf16[512,768]{1,0:T(8,128)(2,1)} %get-tuple-element.189), channel_id=1, source_target_pairs={{0,1},{1,0},{2,3},{3,2},{4,5},{5,4},{6,7},{7,6},{8,9},{9,8},{10,11... | collective-permute-start | bytes 2359304 | tf_op jit(solution)/shard_map/ppermute | solution.py:1067
  168.1 23.7 %collective-permute-start.21 = (bf16[4,64,1024]{2,1,0:T(8,128)(2,1)}, bf16[4,64,1024]{2,1,0:T(8,128)(2,1)}, u32[]{:S(2)}, u32[]{:S(2)}) collective-permute-start(bf16[4,64,1024]{2,1,0:T(8,128)(2,1)} %get-tuple-element.173), channel_id=1, source_target_pairs={{0,2},{1,3},{2,0},{3,1},{4,6},{5,7},{6,4},{7,5},{8,10},{9,11},{10,... | collective-permute-start | bytes 1572872 | tf_op jit(solution)/shard_map/ppermute | solution.py:1061
  169.3 23.7 %collective-permute-start.22 = (bf16[4,64,1024]{2,1,0:T(8,128)(2,1)}, bf16[4,64,1024]{2,1,0:T(8,128)(2,1)}, u32[]{:S(2)}, u32[]{:S(2)}) collective-permute-start(bf16[4,64,1024]{2,1,0:T(8,128)(2,1)} %get-tuple-element.175), channel_id=1, source_target_pairs={{0,4},{4,0},{8,12},{12,8},{16,20},{20,16},{24,28},{28,24},{1,5},{5... | collective-permute-start | bytes 1572872 | tf_op jit(solution)/shard_map/ppermute | solution.py:1095
  190.8 13.6 %collective-permute-start.30 = (bf16[512,768]{1,0:T(8,128)(2,1)}, bf16[512,768]{1,0:T(8,128)(2,1)S(1)}, u32[]{:S(2)}, u32[]{:S(2)}) collective-permute-start(bf16[512,768]{1,0:T(8,128)(2,1)} %get-tuple-element.190), channel_id=1, source_target_pairs={{0,1},{1,0},{2,3},{3,2},{4,5},{5,4},{6,7},{7,6},{8,9},{9,8},{10,11... | collective-permute-start | bytes 2359304 | tf_op jit(solution)/shard_map/ppermute | solution.py:1067
  191.8 11.7 %collective-permute-start.19 = (bf16[8,64,384]{2,1,0:T(8,128)(2,1)}, bf16[8,64,384]{2,1,0:T(8,128)(2,1)S(1)}, u32[]{:S(2)}, u32[]{:S(2)}) collective-permute-start(bf16[8,64,384]{2,1,0:T(8,128)(2,1)} %get-tuple-element.170), channel_id=1, source_target_pairs={{0,4},{4,0},{8,12},{12,8},{16,20},{20,16},{24,28},{28,24},{1,5},{5... | collective-permute-start | bytes 1179656 | tf_op jit(solution)/shard_map/ppermute | solution.py:1095
  193.0 25.1 %collective-permute-start.20 = (bf16[8,64,384]{2,1,0:T(8,128)(2,1)}, bf16[8,64,384]{2,1,0:T(8,128)(2,1)}, u32[]{:S(2)}, u32[]{:S(2)}) collective-permute-start(bf16[8,64,384]{2,1,0:T(8,128)(2,1)} %get-tuple-element.172), channel_id=1, source_target_pairs={{0,2},{1,3},{2,0},{3,1},{4,6},{5,7},{6,4},{7,5},{8,10},{9,11},{10,... | collective-permute-start | bytes 1179656 | tf_op jit(solution)/shard_map/ppermute | solution.py:1061
  198.7 19.5 %collective-permute-start.26 = (bf16[2,128,1024]{2,1,0:T(8,128)(2,1)}, bf16[2,128,1024]{2,1,0:T(8,128)(2,1)S(1)}, u32[]{:S(2)}, u32[]{:S(2)}) collective-permute-start(bf16[2,128,1024]{2,1,0:T(8,128)(2,1)} %get-tuple-element.183), channel_id=1, source_target_pairs={{0,8},{4,12},{8,0},{12,4},{16,24},{20,28},{24,16},{28,20},{1,9},{5... | collective-permute-start | bytes 1572872 | tf_op jit(solution)/shard_map/ppermute | solution.py:1095
  203.5 14.6 %collective-permute-start.27 = (bf16[4,64,640]{2,1,0:T(8,128)(2,1)}, bf16[4,64,640]{2,1,0:T(8,128)(2,1)}, u32[]{:S(2)}, u32[]{:S(2)}) collective-permute-start(bf16[4,64,640]{2,1,0:T(8,128)(2,1)} %get-tuple-element.185), channel_id=1, source_target_pairs={{0,2},{1,3},{2,0},{3,1},{4,6},{5,7},{6,4},{7,5},{8,10},{9,11},{10,... | collective-permute-start | bytes 983048 | tf_op jit(solution)/shard_map/ppermute | solution.py:1061
  204.4 13.7 %collective-permute-start.28 = (bf16[4,64,640]{2,1,0:T(8,128)(2,1)}, bf16[4,64,640]{2,1,0:T(8,128)(2,1)}, u32[]{:S(2)}, u32[]{:S(2)}) collective-permute-start(bf16[4,64,640]{2,1,0:T(8,128)(2,1)} %get-tuple-element.187), channel_id=1, source_target_pairs={{0,4},{4,0},{8,12},{12,8},{16,20},{20,16},{24,28},{28,24},{1,5},{5... | collective-permute-start | bytes 983048 | tf_op jit(solution)/shard_map/ppermute | solution.py:1095
  219.0 20.5 %copy-start.46 = (bf16[1,256,512]{2,1,0:T(8,128)(2,1)S(1)}, bf16[1,256,512]{2,1,0:T(8,128)(2,1)}, u32[]{:S(2)}) copy-start(bf16[1,256,512]{2,1,0:T(8,128)(2,1)} %get-tuple-element.212) | copy-start | bytes 786436
  222.9 31.8 %collective-permute-start.35 = (bf16[2,128,640]{2,1,0:T(8,128)(2,1)}, bf16[2,128,640]{2,1,0:T(8,128)(2,1)}, u32[]{:S(2)}, u32[]{:S(2)}) collective-permute-start(bf16[2,128,640]{2,1,0:T(8,128)(2,1)} %get-tuple-element.204), channel_id=1, source_target_pairs={{0,8},{4,12},{8,0},{12,4},{16,24},{20,28},{24,16},{28,20},{1,9},{5... | collective-permute-start | bytes 983048 | tf_op jit(solution)/shard_map/ppermute | solution.py:1095
  225.2 11.3 %all-to-all-start = ((f32[32,1,384]{2,1,0:T(1,128)}), f32[32,1,384]{2,1,0:T(1,128)S(1)}, u32[]{:S(2)}, u32[]{:S(2)}) async-start(f32[32,1,384]{2,1,0:T(1,128)} %copy.48), calls=%async_computation | async-start | bytes 98304 | tf_op jit(solution)/shard_map/all_to_all | solution.py:1281
  229.0 29.2 %collective-permute-start.32 = (bf16[256,1024]{1,0:T(8,128)(2,1)S(1)}, bf16[256,1024]{1,0:T(8,128)(2,1)S(1)}, u32[]{:S(2)}, u32[]{:S(2)}) collective-permute-start(bf16[256,1024]{1,0:T(8,128)(2,1)S(1)} %copy-done.40), channel_id=1, source_target_pairs={{0,2},{1,3},{2,0},{3,1},{4,6},{5,7},{6,4},{7,5},{8,10},{9,11},{10,... | collective-permute-start | bytes 1572872 | tf_op jit(solution)/shard_map/ppermute | solution.py:1061
  237.7 13.8 %collective-permute-start.33 = (bf16[4,64,384]{2,1,0:T(8,128)(2,1)}, bf16[4,64,384]{2,1,0:T(8,128)(2,1)S(1)}, u32[]{:S(2)}, u32[]{:S(2)}) collective-permute-start(bf16[4,64,384]{2,1,0:T(8,128)(2,1)} %get-tuple-element.200), channel_id=1, source_target_pairs={{0,2},{1,3},{2,0},{3,1},{4,6},{5,7},{6,4},{7,5},{8,10},{9,11},{10,... | collective-permute-start | bytes 589832 | tf_op jit(solution)/shard_map/ppermute | solution.py:1061
  238.1 15.2 %collective-permute-start.34 = (bf16[4,64,384]{2,1,0:T(8,128)(2,1)}, bf16[4,64,384]{2,1,0:T(8,128)(2,1)S(1)}, u32[]{:S(2)}, u32[]{:S(2)}) collective-permute-start(bf16[4,64,384]{2,1,0:T(8,128)(2,1)} %get-tuple-element.202), channel_id=1, source_target_pairs={{0,4},{4,0},{8,12},{12,8},{16,20},{20,16},{24,28},{28,24},{1,5},{5... | collective-permute-start | bytes 589832 | tf_op jit(solution)/shard_map/ppermute | solution.py:1095
  239.5 31.0 %collective-permute-start.39 = (bf16[1,256,512]{2,1,0:T(8,128)(2,1)S(1)}, bf16[1,256,512]{2,1,0:T(8,128)(2,1)S(1)}, u32[]{:S(2)}, u32[]{:S(2)}) collective-permute-start(bf16[1,256,512]{2,1,0:T(8,128)(2,1)S(1)} %copy-done.46), channel_id=1, source_target_pairs={{0,16},{4,20},{8,24},{12,28},{16,0},{20,4},{24,8},{28,12},{1,17},{... | collective-permute-start | bytes 786440 | tf_op jit(solution)/shard_map/ppermute | solution.py:1095
  240.8 10.7 %copy-start.47 = (bf16[1,128,1024]{2,1,0:T(8,128)(2,1)S(1)}, bf16[1,128,1024]{2,1,0:T(8,128)(2,1)}, u32[]{:S(2)}) copy-start(bf16[1,128,1024]{2,1,0:T(8,128)(2,1)} %get-tuple-element.214) | copy-start | bytes 786436
  251.5 18.9 %collective-permute-start.40 = (bf16[1,128,1024]{2,1,0:T(8,128)(2,1)S(1)}, bf16[1,128,1024]{2,1,0:T(8,128)(2,1)S(1)}, u32[]{:S(2)}, u32[]{:S(2)}) collective-permute-start(bf16[1,128,1024]{2,1,0:T(8,128)(2,1)S(1)} %copy-done.47), channel_id=1, source_target_pairs={{0,16},{4,20},{8,24},{12,28},{16,0},{20,4},{24,8},{28,12},{1,17},{... | collective-permute-start | bytes 786440 | tf_op jit(solution)/shard_map/ppermute | solution.py:1095
  253.3 20.6 %collective-permute-start.31 = (bf16[256,1024]{1,0:T(8,128)(2,1)}, bf16[256,1024]{1,0:T(8,128)(2,1)S(1)}, u32[]{:S(2)}, u32[]{:S(2)}) collective-permute-start(bf16[256,1024]{1,0:T(8,128)(2,1)} %get-tuple-element.194), channel_id=1, source_target_pairs={{0,2},{1,3},{2,0},{3,1},{4,6},{5,7},{6,4},{7,5},{8,10},{9,11},{10,... | collective-permute-start | bytes 1572872 | tf_op jit(solution)/shard_map/ppermute | solution.py:1061
  257.6 9.9 %collective-permute-start.37 = (bf16[2,128,384]{2,1,0:T(8,128)(2,1)}, bf16[2,128,384]{2,1,0:T(8,128)(2,1)S(1)}, u32[]{:S(2)}, u32[]{:S(2)}) collective-permute-start(bf16[2,128,384]{2,1,0:T(8,128)(2,1)} %get-tuple-element.208), channel_id=1, source_target_pairs={{0,8},{4,12},{8,0},{12,4},{16,24},{20,28},{24,16},{28,20},{1,9},{5... | collective-permute-start | bytes 589832 | tf_op jit(solution)/shard_map/ppermute | solution.py:1095
  259.4 19.2 %collective-permute-start.36 = (bf16[1,128,640]{2,1,0:T(8,128)(2,1)S(1)}, bf16[1,128,640]{2,1,0:T(8,128)(2,1)S(1)}, u32[]{:S(2)}, u32[]{:S(2)}) collective-permute-start(bf16[1,128,640]{2,1,0:T(8,128)(2,1)S(1)} %copy-done.51), channel_id=1, source_target_pairs={{0,16},{4,20},{8,24},{12,28},{16,0},{20,4},{24,8},{28,12},{1,17},{... | collective-permute-start | bytes 491528 | tf_op jit(solution)/shard_map/ppermute | solution.py:1095
  270.4 8.1 %collective-permute-start.38 = (bf16[1,128,384]{2,1,0:T(8,128)(2,1)}, bf16[1,128,384]{2,1,0:T(8,128)(2,1)S(1)}, u32[]{:S(2)}, u32[]{:S(2)}) collective-permute-start(bf16[1,128,384]{2,1,0:T(8,128)(2,1)} %get-tuple-element.210), channel_id=1, source_target_pairs={{0,16},{4,20},{8,24},{12,28},{16,0},{20,4},{24,8},{28,12},{1,17},{... | collective-permute-start | bytes 294920 | tf_op jit(solution)/shard_map/ppermute | solution.py:1095
  273.9 1.6 collective-permute-start.41
  281.7 1.6 collective-permute-start.42
  (49 other events, 138.4 us)
where the time goes:
time: 292 us; the launch traced here: 286 us
  Pallas kernels  196 us (67%)
  starting transfers between devices  38.7 us (13%)
  waiting for transfers between devices  25.3 us (9%)
  local copies, waits for them, and re-layouts  19.2 us (7%)
  other arithmetic  5.68 us (2%)
    pallas_call x26, Pallas kernels, call(): pl.pallas_call(inner, grid_spec=pltpu.PrefetchScalarGridSpec(num_scalar_p...  196 us
    ppermute x16, starting transfers between devices, swap_bit(): lax.ppermute(value, 'dp', [(i, i ^ 1 << bit) for i in range(dp_size)])  17.6 us
    ppermute x12, starting transfers between devices, across(): return lax.ppermute(value, 'ctx', pairs)  14 us
    ppermute x16, waiting for transfers between devices, swap_bit(): lax.ppermute(value, 'dp', [(i, i ^ 1 << bit) for i in range(dp_size)])  12.6 us
    unnamed x107, local copies, waits for them, and re-layouts  12.5 us
  transfers between devices with their start and end apart: 44, of which 9 were waited for; matrix products, arithmetic and copies ran while one was open for 4% of the time, Pallas kernels for 58%

commit v1 on v0

--- a/solution.py
+++ b/solution.py
@@ -8,6 +8,7 @@
 from jax.sharding import PartitionSpec as P
 
 HEADS = 16
+HIDES = {"step": 20, "attend": 40, "project": 6}
 HEAD_DIM = 64
 PAIR = 2 * HEAD_DIM
 NEG = -1e30
@@ -17,8 +18,11 @@
 BF16 = jnp.bfloat16
 F32 = jnp.float32
 VMEM = 60 * 1024 * 1024
-LESS_VMEM = 32 * 1024 * 1024
-DH_PIECES = 4
+LESS_VMEM = 26 * 1024 * 1024
+DH_PIECES = 1
+PIN = True
+KEEP = False
+COST = 6 * 1150 * 1000 * 1000
 
 NT = (((1,), (1,)), ((), ()))
 NN = (((1,), (0,)), ((), ()))
@@ -29,13 +33,15 @@
     return lax.dot_general(left, right, dims, preferred_element_type=F32)
 
 
-def call(kernel, name, place, args, grid, in_specs, outs, scratch=(), after=(), fill=(), vmem=LESS_VMEM):
+def call(kernel, name, place, args, grid, in_specs, outs, scratch=(), after=(), fill=(), cost=0):
     known = len(args)
     skipped = len(after) + len(fill)
-    stays = [len(out) > 3 and bool(out[3]) for out in outs]
+    stays = [len(out) > 3 and out[3] and not place.long for out in outs]
 
     def settled(array):
         pinned = any(array is other for other in place.pinned)
+        if not pinned and any(array is other for other in place.free):
+            return array
         return pltpu.with_memory_space_constraint(array, pltpu.VMEM if pinned else pltpu.HBM)
 
     def inner(place_ref, *refs):
@@ -54,8 +60,8 @@
         ),
         out_shape=[(pltpu.VMEM if stay else pltpu.HBM)(out[0], out[1]) for out, stay in zip(outs, stays)],
         input_output_aliases={first + index: index for index in range(len(fill))},
-        compiler_params=pltpu.CompilerParams(vmem_limit_bytes=vmem),
-        cost_estimate=pl.CostEstimate(flops=int(2*1.15e9) if name=="step" else 0, bytes_accessed=0, transcendentals=0),
+        compiler_params=pltpu.CompilerParams(vmem_limit_bytes=VMEM if place.long else LESS_VMEM),
+        cost_estimate=pl.CostEstimate(flops=int(1.15e9 * HIDES.get(name, 0)), bytes_accessed=0, transcendentals=0),
         name=name,
     )(place.numbers, *[settled(array) for array in (*args, *after, *fill)])
     place.pinned += [array for array, stay in zip(results, stays) if stay]
@@ -63,9 +69,11 @@
 
 
 class Place:
-    def __init__(self, numbers):
+    def __init__(self, numbers, long):
         self.numbers = numbers
+        self.long = long
         self.pinned = []
+        self.free = []
 
 
 def without_bit(number, spot):
@@ -97,11 +105,29 @@
 
 
 def step_kernel(jobs, place, *refs):
-    ins = sum(len(layout) for _, layout in jobs) * 2
+    ins = sum(len(layout) for _, layout, _ in jobs) * 2
     sources = refs[:ins]
     targets = refs[ins:]
-    for job, (spot, layout) in enumerate(jobs):
-        keep_ref, send_ref = targets[2 * job : 2 * job + 2]
+    for spot, layout, parts in jobs:
+        if spot is None:
+            old_ref, came_ref = sources[:2]
+            sources = sources[2:]
+            targets[0][...] = old_ref[0].astype(F32) + came_ref[0].astype(F32)
+            targets = targets[1:]
+            continue
+        if parts == 2:
+            old_ref, came_ref = sources[:2]
+            sources = sources[2:]
+            for index in range(2):
+                rows = pl.ds(index * targets[0].shape[1], targets[0].shape[1])
+                for number in range(old_ref.shape[0]):
+                    value = old_ref[number, rows].astype(F32) + came_ref[number, rows].astype(F32)
+                    target = targets[(number >> spot) & 1]
+                    target[without_bit(number, spot)] = value.astype(target.dtype)
+                targets = targets[2:]
+            continue
+        keep_ref, send_ref = targets[:2]
+        targets = targets[2:]
         columns = keep_ref.shape[2]
         base = 0
         for rows, width in layout:
@@ -117,18 +143,24 @@
             base += rows * (width // columns)
 
 
-def step_call(place, jobs, after=()):
+def step_call(place, jobs, after=(), cost=0):
     ins = []
     outs = []
     layouts = []
-    for arrays, spot in jobs:
+    for arrays, spot, parts in jobs:
         columns = min(array.shape[2] for array in arrays)
         layout = [array.shape[1:] for array in arrays[::2]]
+        if spot is None:
+            layouts.append((None, layout, 1))
+            ins += arrays
+            outs.append((layout[0], F32, pl.BlockSpec(layout[0], lambda i, s: (0, 0))))
+            continue
         rows = sum(rows * (width // columns) for rows, width in layout)
-        shape = (arrays[0].shape[0] // 2, rows, columns)
-        layouts.append((spot, layout))
+        shape = (arrays[0].shape[0] // 2, rows // parts, columns)
+        layouts.append((spot, layout, parts))
         ins += arrays
-        outs += [(shape, arrays[0].dtype, pl.BlockSpec(shape, lambda i, s: (0, 0, 0)))] * 2
+        spec = pl.BlockSpec(shape, lambda i, s: (0, 0, 0))
+        outs += [(shape, arrays[0].dtype, spec, KEEP), (shape, arrays[0].dtype, spec, PIN)] * parts
     return call(
         functools.partial(step_kernel, layouts),
         "step",
@@ -138,18 +170,18 @@
         [pl.BlockSpec(array.shape, lambda i, s: (0, 0, 0)) for array in ins],
         outs,
         after=after,
-    )
-
-
-def hand_out(stage_ref, member, value, out_refs, start=0):
-    group = len(out_refs)
+        cost=cost,
+    )
+
+
+def hand_out(stage_ref, group, member, value, out_refs):
     rows = stage_ref.shape[1]
     stage_ref[...] = value.reshape(stage_ref.shape)
     for steps, out_ref in enumerate(out_refs):
+        first = out_ref.shape[1] - stage_ref.shape[2]
         for block in range(stage_ref.shape[0] // group):
-            out_ref[start + block * rows : start + (block + 1) * rows] = stage_ref[
-                block * group + (member + steps) % group
-            ]
+            part = stage_ref[block * group + (member + steps) % group]
+            out_ref[block * rows : (block + 1) * rows, first:] = part
 
 
 def project_kernel(group, copies, place, *refs):
@@ -278,13 +310,13 @@
         ],
         [((length, width), BF16, out_tile), ((length, width), F32, out_tile)],
         after=after,
-        vmem=LESS_VMEM if length <= 1024 else VMEM,
     )
 
 
 def attend_back_kernel(
     limit,
     sub,
+    grads,
     place,
     q_ref,
     k_ref,
@@ -294,15 +326,13 @@
     lse_ref,
     segc_ref,
     segr_ref,
-    dq_ref,
-    dk_ref,
-    dv_ref,
-    kt_ref,
-    dk_sum,
-    dv_sum,
+    *refs,
 ):
+    kt_ref, dk_sum, dv_sum, side_ref, stage_ref, rows_ref = refs[-6:]
+    pair = pl.program_id(0)
     step = pl.program_id(1)
     steps = pl.num_programs(1)
+    own_width = side_ref.shape[1] // 3
     length = k_ref.shape[0]
     keys = k_ref[...]
     kt_ref[...] = keys.T
@@ -359,7 +389,9 @@
             dv_all = dv_part if dv_all is None else dv_all + dv_part
             dk_all = dk_part if dk_all is None else dk_all + dk_part
             dq_rows.append(dot(kt_ref[head * HEAD_DIM : (head + 1) * HEAD_DIM], d_scores))
-        dq_ref[part] = (jnp.concatenate(dq_rows, axis=0).T * SCALE).astype(BF16)
+        target = pl.ds(pl.multiple_of(step * q_ref.shape[0] + start, sub), sub)
+        columns = pl.ds(pl.multiple_of(pair * PAIR, PAIR), PAIR)
+        side_ref[target, columns] = (jnp.concatenate(dq_rows, axis=0).T * SCALE).astype(BF16)
     dk_all = dk_all * SCALE
 
     @pl.when(step == 0)
@@ -374,43 +406,104 @@
 
     @pl.when(step == steps - 1)
     def _():
-        dk_ref[...] = dk_sum[...].astype(BF16)
-        dv_ref[...] = dv_sum[...].astype(BF16)
+        for place_of, sum_ref in ((1, dk_sum), (2, dv_sum)):
+            columns = pl.ds(pl.multiple_of(place_of * own_width + pair * PAIR, PAIR), PAIR)
+            side_ref[:, columns] = sum_ref[...].astype(BF16)
+
+    @pl.when((step == steps - 1) & (pair == pl.num_programs(0) - 1))
+    def _():
+        grads(place, side_ref, stage_ref, rows_ref, *refs[:-6])
 
 
 def attend_back(
-    place, first, query, keys, values, d_mixed, mixed, logs, seg_cols, seg_row, limit, after=()
+    place,
+    first,
+    count,
+    query,
+    keys,
+    values,
+    d_mixed,
+    mixed,
+    logs,
+    seg_cols,
+    seg_row,
+    limit,
+    hidden_t,
+    group,
+    chips,
+    slice_rows,
+    branch=None,
+    mixed_parts=(),
+    earlier=(),
+    split=True,
+    after=(),
 ):
-    length, width = mixed.shape
-    block = min(1024, length)
+    length = mixed.shape[0]
+    own = count * PAIR
+    block = length if length <= 1024 else 256
     tile = pl.BlockSpec((block, PAIR), lambda p, j, s: (j, first + p))
     whole = pl.BlockSpec((length, PAIR), lambda p, j, s: (0, first + p))
-    out_tile = pl.BlockSpec((block, PAIR), lambda p, j, s: (j, p))
-    out_whole = pl.BlockSpec((length, PAIR), lambda p, j, s: (0, p))
+    width = hidden_t.shape[0]
+    some = width // chips
+    calls = len(mixed_parts)
+    columns = 3 * own + (width // group if calls else 0)
+    cut = columns // 2 if split else columns
+    sides = (length // group, 3 * own + (earlier[0].shape[1] if earlier else 0))
+    args = [hidden_t]
+    specs = [pl.BlockSpec((width, length), lambda p, j, s: (0, 0), pipeline_mode=pl.Buffered(1))]
+    if calls:
+        arrays = [mixed_parts[j][s] for j in range(calls) for s in range(group)]
+        args += [branch, *arrays]
+        specs.append(
+            pl.BlockSpec((length, width // group), lambda p, j, s: (0, s[0]), pipeline_mode=pl.Buffered(1))
+        )
+        specs += [
+            pl.BlockSpec(array.shape, lambda p, j, s: (0, 0), pipeline_mode=pl.Buffered(1)) for array in arrays
+        ]
+    args += earlier
+    specs += [
+        pl.BlockSpec(array.shape, lambda p, j, s: (0, 0), pipeline_mode=pl.Buffered(1)) for array in earlier
+    ]
+
+    def pieces(columns):
+        shape = (chips // 2, some, columns)
+        spec = pl.BlockSpec(shape, lambda p, j, s: (0, 0, 0))
+        return [(shape, BF16, spec, KEEP), (shape, BF16, spec, PIN)]
+
     return call(
-        functools.partial(attend_back_kernel, limit, min(256, block)),
+        functools.partial(
+            attend_back_kernel,
+            limit,
+            min(256, block),
+            functools.partial(attention_grads, group, calls, chips, cut, bool(earlier)),
+        ),
         "attend_back",
         place,
-        (query, keys, values, d_mixed, mixed, logs, seg_cols, seg_row),
-        (width // PAIR, length // block),
+        (query, keys, values, d_mixed, mixed, logs, seg_cols, seg_row, *args),
+        (own // PAIR, length // block),
         [
             tile,
             whole,
             whole,
             tile,
-            out_tile,
-            out_tile,
+            tile,
+            tile,
             pl.BlockSpec((length, PAIR), lambda p, j, s: (0, 0)),
             pl.BlockSpec((1, block), lambda p, j, s: (0, j)),
+        ]
+        + specs,
+        [(sides, BF16, pl.BlockSpec(sides, lambda p, j, s: (0, 0)))] * group
+        + pieces(cut)
+        + (pieces(columns - cut) if split else []),
+        [
+            pltpu.VMEM((PAIR, length), BF16),
+            pltpu.VMEM((length, PAIR), F32),
+            pltpu.VMEM((length, PAIR), F32),
+            pltpu.VMEM((length, 3 * own), BF16),
+            pltpu.VMEM((chips, some, columns), BF16),
+            pltpu.VMEM((length // slice_rows, slice_rows, 3 * own), BF16),
         ],
-        [
-            ((length, width), BF16, out_tile),
-            ((length, width), BF16, out_whole),
-            ((length, width), BF16, out_whole),
-        ],
-        [pltpu.VMEM((PAIR, length), BF16), pltpu.VMEM((length, PAIR), F32), pltpu.VMEM((length, PAIR), F32)],
         after=after,
-        vmem=LESS_VMEM if length <= 1024 else VMEM,
     )
 
 
@@ -441,11 +534,10 @@
         (1,),
         [whole] * len(parts),
         [
-            ((length, width), BF16, pl.BlockSpec((length, width), lambda i, s: (0, 0))),
+            ((length, width), BF16, pl.BlockSpec((length, width), lambda i, s: (0, 0)), length <= 1024),
             ((8, width), F32, pl.BlockSpec((8, width), lambda i, s: (0, 0))),
         ],
         after=after,
-        vmem=LESS_VMEM if length <= 1024 else VMEM,
     )
 
 
@@ -525,7 +617,7 @@
     half = 0.5 + 0.5 * lax.erf(upper * 0.7071067811865476)
     bell = jnp.exp2(upper * upper * (-0.5 * LOG2E)) * 0.3989422804014327
     active = (upper * half).astype(BF16)
-    hand_out(rows_ref, place[0], active, active_refs)
+    hand_out(rows_ref, group, place[0], active, active_refs)
     slope_ref[...] = (half + upper * bell).astype(BF16)
     stage_ref[...] = dot(active, cot_ref[...], TN).astype(BF16).reshape(stage_ref.shape)
     deal(
@@ -549,7 +641,7 @@
         spec = pl.BlockSpec(
             (parts // 2, chunk, columns), lambda t, s: (jnp.bitwise_xor(t, s[1] // parts), 0, 0)
         )
-        return ((chips // 2, chunk, columns), BF16, spec)
+        return ((chips // 2, chunk, columns), BF16, spec, PIN)
 
     return call(
         functools.partial(feed_up_kernel, number, group, cut),
@@ -571,7 +663,6 @@
         + [piece(width - cut)] * 2,
         [pltpu.VMEM((parts, chunk, width), BF16), pltpu.VMEM((length // rows, rows, tile), BF16)],
         after=after,
-        vmem=LESS_VMEM if length <= 1024 else VMEM,
     )
 
 
@@ -636,11 +727,11 @@
     split = max(1, min(tiles - 1, round(tiles * share)))
     some = width // chips
 
-    def piece(first, last):
+    def piece(first, last, pin):
         spec = pl.BlockSpec(
             (chips // 2, some, tile), lambda t, s: (0, 0, jnp.clip(t, first, last - 1) - first)
         )
-        return ((chips // 2, some, (last - first) * tile), BF16, spec)
+        return ((chips // 2, some, (last - first) * tile), BF16, spec, pin)
 
     return call(
         functools.partial(feed_back_kernel, number, chips, split),
@@ -660,21 +751,21 @@
         ]
         * DH_PIECES
         + [((1, ff), F32, pl.BlockSpec((1, tile), lambda t, s: (0, t)))]
-        + [piece(0, split)] * 2
-        + [piece(split, tiles)] * 2,
+        + [piece(0, split, KEEP), piece(0, split, PIN)]
+        + [piece(split, tiles, KEEP), piece(split, tiles, PIN)],
         [pltpu.VMEM((length, width), F32), pltpu.VMEM((chips, some, tile), BF16)],
         after=after,
-        vmem=LESS_VMEM if length <= 1024 else VMEM,
-    )
-
-
-def feed_down_kernel(group, place, down_ref, middle_ref, vec_ref, *refs):
+    )
+
+
+def feed_down_kernel(group, place, middle_ref, vec_ref, *refs):
+    down_refs = refs[group : 2 * group]
     active_refs = refs[:group]
-    near_ref, far_ref, sum_ref = refs[group:]
+    near_ref, far_ref, sum_ref = refs[2 * group :]
     step = pl.program_id(0)
     total = None
-    for steps, active_ref in enumerate(active_refs):
-        down = down_ref[:, pl.ds((place[0] + group - steps) % group, 1)]
+    for active_ref, down_ref in zip(active_refs, down_refs):
+        down = down_ref[...]
         part = dot(active_ref[...], down.reshape(-1, down.shape[3]))
         total = part if total is None else total + part
 
@@ -705,14 +796,20 @@
         functools.partial(feed_down_kernel, group),
         "feed_down",
         place,
-        (down_weight.reshape(chips, group, chunk, width), middle, vectors) + tuple(active_parts),
+        (middle, vectors) + tuple(active_parts) + (down_weight.reshape(chips, group, chunk, width),) * group,
         (ff // tile,),
         [
-            pl.BlockSpec((tile // chunk, group, chunk, width), lambda i, s: (i, 0, 0, 0)),
             pl.BlockSpec((rows, width), lambda i, s: (0, 0)),
             pl.BlockSpec((8, width), lambda i, s: (0, 0)),
         ]
-        + [pl.BlockSpec((rows, tile), lambda i, s: (0, i))] * group,
+        + [pl.BlockSpec((rows, tile), lambda i, s: (0, i))] * group
+        + [
+            pl.BlockSpec(
+                (tile // chunk, 1, chunk, width),
+                functools.partial(lambda t, i, s: (i, (s[0] + group - t) % group, 0, 0), steps),
+            )
+            for steps in range(group)
+        ],
         [out, out],
         [pltpu.VMEM((rows, width), F32)],
         after=after,
@@ -793,176 +890,204 @@
         ]
         + specs,
         [
-            ((length, width), BF16, row),
+            ((length, width), BF16, row, length <= 1024),
             (
                 (length // group, width),
                 F32,
                 pl.BlockSpec((rows, width), lambda i, s: (i // (turn * group) * turn + i % turn, 0)),
             ),
-            ((length, own), BF16, pl.BlockSpec((rows, own), lambda i, s: (i, 0))),
+            ((length, own), BF16, pl.BlockSpec((rows, own), lambda i, s: (i, 0)), length <= 1024),
             ((8, width), F32, pl.BlockSpec((8, width), lambda i, s: (0, 0))),
         ],
         [pltpu.VMEM((rows, width), F32)],
         after=after,
-        vmem=LESS_VMEM if length <= 1024 else VMEM,
-    )
-
-
-def attention_grad_kernel(group, calls, chips, cut, place, *refs):
-    ht_ref, dq_ref, dk_ref, dv_ref = refs[:4]
-    mixed_refs = refs[5 : 5 + group * calls]
-    side_refs = refs[-6 - group : -6]
-    ka_ref, sa_ref, kb_ref, sb_ref, stage_ref, rows_ref = refs[-6:]
+    )
+
+
+def attention_grads(group, calls, chips, cut, earlier, place, side_ref, stage_ref, rows_ref, ht_ref, *refs):
+    number = group * calls
+    mixed_refs = refs[1 : 1 + number]
+    outs = refs[1 + number :] if calls else refs
+    if earlier:
+        before_refs, outs = outs[:group], outs[group:]
+        for before_ref, out_ref in zip(before_refs, outs):
+            out_ref[:, : before_ref.shape[1]] = before_ref[...]
+    side_refs = outs[:group]
+    piece_refs = outs[group:]
     offset = 0
     if calls:
-        branch = refs[4][...]
+        branch = refs[0][...]
         offset = branch.shape[1]
-        share = chips // (group * calls)
+        share = chips // number
         for index, mixed_ref in enumerate(mixed_refs):
             owner = ((place[0] + group - index % group) % group) * calls + index // group
             grad = dot(mixed_ref[...], branch, TN).astype(BF16)
             rows = grad.shape[0] // share
             stage_ref[pl.ds(owner * share, share), :, :offset] = grad.reshape(share, rows, offset)
-    side = jnp.concatenate([dq_ref[...], dk_ref[...], dv_ref[...]], axis=1)
-    hand_out(rows_ref, place[0], side, side_refs)
+    side = side_ref[...]
+    hand_out(rows_ref, group, place[0], side, side_refs)
     rows = ht_ref.shape[0] // chips
     many = max(1, 256 // rows)
     for start in range(0, chips, many):
         grad = dot(ht_ref[start * rows : (start + many) * rows], side).astype(BF16)
         stage_ref[start : start + many, :, offset:] = grad.reshape(many, rows, grad.shape[1])
+    columns = stage_ref.shape[2]
     for relative in range(chips):
         values = stage_ref[jnp.bitwise_xor(jnp.int32(relative), place[1])]
-        (sa_ref if relative & 2 else ka_ref)[without_bit(relative, 1)] = values[:, :cut]
-        (sb_ref if relative & 1 else kb_ref)[without_bit(relative, 0)] = values[:, cut:]
-
-
-def attention_grad(place, hidden_t, triple, group, chips, slice_rows, branch=None, mixed_parts=(), after=()):
-    width, length = hidden_t.shape
-    own = triple[0].shape[1]
-    some = width // chips
-    calls = len(mixed_parts)
-    columns = 3 * own + (width // group if calls else 0)
-    cut = columns // 2
-    args = [hidden_t, *triple]
-    specs = [pl.BlockSpec((width, length), lambda i, s: (0, 0))]
-    specs += [pl.BlockSpec((length, own), lambda i, s: (0, 0))] * 3
-    if calls:
-        arrays = [mixed_parts[j][s] for j in range(calls) for s in range(group)]
-        args += [branch, *arrays]
-        specs.append(pl.BlockSpec((length, width // group), lambda i, s: (0, s[0])))
-        specs += [pl.BlockSpec(array.shape, lambda i, s: (0, 0)) for array in arrays]
-    sides = (length // group, 3 * own)
-
-    def piece(rows, columns):
-        shape = (chips // 2, rows, columns)
-        return (shape, BF16, pl.BlockSpec(shape, lambda i, s: (0, 0, 0)))
-
-    return call(
-        functools.partial(attention_grad_kernel, group, calls, chips, cut),
-        "attention_grad",
-        place,
-        tuple(args),
-        (1,),
-        specs,
-        [(sides, BF16, pl.BlockSpec(sides, lambda i, s: (0, 0)))] * group
-        + [piece(some, cut)] * 2
-        + [piece(some, columns - cut)] * 2,
-        [
-            pltpu.VMEM((chips, some, columns), BF16),
-            pltpu.VMEM((length // slice_rows, slice_rows, 3 * own), BF16),
-        ],
-        after=after,
-        vmem=LESS_VMEM if length <= 1024 else VMEM,
-    )
-
-
-def hidden_back_kernel(group, calls, place, x_ref, base_ref, vec_ref, *refs):
-    number = group * calls
+        if len(piece_refs) > 2:
+            piece_refs[bool(relative & 2)][without_bit(relative, 1)] = values[:, :cut]
+        piece_refs[(relative & 1) - 2][without_bit(relative, 0)] = values[:, cut % columns :]
+
+
+def hidden_back_kernel(number, side_spot, share, place, x_ref, base_ref, vec_ref, *refs):
     side_refs = refs[:number]
-    weight_refs = refs[number : 4 * number]
-    near_ref, far_ref, sums_ref = refs[4 * number :]
-    total = None
-    for index, side_ref in enumerate(side_refs):
-        side = side_ref[...]
-        each = side.shape[1] // 3
-        row_sums = jnp.sum(side.astype(F32), axis=0, keepdims=True)
-        spot = ((place[0] + group - index % group) % group) * calls + index // group
-        spot = pl.ds(pl.multiple_of(spot * each, each), each)
-        sums_ref[2:3, spot] = row_sums[:, :each]
-        sums_ref[3:4, spot] = row_sums[:, 2 * each :]
-        for third in range(3):
-            part = dot(side[:, third * each : (third + 1) * each], weight_refs[3 * index + third][...], NT)
-            total = part if total is None else total + part
-    normal, inverse = norm_parts(x_ref[...].reshape(total.shape).astype(F32))
-    sums_ref[0:1] = jnp.sum(total * normal, axis=0, keepdims=True)
-    sums_ref[1:2] = jnp.sum(total, axis=0, keepdims=True)
-    sums_ref[4:8] = jnp.zeros((4, total.shape[1]), F32)
-    result = (base_ref[...] + norm_back(total, normal, inverse, vec_ref[0:1])).astype(BF16)
+    weight_refs = refs[number : number + 3]
+    small_refs = refs[number + 3 : number + 5]
+    near_ref, far_ref, sums_ref, sum_ref = refs[number + 5 :]
+    step = pl.program_id(0)
+    each = side_refs[0].shape[1] // 3
     half = near_ref.shape[0]
-    near_ref[...] = result[:half]
-    far_ref[...] = result[half:]
-
-
-def hidden_back(place, x_rows, d_middle, vectors, side_parts, qkv_weight, slice_rows, after=()):
-    calls = len(side_parts)
-    group = len(side_parts[0])
-    rows, columns = side_parts[0][0].shape
+
+    @pl.when(step == 0)
+    def _():
+        sum_ref[...] = jnp.zeros_like(sum_ref)
+        sums_ref[...] = jnp.zeros_like(sums_ref)
+
+    def add(index):
+        @pl.when(step == index)
+        def _():
+            side = side_refs[index][...]
+            row_sums = jnp.sum(side.astype(F32), axis=0, keepdims=True)
+            spot = pl.ds(pl.multiple_of(side_spot(index, place) * each, each), each)
+            sums_ref[2:3, spot] = row_sums[:, :each]
+            sums_ref[3:4, spot] = row_sums[:, 2 * each :]
+            total = None
+            for third, weight_ref in enumerate(weight_refs):
+                part = dot(side[:, third * each : (third + 1) * each], weight_ref[...], NT)
+                total = part if total is None else total + part
+            sum_ref[...] += total
+
+    for index in range(number):
+        add(index)
+
+    @pl.when(step == number - 1)
+    def _():
+        sums = []
+        for start, out_ref, block in ((0, near_ref, 0), (half, far_ref, x_ref.shape[0] // 2)):
+            total = sum_ref[start : start + half]
+            rows = x_ref[block : block + x_ref.shape[0] // 2].reshape(total.shape)
+            normal, inverse = norm_parts(rows.astype(F32))
+            sums.append(jnp.sum(total * normal, axis=0, keepdims=True))
+            sums.append(jnp.sum(total, axis=0, keepdims=True))
+            result = base_ref[start : start + half] + norm_back(total, normal, inverse, vec_ref[0:1])
+            out_ref[...] = result.astype(BF16)
+        sums_ref[0:1] = sums[0] + sums[2]
+        sums_ref[1:2] = sums[1] + sums[3]
+        sums_ref[4:5] = small_refs[0][2:3] * share
+        sums_ref[5:7] = small_refs[0][0:2] * share
+        sums_ref[7:8] = small_refs[1][0:1] * share
+
+
+def hidden_back(
+    place, x_rows, d_middle, vectors, sides, calls, qkv_weight, sums, cot_sums, slice_rows, after=()
+):
+    group = len(sides)
+    rows, columns = sides[0].shape
+    columns = columns // calls
     each = columns // 3
     length, width = x_rows.shape
     slices = length // group // slice_rows
     whole = pl.BlockSpec((rows, width), lambda i, s: (0, 0))
-    arrays = []
-    weights = []
-    for j in range(calls):
-        for steps in range(group):
-            arrays.append(side_parts[j][steps])
-            for third in range(3):
-                weights.append(
-                    pl.BlockSpec(
-                        (width, each),
-                        functools.partial(
-                            lambda j, t, third, i, s: (
-                                0,
-                                third * group * calls + ((s[0] + group - t) % group) * calls + j,
-                            ),
-                            j,
-                            steps,
-                            third,
-                        ),
-                    )
-                )
+    count = calls * group
+    eight = pl.BlockSpec((8, width), lambda i, s: (0, 0))
+
+    def side_spot(index, numbers):
+        return ((numbers[0] + group - index % group) % group) * calls + index // group
+
+    weights = [
+        pl.BlockSpec(
+            (width, each),
+            functools.partial(lambda third, i, s: (0, third * group * calls + side_spot(i, s)), third),
+        )
+        for third in range(3)
+    ]
     out = ((rows // 2, width), BF16, pl.BlockSpec((rows // 2, width), lambda i, s: (0, 0)))
     return call(
-        functools.partial(hidden_back_kernel, group, calls),
+        functools.partial(hidden_back_kernel, count, side_spot, 1.0 / group),
         "hidden_back",
         place,
         (x_rows.reshape(slices, group, slice_rows, width), d_middle, vectors)
-        + tuple(arrays)
-        + (qkv_weight,) * len(weights),
-        (1,),
+        + tuple(sides) * calls
+        + (qkv_weight,) * 3
+        + (sums, cot_sums),
+        (count,),
         [
             pl.BlockSpec((slices, 1, slice_rows, width), lambda i, s: (0, s[0], 0, 0)),
             whole,
             pl.BlockSpec((8, width), lambda i, s: (0, 0)),
         ]
-        + [pl.BlockSpec((rows, columns), lambda i, s: (0, 0))] * len(arrays)
-        + weights,
+        + [
+            pl.BlockSpec((rows, columns), functools.partial(lambda j, i, s: (0, j), index // group))
+            for index in range(count)
+        ]
+        + weights
+        + [eight, eight],
         [out, out, ((8, width), F32, pl.BlockSpec((8, width), lambda i, s: (0, 0)))],
+        [pltpu.VMEM((rows, width), F32)],
         after=after,
-        vmem=LESS_VMEM if length <= 1024 else VMEM,
-    )
-
-
-def part_kernel(takes, whole, place, *refs):
-    arrays = (len(refs) - 2 - bool(whole)) // 2
-    own_ref, send_ref = refs[2 * arrays : 2 * arrays + 2]
+    )
+
+
+def join_kernel(place, near_ref, far_ref, out_ref):
+    half = place[1] % 2
+    out_ref[half, 0] = near_ref[...]
+    out_ref[1 - half, 0] = far_ref[...]
+
+
+def join(place, near, far, after=()):
+    shape = (2, 1) + near.shape
+    whole = pl.BlockSpec(near.shape, lambda i, s: (0, 0))
+    return call(
+        join_kernel,
+        "join",
+        place,
+        (near, far),
+        (1,),
+        [whole, whole],
+        [(shape, BF16, pl.BlockSpec(shape, lambda i, s: (0, 0, 0, 0)))],
+        after=after,
+    )[0]
+
+
+def later(place, array, after):
+    return call(
+        lambda place_ref, out_ref: None,
+        "later",
+        place,
+        (),
+        (1,),
+        [],
+        [(array.shape, array.dtype, pl.BlockSpec(memory_space=pl.ANY))],
+        after=after,
+        fill=[array],
+    )[0]
+
+
+def part_kernel(counts, takes, whole, place, *refs):
+    sources = []
+    for count in counts:
+        sources.append(refs[:count])
+        refs = refs[count:]
+    own_ref, send_ref = refs[:2]
     rows = own_ref.shape[0]
     mine = place[0] == 0
     start = 0
 
     def total(index, first, count):
         part = pl.ds(first, count)
-        return refs[2 * index][0, part].astype(F32) + refs[2 * index + 1][0, part].astype(F32)
+        if len(sources[index]) == 1:
+            return sources[index][0][part]
+        return sources[index][0][0, part].astype(F32) + sources[index][1][0, part].astype(F32)
 
     for index, first in takes:
         both = total(index, first, 2 * rows)
@@ -970,30 +1095,34 @@
         own_ref[:, start : start + columns] = jnp.where(mine, both[:rows], both[rows:])
         send_ref[:, start : start + columns] = jnp.where(mine, both[rows:], both[:rows]).astype(BF16)
         start += columns
-    if whole:
-        out_ref = refs[-1]
-        start = 0
-        for index, first in whole:
-            value = total(index, first, out_ref.shape[0])
-            out_ref[:, start : start + value.shape[1]] = value
-            start += value.shape[1]
-
-
-def part_rows(place, arrays, takes, rows, whole=(), whole_rows=0, after=()):
-    columns = sum(arrays[2 * index].shape[2] for index, _ in takes)
+    out_ref = refs[2]
+    start = 0
+    for index, first in whole:
+        value = total(index, first, out_ref.shape[0])
+        out_ref[:, start : start + value.shape[1]] = value
+        start += value.shape[1]
+
+
+def part_rows(place, sources, takes, rows, whole, whole_rows, after=()):
+    columns = sum(sources[index][0].shape[-1] for index, _ in takes)
     out = pl.BlockSpec((rows, columns), lambda i, s: (0, 0))
-    outs = [((rows, columns), F32, out), ((rows, columns), BF16, out)]
-    if whole:
-        shape = (whole_rows, sum(arrays[2 * index].shape[2] for index, _ in whole))
-        outs.append((shape, F32, pl.BlockSpec(shape, lambda i, s: (0, 0))))
+    shape = (whole_rows, sum(sources[index][0].shape[-1] for index, _ in whole))
+    arrays = [array for parts in sources for array in parts]
     return call(
-        functools.partial(part_kernel, takes, whole),
+        functools.partial(part_kernel, [len(parts) for parts in sources], takes, whole),
         "part_rows",
         place,
         tuple(arrays),
         (1,),
-        [pl.BlockSpec(array.shape, lambda i, s: (0, 0, 0)) for array in arrays],
-        outs,
+        [
+            pl.BlockSpec(array.shape, functools.partial(lambda n, i, s: (0,) * n, array.ndim))
+            for array in arrays
+        ],
+        [
+            ((rows, columns), F32, out),
+            ((rows, columns), BF16, out),
+            (shape, F32, pl.BlockSpec(shape, lambda i, s: (0, 0))),
+        ],
         after=after,
     )
 
@@ -1054,17 +1183,21 @@
     own_width = width // group
     own_ff = ff // group
     chunk = own_ff // chips
-    place = Place(jnp.stack([member, dp_index * 2 + half]).astype(jnp.int32))
+    place = Place(jnp.stack([member, dp_index * 2 + half]).astype(jnp.int32), length > 1024)
+
+    def moved(value):
+        place.free.append(value)
+        return value
 
     def across(value):
         pairs = [(i, (i + group) % ctx_size) for i in range(ctx_size)]
-        return lax.ppermute(value, "ctx", pairs)
+        return moved(lax.ppermute(value, "ctx", pairs))
 
     def around(value, steps):
         pairs = [
             (h * group + g, h * group + (g + steps) % group) for h in range(2) for g in range(group)
         ]
-        return lax.ppermute(value, "ctx", pairs)
+        return moved(lax.ppermute(value, "ctx", pairs))
 
     def all_around(value):
         return [value] + [around(value, steps) for steps in range(1, group)]
@@ -1092,18 +1225,29 @@
     def swap_bit(value, bit):
         if bit < 0:
             return across(value)
-        return lax.ppermute(value, "dp", [(i, i ^ (1 << bit)) for i in range(dp_size)])
+        return moved(lax.ppermute(value, "dp", [(i, i ^ (1 << bit)) for i in range(dp_size)]))
 
     all_bits = list(range(dp_bits - 1, -1, -1)) + [-1]
     rest_bits = list(range(1, dp_bits))
 
     class Halving:
-        def __init__(self, keep, send, bits, order):
+        def __init__(self, keep, send, bits, order, then=()):
             self.order = list(order)
+            self.then = then
             self.left = list(bits)
             self.keep = keep
             self.came = swap_bit(send, self.order[0])
+            if not place.long:
+                place.pinned.append(self.came)
             self.order.pop(0)
+
+    def crossed(pieces):
+        first = [bit for bit in all_bits if bit != 0]
+        second = [bit for bit in all_bits if bit != -1]
+        return [
+            Halving(*pieces[:2], first, [0] + rest_bits, (-1, 0)),
+            Halving(*pieces[2:], second, [-1] + rest_bits, (-1, 0)),
+        ]
 
     def pair(pieces):
         first = [bit for bit in all_bits if bit != 0]
@@ -1113,20 +1257,51 @@
             Halving(*pieces[2:], second, [-1, 0] + rest_bits),
         ]
 
-    def step(after, *jobs):
+    def lone(pieces):
+        return Halving(*pieces, [bit for bit in all_bits if bit != -1], [-1, 0] + rest_bits)
+
+    state = {}
+
+    def go(after, *names):
+        jobs = []
+        counts = []
+        for name in names:
+            item = state[name]
+            if isinstance(item, list) and item[0].order[:1] != item[1].order[:1]:
+                jobs += [[item[0]], [item[1]]]
+                counts.append(2)
+            else:
+                jobs.append(item if isinstance(item, list) else [item])
+                counts.append(1)
+        ready, results = step(after, *jobs, cost=COST)
+        for name, count in zip(names, counts):
+            state[name] = [results.pop(0), results.pop(0)] if count == 2 else results.pop(0)
+        return ready
+
+    def step(after, *jobs, cost=0):
         asked = []
         for halvings in jobs:
             first = halvings[0]
-            bit = first.order[0]
             arrays = [array for halving in halvings for array in (halving.keep, halving.came)]
-            asked.append((arrays, len(first.left) - 1 - first.left.index(bit)))
-        sums = step_call(place, asked, after)
+            if first.order:
+                asked.append((arrays, len(first.left) - 1 - first.left.index(first.order[0]), 1))
+            elif first.then:
+                asked.append((arrays, 0, 2))
+            else:
+                asked.append((arrays, None, 1))
+        sums = list(step_call(place, asked, after, cost))
+        ready = sums[:1]
         results = []
-        for index, halvings in enumerate(jobs):
+        for halvings in jobs:
             first = halvings[0]
-            left = [bit for bit in first.left if bit != first.order[0]]
-            results.append(Halving(sums[2 * index], sums[2 * index + 1], left, first.order))
-        return list(sums[:1]), results
+            if first.order:
+                left = [bit for bit in first.left if bit != first.order[0]]
+                results.append(Halving(sums.pop(0), sums.pop(0), left, first.order, first.then))
+            elif first.then:
+                results.append([Halving(sums.pop(0), sums.pop(0), [], [bit]) for bit in first.then])
+            else:
+                results.append(sums.pop(0))
+        return ready, results
 
     slices = 2 if group > 2 else 1
     slice_rows = rows // slices
@@ -1140,9 +1315,11 @@
     vectors = vectors.astype(F32)
     filled = ()
     for side, both_of in enumerate((own_inputs, far_inputs)):
+        if filled:
+            both_of = later(place, both_of, filled[3:4])
         for c, part in enumerate(sliced(both_of)):
             start = (side * slices + c) * (length // (2 * slices))
-            copied = cotangent if not filled else None
+            copied = cotangent if side == 1 and c == 0 else None
             filled = project(
                 place, all_around(part), start, length, vectors, qkv_weight, qv_bias, filled, copied
             )
@@ -1178,19 +1355,9 @@
     pairs = own_width // PAIR
     calls = min(2, pairs)
     each = pairs // calls
-    mixed = []
-    logs = []
-    mixed_parts = []
-    ready = []
-    for j in range(calls):
-        mixed_j, logs_j = attend(
-            place, j * each, each, query, keys, values, seg_cols, seg_row, limit, after=ready
-        )
-        mixed.append(mixed_j)
-        logs.append(logs_j)
-        mixed_parts.append(all_around(mixed_j))
-        ready = [mixed_j]
-    cot_rows, cot_sums = collect(place, cot_parts, group, after=ready)
+    mixed, logs = attend(place, 0, pairs, query, keys, values, seg_cols, seg_row, limit)
+    mixed_parts = [all_around(mixed)]
+    cot_rows, cot_sums = collect(place, cot_parts, group, after=[mixed])
     middle, middle_own, hidden2, hidden2_t = close(
         place, x_rows, mixed_parts, group, out_weight, vectors, slice_rows, after=[cot_rows]
     )
@@ -1209,7 +1376,7 @@
     active_parts = up_out[:group]
     slope, *down_pieces = up_out[group:]
     active_parts = [active_parts[0]] + [around(active_parts[steps], steps) for steps in range(1, group)]
-    down = pair(down_pieces)
+    state["down"] = crossed(down_pieces)
     back = feed_back(
         place,
         hidden2_t,
@@ -1226,56 +1393,63 @@
     dh_pieces = back[:DH_PIECES]
     upb_grad, *up_pieces = back[DH_PIECES:]
     dh_parts = [all_around(piece) for piece in dh_pieces]
-    up = pair(up_pieces)
-
-    ready, down = step(dh_pieces[:1], [down[0]], [down[1]])
+    state["up"] = pair(up_pieces)
+
+    ready = go(dh_pieces[:1], "down")
     branch, d_middle, d_mixed, sums = middle_back(
         place, middle, cot_rows, vectors, out_weight, dh_parts, slice_rows, after=ready
     )
 
-    def back_of(j, after):
-        return attend_back(
-            place, j * each, query, keys, values, d_mixed, mixed[j], logs[j], seg_cols, seg_row, limit, after=after
-        )
-
-    def grad_of(j, triple, after):
-        results = attention_grad(
+    out_near, out_far = feed_down(place, active_parts, down_weight, middle_own, vectors, chips, after=[branch])
+    out_far = across(out_far)
+
+    def back_of(j, earlier, after):
+        results = attend_back(
             place,
+            j * each,
+            each,
+            query,
+            keys,
+            values,
+            d_mixed,
+            mixed,
+            logs,
+            seg_cols,
+            seg_row,
+            limit,
             hidden1_t,
-            triple,
             group,
             chips,
             slice_rows,
             branch if j == 0 else None,
             mixed_parts if j == 0 else (),
+            earlier,
             after=after,
         )
-        sides = results[:group]
-        sides = [sides[0]] + [around(sides[steps], steps) for steps in range(1, group)]
-        return pair(results[group:]), sides, list(results[:1])
-
-    triple = back_of(0, [branch])
-    early, sides, ready = grad_of(0, triple, triple[:1])
-    sides_of = [sides]
-    ready, (down,) = step(ready, down)
+        pieces = results[group:]
+        halvings = pair(pieces) if len(pieces) > 2 else [lone(pieces)]
+        halvings = halvings if len(halvings) > 1 else halvings[0]
+        return halvings, list(results[:group]), list(results[:1])
+
+    state["early"], sides, ready = back_of(0, [], [out_near])
+    block_output = join(place, out_near, out_far, after=ready)
+    ready = [block_output]
+    ready = go(ready, "down", "up")
     if calls > 1:
-        ready, up = step(ready, [up[0]], [up[1]])
-        triple = back_of(1, ready)
-        late, sides, ready = grad_of(1, triple, triple[:1])
-        sides_of.append(sides)
-        ready, (up, down, *early) = step(ready, up, [down], [early[0]], [early[1]])
+        state["late"], sides, ready = back_of(1, sides, ready)
     else:
-        ready, (*up, down) = step(ready, [up[0]], [up[1]], [down])
-        ready, (up, *early) = step(ready, up, [early[0]], [early[1]])
+        state["late"] = state.pop("early")
+    others = [name for name in ("early",) if name in state]
+    sides = [sides[0]] + [around(sides[steps], steps) for steps in range(1, group)]
+    ready = go(ready, "up", "down", *others)
     input_near, input_far, own_sums = hidden_back(
-        place, x_rows, d_middle, vectors, sides_of, qkv_weight, slice_rows, after=ready
-    )
+        place, x_rows, d_middle, vectors, sides, calls, qkv_weight, sums, cot_sums, slice_rows, after=ready
+    )
+    ready = go([input_near], "late", "up", *others)
 
     own = width // (chips * group)
-    both = 1.0 / group
     member_is = (jnp.arange(group, dtype=jnp.int32) == member).astype(F32)
-    sums_of = jnp.concatenate([own_sums[:4], sums[2:3] * both, sums[:2] * both, cot_sums[:1] * both])
-    small = jnp.transpose(sums_of.reshape(8, chips * group, own), (1, 0, 2)).reshape(chips * group, 8 * own)
+    small = jnp.transpose(own_sums.reshape(8, chips * group, own), (1, 0, 2)).reshape(chips * group, 8 * own)
     upb_full = (upb_grad.reshape(chips, 1, chunk) * member_is[None, :, None]).reshape(chips * group, chunk)
     small = jnp.concatenate([small, upb_full], axis=1)
     small = lax.all_to_all(small, ("dp", "ctx"), 0, 0, tiled=True)
@@ -1283,31 +1457,16 @@
     small_rows = small[: 8 * own].reshape(8, own)
     upb_out = small[8 * own :]
 
-    ready = [input_near]
-    if calls > 1:
-        ready, (*late, up, early) = step(ready, [late[0]], [late[1]], [up], early)
-    else:
-        ready, (early,) = step(ready, early)
-    out_near, out_far = feed_down(place, active_parts, down_weight, middle_own, vectors, chips, after=ready)
-    ready = [out_near]
-    if calls > 1:
-        ready, (late, early) = step(ready, late, [early])
-        tails = [down, up, early, late]
-    else:
-        tails = [down, up, early]
-    while any(tail.order for tail in tails):
-        active = [tail for tail in tails if tail.order]
-        ready, stepped = step(ready, *[[tail] for tail in active])
-        for tail, new in zip(active, stepped):
-            tails[tails.index(tail)] = new
-
-    def hand_back(near, far):
-        came = across(far)
-        first = half == 0
-        return jnp.stack([jnp.where(first, near, came), jnp.where(first, came, near)])[:, None]
-
-    block_output = hand_back(out_near, out_far)
-    input_grad = hand_back(input_near, input_far)
+    input_far = across(input_far)
+    ready = go(ready, "late", "up", *others)
+    input_grad = join(place, input_near, input_far, after=ready)
+    ready = [input_grad]
+
+    def waits(item):
+        return isinstance(item, Halving) and (item.order or item.then)
+
+    while any(waits(item) for item in state.values()):
+        ready = go(ready, *[name for name in state if waits(state[name])])
 
     some = width // chips
 
@@ -1319,46 +1478,48 @@
         ]
         return in_order(parts, 1)
 
-    def sums_in(tail):
-        return tail.keep[0].astype(F32) + tail.came[0].astype(F32)
-
-    down, up, *rest = tails
+    def parts_of(item):
+        return [item.keep, item.came] if isinstance(item, Halving) else [item]
+
+    def sums_in(item):
+        parts = parts_of(item)
+        return parts[0] if len(parts) == 1 else parts[0][0].astype(F32) + parts[1][0].astype(F32)
+
+    rest = others + ["late"]
     if group == 2 and own % 16 == 0:
-        columns = up.keep.shape[2]
-        up_own, up_send, down_out = part_rows(
+        sources = [parts_of(item) for item in state["down"] + [state[name] for name in ["up"] + rest]]
+        own_rows, send_rows, down_out = part_rows(
             place,
-            [down.keep, down.came, up.keep, up.came],
-            [(1, k * some) for k in range(own_ff // columns)],
+            sources,
+            [(2, k * some) for k in range(own_ff // sources[2][0].shape[-1])]
+            + [
+                (index, first)
+                for index in range(3, len(sources))
+                for first in range(0, sources[index][0].shape[-2], some)
+            ],
             own,
-            [(0, k * chunk) for k in range(2)],
+            [(0, 0), (1, 0)],
             chunk,
             ready,
         )
         moves = [(k * chunk, chunk, 0, k * 2 * chunk, chunk) for k in range(chips)]
-        (up_out,) = emit(place, up_own, around(up_send, 1), moves, [ff])
-        rest_own, rest_send = part_rows(
-            place,
-            [array for tail in rest for array in (tail.keep, tail.came)],
-            [(index, first) for index in range(calls) for first in (0, some)],
-            own,
-            after=[up_out],
-        )
-        moves = [(0, own_width, 0, 0, own_width)] + [
-            (own_width + (j * 3 + t) * each * PAIR, each * PAIR, 1, t * width + j * each * PAIR, own_width)
+        moves += [(own_ff, own_width, 1, 0, own_width)]
+        moves += [
+            (own_ff + own_width + (j * 3 + t) * each * PAIR, each * PAIR, 2, t * width + j * each * PAIR, own_width)
             for j in range(calls)
             for t in range(3)
         ]
-        out_out, qkv_out = emit(place, rest_own, around(rest_send, 1), moves, [width, 3 * width])
+        up_out, out_out, qkv_out = emit(place, own_rows, around(send_rows, 1), moves, [ff, width, 3 * width])
     else:
 
-        def blocks_of(tail, rows):
-            value = sums_in(tail)
+        def blocks_of(value, rows):
             return [value[start : start + rows] for start in range(0, value.shape[0], rows)]
 
-        down_out = jnp.concatenate(blocks_of(down, chunk), axis=1)
-        up_out = exchange(jnp.concatenate(blocks_of(up, some), axis=1)).reshape(own, group, chips, chunk)
+        down_out = jnp.concatenate([sums_in(item) for item in state["down"]], axis=1)
+        up_out = jnp.concatenate(blocks_of(sums_in(state["up"]), some), axis=1)
+        up_out = exchange(up_out).reshape(own, group, chips, chunk)
         up_out = jnp.swapaxes(up_out, 1, 2).reshape(own, ff)
-        parts = [part for tail in rest for part in blocks_of(tail, some)]
+        parts = [part for name in rest for part in blocks_of(sums_in(state[name]), some)]
         rest = exchange(jnp.concatenate(parts, axis=1))
         out_out = rest[:, :, :own_width].reshape(own, width)
         qkv_out = rest[:, :, own_width:].reshape(own, group, calls, 3, each * PAIR)

time: 292 us -> 260 us (0.89)
  Pallas kernels: 196 us -> 175 us
  local copies, waits for them, and re-layouts: 19.2 us -> 6.79 us
  other arithmetic: 5.68 us -> 1.1 us
  waiting for transfers between devices: 25.3 us -> 29.5 us
    pallas_call x26 -> x23, Pallas kernels: 196 us -> 175 us  [call(): pl.pallas_call(inner, grid_spec=pltpu.PrefetchScalarGridSpec(num_scalar_p...]
    ppermute x27 -> x21, waiting for transfers between devices: 7.18 us -> 20.2 us  [the longest x12 15.5 us: across(): return moved(lax.ppermute(value, 'ctx', pairs))]
    unnamed x107 -> x31, local copies, waits for them, and re-layouts: 12.5 us -> 0.86 us
    ppermute x16, waiting for transfers between devices: 12.6 us -> 6.01 us  [swap_bit(): lax.ppermute(value, 'dp', [(i, i ^ 1 << bit) for i in range(dp_size)])]
    ppermute x16, starting transfers between devices: 17.6 us -> 22 us  [swap_bit(): lax.ppermute(value, 'dp', [(i, i ^ 1 << bit) for i in range(dp_size)])]
    ppermute x27 -> x21, starting transfers between devices: 17.3 us -> 16 us  [the longest x12 14.8 us: across(): return moved(lax.ppermute(value, 'ctx', pairs))]
  transfers between devices with their start and end apart: 44 -> 38, of which waited for: 9 -> 12; matrix products, arithmetic and copies ran while one was open for 4% -> 2% of each run, Pallas kernels for 58% -> 55%
where the time goes in v1:
time: 260 us; the launch traced here: 255 us
  Pallas kernels  175 us (67%)
  starting transfers between devices  40.5 us (16%)
  waiting for transfers between devices  29.5 us (11%)
  local copies, waits for them, and re-layouts  6.79 us (3%)
    pallas_call x23, Pallas kernels, call(): pl.pallas_call(inner, grid_spec=pltpu.PrefetchScalarGridSpec(num_scalar_p...  175 us
    ppermute x16, starting transfers between devices, swap_bit(): lax.ppermute(value, 'dp', [(i, i ^ 1 << bit) for i in range(dp_size)])  22 us
    ppermute x12, waiting for transfers between devices, across(): return moved(lax.ppermute(value, 'ctx', pairs))  15.5 us
    ppermute x12, starting transfers between devices, across(): return moved(lax.ppermute(value, 'ctx', pairs))  14.8 us
    ppermute x16, waiting for transfers between devices, swap_bit(): lax.ppermute(value, 'dp', [(i, i ^ 1 << bit) for i in range(dp_size)])  6.01 us
  transfers between devices with their start and end apart: 38, of which 12 were waited for; matrix products, arithmetic and copies ran while one was open for 2% of the time, Pallas kernels for 55%

profile of v1, /device:TPU:0, one launch (start us, length us, event | category | flops | bytes accessed | tf_op | source)
XLA Modules:
  0.0 254.6 jit_solution(9784313811563371333)
XLA Ops:
  0.8 1.3 dynamic-slice_bitcast_fusion
  2.6 2.6 %collective-permute-start.1 = (bf16[256,1024]{1,0:T(8,128)(2,1)S(1)}, bf16[256,1024]{1,0:T(8,128)(2,1)S(1)}, u32[]{:S(2)}, u32[]{:S(2)}) collective-permute-start(bf16[256,1024]{1,0:T(8,128)(2,1)S(1)} %get-tuple-element.200), channel_id=1, source_target_pairs={{0,2},{1,3},{2,0},{3,1},{4,6},{5,7},{6,4},{7,5},{8,10},{9,11},{10,... | collective-permute-start | bytes 1572872 | tf_op jit(solution)/shard_map/ppermute | solution.py:1194
  6.0 6.5 %project.2 = (bf16[1024,1024]{1,0:T(8,128)(2,1)}, bf16[1024,1024]{1,0:T(8,128)(2,1)}, bf16[1024,512]{1,0:T(8,128)(2,1)}, bf16[1024,512]{1,0:T(8,128)(2,1)}, bf16[1024,512]{1,0:T(8,128)(2,1)}) custom-call(s32[2]{0:T(128)S(1)} %pad_add_fusion.place_ref, bf16[256,1024]{1,0:T(8,128)(2,1)} %copy-done.3, bf16[256,1024]{1,0:T(8,128)(2,1)S(1)} %collective-permute-done.refs_1_, ...), custom_call_target="tpu_custom_call" | custom-call | flops 6899999744 | tf_op jit(solution)/shard_map/project/pallas_call | solution.py:52
  12.6 5.1 %collective-permute-done.1.refs_1_ = bf16[256,1024]{1,0:T(8,128)(2,1)S(1)} collective-permute-done((bf16[256,1024]{1,0:T(8,128)(2,1)S(1)}, bf16[256,1024]{1,0:T(8,128)(2,1)S(1)}, u32[]{:S(2)}, u32[]{:S(2)}) %collective-permute-start.1) | collective-permute-done | bytes 524320 | tf_op jit(solution)/shard_map/ppermute | solution.py:1194
  19.5 1.7 collective-permute-done.2.refs_1_
  21.2 6.8 %project.3 = (bf16[1024,1024]{1,0:T(8,128)(2,1)}, bf16[1024,1024]{1,0:T(8,128)(2,1)}, bf16[1024,512]{1,0:T(8,128)(2,1)}, bf16[1024,512]{1,0:T(8,128)(2,1)}, bf16...) custom-call(s32[2]{0:T(128)S(1)} %pad_add_fusion.place_ref, ...), custom_call_target="tpu_custom_call", output_to_operand_aliasing={{0}: (10, {}), {1}: (11, {}), {2}: (12, {}), {3}: (13, {}),... | custom-call | flops 6899999744 | tf_op jit(solution)/shard_map/project/pallas_call | solution.py:52
  28.0 1.8 collective-permute-start.5
  30.8 16.1 %attend.1 = (bf16[1024,512]{1,0:T(8,128)(2,1)}, f32[1024,512]{1,0:T(8,128)}) custom-call(s32[2]{0:T(128)S(1)} %pad_add_fusion.place_ref, bf16[1024,512]{1,0:T(8,128)(2,1)} %get-tuple-element.113.refs_0_, bf16[1024,512]{1,0:T(8,128)(2,1)} %get-tuple-element.114.refs_1_, bf16[1024,512]{1,0:T(8,128)(2,1)} %get-tuple-element.115.refs_2_, ...), custom_call_target="tpu_custom_call" | custom-call | flops 46000001024 | tf_op jit(solution)/shard_map/attend/pallas_call | solution.py:52
  48.1 2.2 collective-permute-done.4.refs_1_
  51.1 2.6 %collect.1 = (bf16[1024,1024]{1,0:T(8,128)(2,1)S(1)}, f32[8,1024]{1,0:T(8,128)}) custom-call(s32[2]{0:T(128)S(1)} %pad_add_fusion.place_ref, bf16[256,1024]{1,0:T(8,128)(2,1)} %get-tuple-element.117.refs_0_, bf16[256,1024]{1,0:T(8,128)(2,1)S(1)} %collective-permute-done.4.refs_1_, bf16[256,1024]{1,0:T(8,128)(2,1)S(1)} %collective-permute-done.5.refs_2_, ...), custom_call_target="tpu_custom_call" | custom-call | tf_op jit(solution)/shard_map/collect/pallas_call | solution.py:52
  53.7 7.9 %close.1 = (f32[1024,1024]{1,0:T(8,128)}, f32[512,1024]{1,0:T(8,128)}, bf16[1024,1024]{1,0:T(8,128)(2,1)S(1)}, bf16[1024,1024]{1,0:T(8,128)(2,1)S(1)}) custom-call(s32[2]{0:T(128)S(1)} %pad_add_fusion.place_ref, bf16[1024,1024]{1,0:T(8,128)(2,1)} %get-tuple-element.112.refs_0_, f32[8,1024]{1,0:T(8,128)} %convert_element_type.13.refs_2_.refs_1_, ...), custom_call_target="tpu_custom_call" | custom-call | tf_op jit(solution)/shard_map/close/pallas_call | solution.py:52
  61.6 15.1 %feed_up.1 = (bf16[512,2048]{1,0:T(8,128)(2,1)}, bf16[512,2048]{1,0:T(8,128)(2,1)}, bf16[1024,2048]{1,0:T(8,128)(2,1)S(1)}, bf16[8,128,512]{2,1,0:T(8,128)(2,1)S...) custom-call(s32[2]{0:T(128)S(1)} %pad_add_fusion.place_ref, ...), custom_call_target="tpu_custom_call" | custom-call | tf_op jit(solution)/shard_map/feed_up/pallas_call | solution.py:52
  76.7 1.6 collective-permute-start.9
  78.8 21.4 %feed_back.1 = (bf16[1024,1024]{1,0:T(8,128)(2,1)}, f32[1,2048]{1,0:T(1,128)}, bf16[8,64,1024]{2,1,0:T(8,128)(2,1)}, bf16[8,64,1024]{2,1,0:T(8,128)(2,1)S(1)}, b...) custom-call(s32[2]{0:T(128)S(1)} %pad_add_fusion.place_ref, ...), custom_call_target="tpu_custom_call" | custom-call | tf_op jit(solution)/shard_map/feed_back/pallas_call | solution.py:52
  100.5 1.8 collective-permute-start.14
  103.2 2.0 step.6
  105.2 1.6 collective-permute-start.12
  106.8 9.7 %middle_back.1 = (bf16[1024,1024]{1,0:T(8,128)(2,1)S(1)}, f32[512,1024]{1,0:T(8,128)}, bf16[1024,512]{1,0:T(8,128)(2,1)S(1)}, f32[8,1024]{1,0:T(8,128)}) custom-call(s32[2]{0:T(128)S(1)} %pad_add_fusion.place_ref, f32[1024,1024]{1,0:T(8,128)} %get-tuple-element.124.refs_0_, bf16[1024,1024]{1,0:T(8,128)(2,1)S(1)} %get-tuple-element.119.refs_6_.refs_1_, ...), custom_call_target="tpu_custom_call" | custom-call | tf_op jit(solution)/shard_map/middle_back/pallas_call | solution.py:52
  116.5 10.3 %feed_down.1 = (bf16[256,1024]{1,0:T(8,128)(2,1)}, bf16[256,1024]{1,0:T(8,128)(2,1)}) custom-call(s32[2]{0:T(128)S(1)} %pad_add_fusion.place_ref, f32[512,1024]{1,0:T(8,128)} %get-tuple-element.120.refs_0_, f32[8,1024]{1,0:T(8,128)} %convert_element_type.13.refs_2_.refs_1_, bf16[512,2048]{1,0:T(8,128)(2,1)} %get-tuple-element.122.refs_2_, ...), custom_call_target="tpu_custom_call" | custom-call | tf_op jit(solution)/shard_map/feed_down/pallas_call | solution.py:52
  127.3 20.0 %attend_back.2 = (bf16[512,768]{1,0:T(8,128)(2,1)}, bf16[512,768]{1,0:T(8,128)(2,1)}, bf16[8,64,640]{2,1,0:T(8,128)(2,1)}, bf16[8,64,640]{2,1,0:T(8,128)(2,1)S(1...) custom-call(s32[2]{0:T(128)S(1)} %pad_add_fusion.place_ref, ...), custom_call_target="tpu_custom_call" | custom-call | tf_op jit(solution)/shard_map/attend_back/pallas_call | solution.py:52
  147.3 1.3 collective-permute-start.19
  148.6 1.5 collective-permute-start.20
  150.1 2.6 %join.2.refs_6_ = bf16[2,1,256,1024]{3,2,1,0:T(8,128)(2,1)} custom-call(s32[2]{0:T(128)S(1)} %pad_add_fusion.place_ref, bf16[256,1024]{1,0:T(8,128)(2,1)} %get-tuple-element.134.refs_12_.refs_0_, bf16[256,1024]{1,0:T(8,128)(2,1)S(1)} %collective-permute-done.11.refs_1_, bf16[512,768]{1,0:T(8,128)(2,1)} %get-tuple-element.139.refs_2_.refs_9_), custom_call_target="tpu_custom_call" | custom-call | tf_op jit(solution)/shard_map/join/pallas_call | solution.py:52
  152.7 3.7 %step.7 = (bf16[2,256,512]{2,1,0:T(8,128)(2,1)}, bf16[2,256,512]{2,1,0:T(8,128)(2,1)S(1)}, bf16[4,64,1024]{2,1,0:T(8,128)(2,1)}, bf16[4,64,1024]{2,1,0:T(8,128)(...) custom-call(s32[2]{0:T(128)S(1)} %pad_add_fusion.place_ref, ...), custom_call_target="tpu_custom_call" | custom-call | flops 23000000512 | tf_op jit(solution)/shard_map/step/pallas_call | solution.py:52
  157.7 2.6 %collective-permute-start.18 = (bf16[2,256,512]{2,1,0:T(8,128)(2,1)S(1)}, bf16[2,256,512]{2,1,0:T(8,128)(2,1)S(1)}, u32[]{:S(2)}, u32[]{:S(2)}) collective-permute-start(bf16[2,256,512]{2,1,0:T(8,128)(2,1)S(1)} %get-tuple-element.156), channel_id=1, source_target_pairs={{0,16},{4,20},{8,24},{12,28},{16,0},{20,4},{24,8},{28,12},{1,17},{... | collective-permute-start | bytes 1572872 | tf_op jit(solution)/shard_map/ppermute | solution.py:1228
  160.3 19.2 %attend_back.3 = (bf16[512,1536]{1,0:T(8,128)(2,1)}, bf16[512,1536]{1,0:T(8,128)(2,1)}, bf16[8,64,384]{2,1,0:T(8,128)(2,1)}, bf16[8,64,384]{2,1,0:T(8,128)(2,1)S...) custom-call(s32[2]{0:T(128)S(1)} %pad_add_fusion.place_ref, ...), custom_call_target="tpu_custom_call" | custom-call | tf_op jit(solution)/shard_map/attend_back/pallas_call | solution.py:52
  179.6 2.6 %collective-permute-done.18.refs_5_ = bf16[2,256,512]{2,1,0:T(8,128)(2,1)S(1)} collective-permute-done((bf16[2,256,512]{2,1,0:T(8,128)(2,1)S(1)}, bf16[2,256,512]{2,1,0:T(8,128)(2,1)S(1)}, u32[]{:S(2)}, u32[]{:S(2)}) %collective-permute-start.18) | collective-permute-done | bytes 524320 | tf_op jit(solution)/shard_map/ppermute | solution.py:1228
  182.2 3.9 %step.8 = (bf16[2,128,1024]{2,1,0:T(8,128)(2,1)}, bf16[2,128,1024]{2,1,0:T(8,128)(2,1)S(1)}, bf16[1,128,512]{2,1,0:T(8,128)(2,1)}, bf16[1,128,512]{2,1,0:T(8,128...) custom-call(s32[2]{0:T(128)S(1)} %pad_add_fusion.place_ref, ...), custom_call_target="tpu_custom_call" | custom-call | flops 23000000512 | tf_op jit(solution)/shard_map/step/pallas_call | solution.py:52
  186.9 1.5 collective-permute-start.22
  188.4 1.5 collective-permute-start.23
  190.9 10.6 %hidden_back.1 = (bf16[256,1024]{1,0:T(8,128)(2,1)}, bf16[256,1024]{1,0:T(8,128)(2,1)}, f32[8,1024]{1,0:T(8,128)}) custom-call(s32[2]{0:T(128)S(1)} %pad_add_fusion.place_ref, bf16[2,2,256,1024]{3,2,1,0:T(8,128)(2,1)} %bitcast.28, f32[512,1024]{1,0:T(8,128)} %get-tuple-element.140.refs_1_, f32[8,1024]{1,0:T(8,128)} %convert_element_type.13.refs_2_.refs_1_, ...), custom_call_target="tpu_custom_call" | custom-call | tf_op jit(solution)/shard_map/hidden_back/pallas_call | solution.py:52
  201.5 4.3 %collective-permute-done.25.refs_7_ = bf16[4,64,640]{2,1,0:T(8,128)(2,1)S(1)} collective-permute-done((bf16[4,64,640]{2,1,0:T(8,128)(2,1)S(1)}, bf16[4,64,640]{2,1,0:T(8,128)(2,1)S(1)}, u32[]{:S(2)}, u32[]{:S(2)}) %collective-permute-start.25) | collective-permute-done | bytes 327712 | tf_op jit(solution)/shard_map/ppermute | solution.py:1194
  205.9 3.2 %step.9 = (bf16[4,64,384]{2,1,0:T(8,128)(2,1)}, bf16[4,64,384]{2,1,0:T(8,128)(2,1)S(1)}, bf16[4,64,384]{2,1,0:T(8,128)(2,1)}, bf16[4,64,384]{2,1,0:T(8,128)(2,1)...) custom-call(s32[2]{0:T(128)S(1)} %pad_add_fusion.place_ref, ...), custom_call_target="tpu_custom_call" | custom-call | flops 23000000512 | tf_op jit(solution)/shard_map/step/pallas_call | solution.py:52
  209.3 3.4 %collective-permute-start.29 = (bf16[1,128,1024]{2,1,0:T(8,128)(2,1)S(1)}, bf16[1,128,1024]{2,1,0:T(8,128)(2,1)S(1)}, u32[]{:S(2)}, u32[]{:S(2)}) collective-permute-start(bf16[1,128,1024]{2,1,0:T(8,128)(2,1)S(1)} %get-tuple-element.178), channel_id=1, source_target_pairs={{0,16},{4,20},{8,24},{12,28},{16,0},{20,4},{24,8},{28,12},{1,17},{... | collective-permute-start | bytes 786440 | tf_op jit(solution)/shard_map/ppermute | solution.py:1228
  212.7 1.5 collective-permute-start.27
  215.5 5.1 %collective-permute-done.27.refs_1_ = bf16[4,64,384]{2,1,0:T(8,128)(2,1)S(1)} collective-permute-done((bf16[4,64,384]{2,1,0:T(8,128)(2,1)S(1)}, bf16[4,64,384]{2,1,0:T(8,128)(2,1)S(1)}, u32[]{:S(2)}, u32[]{:S(2)}) %collective-permute-start.27) | collective-permute-done | bytes 196640 | tf_op jit(solution)/shard_map/ppermute | solution.py:1194
  220.7 2.2 collective-permute-done.30.refs_7_
  222.8 2.8 %step.10 = (bf16[2,128,384]{2,1,0:T(8,128)(2,1)}, bf16[2,128,384]{2,1,0:T(8,128)(2,1)S(1)}, f32[128,1024]{1,0:T(8,128)}, bf16[1,128,640]{2,1,0:T(8,128)(2,1)}, bf16[1,128,640]{2,1,0:T(8,128)(2,1)S(1)}) custom-call(s32[2]{0:T(128)S(1)} %pad_add_fusion.place_ref, bf16[4,64,384]{2,1,0:T(8,128)(2,1)} %get-tuple-element.173.refs_0_.refs_8_, ...), custom_call_target="tpu_custom_call" | custom-call | flops 23000000512 | tf_op jit(solution)/shard_map/step/pallas_call | solution.py:52
  225.6 3.4 %collective-permute-start.34 = (bf16[2,128,384]{2,1,0:T(8,128)(2,1)S(1)}, bf16[2,128,384]{2,1,0:T(8,128)(2,1)S(1)}, u32[]{:S(2)}, u32[]{:S(2)}) collective-permute-start(bf16[2,128,384]{2,1,0:T(8,128)(2,1)S(1)} %get-tuple-element.191), channel_id=1, source_target_pairs={{0,8},{4,12},{8,0},{12,4},{16,24},{20,28},{24,16},{28,20},{1,9},{5... | collective-permute-start | bytes 589832 | tf_op jit(solution)/shard_map/ppermute | solution.py:1228
  229.1 1.5 collective-permute-start.31
  231.5 1.4 collective-permute-start.33
  232.8 2.6 %join.3.refs_2_ = bf16[2,1,256,1024]{3,2,1,0:T(8,128)(2,1)} custom-call(s32[2]{0:T(128)S(1)} %pad_add_fusion.place_ref, bf16[256,1024]{1,0:T(8,128)(2,1)} %get-tuple-element.162.refs_10_.refs_0_, bf16[256,1024]{1,0:T(8,128)(2,1)S(1)} %collective-permute-done.21.refs_1_, bf16[2,128,384]{2,1,0:T(8,128)(2,1)} %get-tuple-element.181.refs_2_.refs_0_), custom_call_target="tpu_custom_call" | custom-call | tf_op jit(solution)/shard_map/join/pallas_call | solution.py:52
  235.5 2.1 step.11
  237.6 1.6 collective-permute-start.35
  239.9 2.6 %all-to-all-start = ((f32[32,1,384]{2,1,0:T(1,128)}), f32[32,1,384]{2,1,0:T(1,128)S(1)}, u32[]{:S(2)}, u32[]{:S(2)}) async-start(f32[32,1,384]{2,1,0:T(1,128)} %copy.43), calls=%async_computation | async-start | bytes 98304 | tf_op jit(solution)/shard_map/all_to_all | solution.py:1455
  243.6 3.0 %part_rows.1 = (f32[32,4096]{1,0:T(8,128)}, bf16[32,4096]{1,0:T(8,128)(2,1)}, f32[128,1024]{1,0:T(8,128)}) custom-call(s32[2]{0:T(128)S(1)} %pad_add_fusion.place_ref, bf16[1,128,512]{2,1,0:T(8,128)(2,1)} %get-tuple-element.184.refs_0_, bf16[1,128,512]{2,1,0:T(8,128)(2,1)S(1)} %collective-permute-done.31.refs_1_, ...), custom_call_target="tpu_custom_call" | custom-call | tf_op jit(solution)/shard_map/part_rows/pallas_call | solution.py:52
  246.6 3.2 %all-to-all-done = f32[32,1,384]{2,1,0:T(1,128)S(1)} async-done(((f32[32,1,384]{2,1,0:T(1,128)}), f32[32,1,384]{2,1,0:T(1,128)S(1)}, u32[]{:S(2)}, u32[]{:S(2)}) %all-to-all-start) | async-done | bytes 49184 | tf_op jit(solution)/shard_map/all_to_all | solution.py:1455
  251.7 2.6 %emit.1 = (f32[32,4096]{1,0:T(8,128)}, f32[32,1024]{1,0:T(8,128)}, f32[32,3072]{1,0:T(8,128)}) custom-call(s32[2]{0:T(128)S(1)} %pad_add_fusion.place_ref, f32[32,4096]{1,0:T(8,128)} %get-tuple-element.194.refs_0_, bf16[32,4096]{1,0:T(8,128)(2,1)S(1)} %collective-permute-done.36.refs_1_), custom_call_target="tpu_custom_call" | custom-call | tf_op jit(solution)/shard_map/emit/pallas_call | solution.py:52
  (116 shorter events, 17.8 us)
Async XLA Ops:
  0.6 46.9 %copy-start = (bf16[4096]{0:T(1024)(128)(2,1)S(1)}, bf16[4096]{0:T(1024)(128)(2,1)}, u32[]{:S(2)}) copy-start(bf16[4096]{0:T(1024)(128)(2,1)} %param.27) | copy-start | bytes 24580
  0.7 4.5 %copy-start.11 = (bf16[1024]{0:T(1024)(128)(2,1)S(1)}, bf16[1024]{0:T(1024)(128)(2,1)}, u32[]{:S(2)}) copy-start(bf16[1024]{0:T(1024)(128)(2,1)} %param.24) | copy-start | bytes 6148
  0.7 4.5 %copy-start.12 = (bf16[1024]{0:T(1024)(128)(2,1)S(1)}, bf16[1024]{0:T(1024)(128)(2,1)}, u32[]{:S(2)}) copy-start(bf16[1024]{0:T(1024)(128)(2,1)} %param.25) | copy-start | bytes 6148
  0.7 4.5 %copy-start.13 = (bf16[1024]{0:T(1024)(128)(2,1)S(1)}, bf16[1024]{0:T(1024)(128)(2,1)}, u32[]{:S(2)}) copy-start(bf16[1024]{0:T(1024)(128)(2,1)} %param.29) | copy-start | bytes 6148
  2.0 4.0 %collective-permute-start = (bf16[256,1024]{1,0:T(8,128)(2,1)S(1)}, bf16[256,1024]{1,0:T(8,128)(2,1)S(1)}, u32[]{:S(2)}, u32[]{:S(2)}) collective-permute-start(bf16[256,1024]{1,0:T(8,128)(2,1)S(1)} %get-tuple-element.201.refs_0_), channel_id=1, source_target_pairs={{0,1},{1,0},{2,3},{3,2},{4,5},{5,4},{6,7},{7,6},{8,9},{9,8},{10,11... | collective-permute-start | bytes 1572872 | tf_op jit(solution)/shard_map/ppermute | solution.py:1200
  2.6 15.1 %collective-permute-start.1 = (bf16[256,1024]{1,0:T(8,128)(2,1)S(1)}, bf16[256,1024]{1,0:T(8,128)(2,1)S(1)}, u32[]{:S(2)}, u32[]{:S(2)}) collective-permute-start(bf16[256,1024]{1,0:T(8,128)(2,1)S(1)} %get-tuple-element.200), channel_id=1, source_target_pairs={{0,2},{1,3},{2,0},{3,1},{4,6},{5,7},{6,4},{7,5},{8,10},{9,11},{10,... | collective-permute-start | bytes 1572872 | tf_op jit(solution)/shard_map/ppermute | solution.py:1194
  12.6 6.6 %copy-start.14 = (s32[2,1,16]{2,1,0:T(1,128)S(1)}, s32[2,1,16]{2,1,0:T(1,128)}, u32[]{:S(2)}) copy-start(s32[2,1,16]{2,1,0:T(1,128)} %param.17) | copy-start | bytes 388
  19.0 2.2 collective-permute-start.2
  19.5 10.3 %copy-start.5 = (s32[1024]{0:T(1024)}, s32[1024]{0:T(1024)S(1)}, u32[]{:S(2)}) copy-start(s32[1024]{0:T(1024)S(1)} %convert_reduce_fusion) | copy-start | bytes 12292
  28.0 19.4 %collective-permute-start.5 = (bf16[256,1024]{1,0:T(8,128)(2,1)}, bf16[256,1024]{1,0:T(8,128)(2,1)S(1)}, u32[]{:S(2)}, u32[]{:S(2)}) collective-permute-start(bf16[256,1024]{1,0:T(8,128)(2,1)} %get-tuple-element.118), channel_id=1, source_target_pairs={{0,2},{1,3},{2,0},{3,1},{4,6},{5,7},{6,4},{7,5},{8,10},{9,11},{10,... | collective-permute-start | bytes 1572872 | tf_op jit(solution)/shard_map/ppermute | solution.py:1194
  30.8 16.1 %copy-start.4 = (bf16[256,1024]{1,0:T(8,128)(2,1)S(1)}, bf16[256,1024]{1,0:T(8,128)(2,1)}, u32[]{:S(2)}) copy-start(bf16[256,1024]{1,0:T(8,128)(2,1)} %get-tuple-element.117.refs_0_) | copy-start | bytes 1572868
  46.9 6.8 %collective-permute-start.3 = (bf16[1024,512]{1,0:T(8,128)(2,1)}, bf16[1024,512]{1,0:T(8,128)(2,1)S(1)}, u32[]{:S(2)}, u32[]{:S(2)}) collective-permute-start(bf16[1024,512]{1,0:T(8,128)(2,1)} %get-tuple-element.116.refs_4_.refs_2_.refs_10_), channel_id=1, source_target_pairs={{0,1},{1,0},{2,3},{3,2},{4,5},{5,4},{6,7},{7,6},{8,9},{9,8},{10,11... | collective-permute-start | bytes 3145736 | tf_op jit(solution)/shard_map/ppermute | solution.py:1200
  46.9 3.4 %collective-permute-start.4 = (bf16[256,1024]{1,0:T(8,128)(2,1)S(1)}, bf16[256,1024]{1,0:T(8,128)(2,1)S(1)}, u32[]{:S(2)}, u32[]{:S(2)}) collective-permute-start(bf16[256,1024]{1,0:T(8,128)(2,1)S(1)} %copy-done.4), channel_id=1, source_target_pairs={{0,1},{1,0},{2,3},{3,2},{4,5},{5,4},{6,7},{7,6},{8,9},{9,8},{10,11... | collective-permute-start | bytes 1572872 | tf_op jit(solution)/shard_map/ppermute | solution.py:1200
  47.4 3.6 %collective-permute-start.6 = (bf16[256,1024]{1,0:T(8,128)(2,1)S(1)}, bf16[256,1024]{1,0:T(8,128)(2,1)S(1)}, u32[]{:S(2)}, u32[]{:S(2)}) collective-permute-start(bf16[256,1024]{1,0:T(8,128)(2,1)S(1)} %collective-permute-done.5.refs_2_), channel_id=1, source_target_pairs={{0,1},{1,0},{2,3},{3,2},{4,5},{5,4},{6,7},{7,6},{8,9},{9,8},{10,11... | collective-permute-start | bytes 1572872 | tf_op jit(solution)/shard_map/ppermute | solution.py:1200
  76.7 25.5 %collective-permute-start.9 = (bf16[8,128,512]{2,1,0:T(8,128)(2,1)S(1)}, bf16[8,128,512]{2,1,0:T(8,128)(2,1)S(1)}, u32[]{:S(2)}, u32[]{:S(2)}) collective-permute-start(bf16[8,128,512]{2,1,0:T(8,128)(2,1)S(1)} %get-tuple-element.129), channel_id=1, source_target_pairs={{0,4},{4,0},{8,12},{12,8},{16,20},{20,16},{24,28},{28,24},{1,5},{5... | collective-permute-start | bytes 3145736 | tf_op jit(solution)/shard_map/ppermute | solution.py:1228
  78.3 25.0 %collective-permute-start.10 = (bf16[8,128,512]{2,1,0:T(8,128)(2,1)S(1)}, bf16[8,128,512]{2,1,0:T(8,128)(2,1)S(1)}, u32[]{:S(2)}, u32[]{:S(2)}) collective-permute-start(bf16[8,128,512]{2,1,0:T(8,128)(2,1)S(1)} %get-tuple-element.131), channel_id=1, source_target_pairs={{0,2},{1,3},{2,0},{3,1},{4,6},{5,7},{6,4},{7,5},{8,10},{9,11},{10,... | collective-permute-start | bytes 3145736 | tf_op jit(solution)/shard_map/ppermute | solution.py:1194
  78.8 37.7 %collective-permute-start.7 = (bf16[512,2048]{1,0:T(8,128)(2,1)}, bf16[512,2048]{1,0:T(8,128)(2,1)S(1)}, u32[]{:S(2)}, u32[]{:S(2)}) collective-permute-start(bf16[512,2048]{1,0:T(8,128)(2,1)} %get-tuple-element.123), channel_id=1, source_target_pairs={{0,1},{1,0},{2,3},{3,2},{4,5},{5,4},{6,7},{7,6},{8,9},{9,8},{10,11... | collective-permute-start | bytes 6291464 | tf_op jit(solution)/shard_map/ppermute | solution.py:1200
  100.2 52.6 %collective-permute-start.13 = (bf16[8,64,1024]{2,1,0:T(8,128)(2,1)S(1)}, bf16[8,64,1024]{2,1,0:T(8,128)(2,1)S(1)}, u32[]{:S(2)}, u32[]{:S(2)}) collective-permute-start(bf16[8,64,1024]{2,1,0:T(8,128)(2,1)S(1)} %get-tuple-element.144), channel_id=1, source_target_pairs={{0,4},{4,0},{8,12},{12,8},{16,20},{20,16},{24,28},{28,24},{1,5},{5... | collective-permute-start | bytes 3145736 | tf_op jit(solution)/shard_map/ppermute | solution.py:1228
  100.5 52.3 %collective-permute-start.14 = (bf16[8,64,1024]{2,1,0:T(8,128)(2,1)S(1)}, bf16[8,64,1024]{2,1,0:T(8,128)(2,1)S(1)}, u32[]{:S(2)}, u32[]{:S(2)}) collective-permute-start(bf16[8,64,1024]{2,1,0:T(8,128)(2,1)S(1)} %get-tuple-element.146), channel_id=1, source_target_pairs={{0,2},{1,3},{2,0},{3,1},{4,6},{5,7},{6,4},{7,5},{8,10},{9,11},{10,... | collective-permute-start | bytes 3145736 | tf_op jit(solution)/shard_map/ppermute | solution.py:1194
  102.2 4.6 %collective-permute-start.8 = (bf16[1024,1024]{1,0:T(8,128)(2,1)}, bf16[1024,1024]{1,0:T(8,128)(2,1)S(1)}, u32[]{:S(2)}, u32[]{:S(2)}) collective-permute-start(bf16[1024,1024]{1,0:T(8,128)(2,1)} %get-tuple-element.128.refs_4_), channel_id=1, source_target_pairs={{0,1},{1,0},{2,3},{3,2},{4,5},{5,4},{6,7},{7,6},{8,9},{9,8},{10,11... | collective-permute-start | bytes 6291464 | tf_op jit(solution)/shard_map/ppermute | solution.py:1200
  105.2 47.5 %collective-permute-start.12 = (bf16[4,256,512]{2,1,0:T(8,128)(2,1)S(1)}, bf16[4,256,512]{2,1,0:T(8,128)(2,1)S(1)}, u32[]{:S(2)}, u32[]{:S(2)}) collective-permute-start(bf16[4,256,512]{2,1,0:T(8,128)(2,1)S(1)} %get-tuple-element.142), channel_id=1, source_target_pairs={{0,8},{4,12},{8,0},{12,4},{16,24},{20,28},{24,16},{28,20},{1,9},{5... | collective-permute-start | bytes 3145736 | tf_op jit(solution)/shard_map/ppermute | solution.py:1228
  126.8 21.8 %collective-permute-start.11 = (bf16[256,1024]{1,0:T(8,128)(2,1)}, bf16[256,1024]{1,0:T(8,128)(2,1)S(1)}, u32[]{:S(2)}, u32[]{:S(2)}) collective-permute-start(bf16[256,1024]{1,0:T(8,128)(2,1)} %get-tuple-element.135), channel_id=1, source_target_pairs={{0,2},{1,3},{2,0},{3,1},{4,6},{5,7},{6,4},{7,5},{8,10},{9,11},{10,... | collective-permute-start | bytes 1572872 | tf_op jit(solution)/shard_map/ppermute | solution.py:1194
  147.3 32.2 %collective-permute-start.19 = (bf16[8,64,640]{2,1,0:T(8,128)(2,1)S(1)}, bf16[8,64,640]{2,1,0:T(8,128)(2,1)S(1)}, u32[]{:S(2)}, u32[]{:S(2)}) collective-permute-start(bf16[8,64,640]{2,1,0:T(8,128)(2,1)S(1)} %get-tuple-element.158), channel_id=1, source_target_pairs={{0,4},{4,0},{8,12},{12,8},{16,20},{20,16},{24,28},{28,24},{1,5},{5... | collective-permute-start | bytes 1966088 | tf_op jit(solution)/shard_map/ppermute | solution.py:1228
  148.6 31.0 %collective-permute-start.20 = (bf16[8,64,640]{2,1,0:T(8,128)(2,1)S(1)}, bf16[8,64,640]{2,1,0:T(8,128)(2,1)S(1)}, u32[]{:S(2)}, u32[]{:S(2)}) collective-permute-start(bf16[8,64,640]{2,1,0:T(8,128)(2,1)S(1)} %get-tuple-element.160), channel_id=1, source_target_pairs={{0,2},{1,3},{2,0},{3,1},{4,6},{5,7},{6,4},{7,5},{8,10},{9,11},{10,... | collective-permute-start | bytes 1966088 | tf_op jit(solution)/shard_map/ppermute | solution.py:1194
  156.4 23.1 %collective-permute-start.16 = (bf16[4,64,1024]{2,1,0:T(8,128)(2,1)S(1)}, bf16[4,64,1024]{2,1,0:T(8,128)(2,1)S(1)}, u32[]{:S(2)}, u32[]{:S(2)}) collective-permute-start(bf16[4,64,1024]{2,1,0:T(8,128)(2,1)S(1)} %get-tuple-element.153), channel_id=1, source_target_pairs={{0,2},{1,3},{2,0},{3,1},{4,6},{5,7},{6,4},{7,5},{8,10},{9,11},{10,... | collective-permute-start | bytes 1572872 | tf_op jit(solution)/shard_map/ppermute | solution.py:1194
  157.0 22.6 %collective-permute-start.17 = (bf16[4,64,1024]{2,1,0:T(8,128)(2,1)S(1)}, bf16[4,64,1024]{2,1,0:T(8,128)(2,1)S(1)}, u32[]{:S(2)}, u32[]{:S(2)}) collective-permute-start(bf16[4,64,1024]{2,1,0:T(8,128)(2,1)S(1)} %get-tuple-element.155), channel_id=1, source_target_pairs={{0,4},{4,0},{8,12},{12,8},{16,20},{20,16},{24,28},{28,24},{1,5},{5... | collective-permute-start | bytes 1572872 | tf_op jit(solution)/shard_map/ppermute | solution.py:1228
  157.7 24.5 %collective-permute-start.18 = (bf16[2,256,512]{2,1,0:T(8,128)(2,1)S(1)}, bf16[2,256,512]{2,1,0:T(8,128)(2,1)S(1)}, u32[]{:S(2)}, u32[]{:S(2)}) collective-permute-start(bf16[2,256,512]{2,1,0:T(8,128)(2,1)S(1)} %get-tuple-element.156), channel_id=1, source_target_pairs={{0,16},{4,20},{8,24},{12,28},{16,0},{20,4},{24,8},{28,12},{1,17},{... | collective-permute-start | bytes 1572872 | tf_op jit(solution)/shard_map/ppermute | solution.py:1228
  179.5 10.9 %collective-permute-start.15 = (bf16[512,1536]{1,0:T(8,128)(2,1)}, bf16[512,1536]{1,0:T(8,128)(2,1)S(1)}, u32[]{:S(2)}, u32[]{:S(2)}) collective-permute-start(bf16[512,1536]{1,0:T(8,128)(2,1)} %get-tuple-element.149), channel_id=1, source_target_pairs={{0,1},{1,0},{2,3},{3,2},{4,5},{5,4},{6,7},{7,6},{8,9},{9,8},{10,11... | collective-permute-start | bytes 4718600 | tf_op jit(solution)/shard_map/ppermute | solution.py:1200
  186.1 19.7 %collective-permute-start.24 = (bf16[2,128,1024]{2,1,0:T(8,128)(2,1)S(1)}, bf16[2,128,1024]{2,1,0:T(8,128)(2,1)S(1)}, u32[]{:S(2)}, u32[]{:S(2)}) collective-permute-start(bf16[2,128,1024]{2,1,0:T(8,128)(2,1)S(1)} %get-tuple-element.168), channel_id=1, source_target_pairs={{0,8},{4,12},{8,0},{12,4},{16,24},{20,28},{24,16},{28,20},{1,9},{5... | collective-permute-start | bytes 1572872 | tf_op jit(solution)/shard_map/ppermute | solution.py:1228
  186.9 14.7 %collective-permute-start.22 = (bf16[8,64,384]{2,1,0:T(8,128)(2,1)S(1)}, bf16[8,64,384]{2,1,0:T(8,128)(2,1)S(1)}, u32[]{:S(2)}, u32[]{:S(2)}) collective-permute-start(bf16[8,64,384]{2,1,0:T(8,128)(2,1)S(1)} %get-tuple-element.165), channel_id=1, source_target_pairs={{0,4},{4,0},{8,12},{12,8},{16,20},{20,16},{24,28},{28,24},{1,5},{5... | collective-permute-start | bytes 1179656 | tf_op jit(solution)/shard_map/ppermute | solution.py:1228
  188.4 13.2 %collective-permute-start.23 = (bf16[8,64,384]{2,1,0:T(8,128)(2,1)S(1)}, bf16[8,64,384]{2,1,0:T(8,128)(2,1)S(1)}, u32[]{:S(2)}, u32[]{:S(2)}) collective-permute-start(bf16[8,64,384]{2,1,0:T(8,128)(2,1)S(1)} %get-tuple-element.167), channel_id=1, source_target_pairs={{0,2},{1,3},{2,0},{3,1},{4,6},{5,7},{6,4},{7,5},{8,10},{9,11},{10,... | collective-permute-start | bytes 1179656 | tf_op jit(solution)/shard_map/ppermute | solution.py:1194
  189.9 16.0 %collective-permute-start.25 = (bf16[4,64,640]{2,1,0:T(8,128)(2,1)S(1)}, bf16[4,64,640]{2,1,0:T(8,128)(2,1)S(1)}, u32[]{:S(2)}, u32[]{:S(2)}) collective-permute-start(bf16[4,64,640]{2,1,0:T(8,128)(2,1)S(1)} %get-tuple-element.170), channel_id=1, source_target_pairs={{0,2},{1,3},{2,0},{3,1},{4,6},{5,7},{6,4},{7,5},{8,10},{9,11},{10,... | collective-permute-start | bytes 983048 | tf_op jit(solution)/shard_map/ppermute | solution.py:1194
  190.4 15.5 %collective-permute-start.26 = (bf16[4,64,640]{2,1,0:T(8,128)(2,1)S(1)}, bf16[4,64,640]{2,1,0:T(8,128)(2,1)S(1)}, u32[]{:S(2)}, u32[]{:S(2)}) collective-permute-start(bf16[4,64,640]{2,1,0:T(8,128)(2,1)S(1)} %get-tuple-element.172), channel_id=1, source_target_pairs={{0,4},{4,0},{8,12},{12,8},{16,20},{20,16},{24,28},{28,24},{1,5},{5... | collective-permute-start | bytes 983048 | tf_op jit(solution)/shard_map/ppermute | solution.py:1228
  209.1 13.8 %collective-permute-start.30 = (bf16[2,128,640]{2,1,0:T(8,128)(2,1)S(1)}, bf16[2,128,640]{2,1,0:T(8,128)(2,1)S(1)}, u32[]{:S(2)}, u32[]{:S(2)}) collective-permute-start(bf16[2,128,640]{2,1,0:T(8,128)(2,1)S(1)} %get-tuple-element.180), channel_id=1, source_target_pairs={{0,8},{4,12},{8,0},{12,4},{16,24},{20,28},{24,16},{28,20},{1,9},{5... | collective-permute-start | bytes 983048 | tf_op jit(solution)/shard_map/ppermute | solution.py:1228
  209.3 11.3 %collective-permute-start.29 = (bf16[1,128,1024]{2,1,0:T(8,128)(2,1)S(1)}, bf16[1,128,1024]{2,1,0:T(8,128)(2,1)S(1)}, u32[]{:S(2)}, u32[]{:S(2)}) collective-permute-start(bf16[1,128,1024]{2,1,0:T(8,128)(2,1)S(1)} %get-tuple-element.178), channel_id=1, source_target_pairs={{0,16},{4,20},{8,24},{12,28},{16,0},{20,4},{24,8},{28,12},{1,17},{... | collective-permute-start | bytes 786440 | tf_op jit(solution)/shard_map/ppermute | solution.py:1228
  212.7 7.8 %collective-permute-start.27 = (bf16[4,64,384]{2,1,0:T(8,128)(2,1)S(1)}, bf16[4,64,384]{2,1,0:T(8,128)(2,1)S(1)}, u32[]{:S(2)}, u32[]{:S(2)}) collective-permute-start(bf16[4,64,384]{2,1,0:T(8,128)(2,1)S(1)} %get-tuple-element.174), channel_id=1, source_target_pairs={{0,2},{1,3},{2,0},{3,1},{4,6},{5,7},{6,4},{7,5},{8,10},{9,11},{10,... | collective-permute-start | bytes 589832 | tf_op jit(solution)/shard_map/ppermute | solution.py:1194
  214.2 6.3 %collective-permute-start.28 = (bf16[4,64,384]{2,1,0:T(8,128)(2,1)S(1)}, bf16[4,64,384]{2,1,0:T(8,128)(2,1)S(1)}, u32[]{:S(2)}, u32[]{:S(2)}) collective-permute-start(bf16[4,64,384]{2,1,0:T(8,128)(2,1)S(1)} %get-tuple-element.176), channel_id=1, source_target_pairs={{0,4},{4,0},{8,12},{12,8},{16,20},{20,16},{24,28},{28,24},{1,5},{5... | collective-permute-start | bytes 589832 | tf_op jit(solution)/shard_map/ppermute | solution.py:1228
  214.9 17.9 %collective-permute-start.21 = (bf16[256,1024]{1,0:T(8,128)(2,1)}, bf16[256,1024]{1,0:T(8,128)(2,1)S(1)}, u32[]{:S(2)}, u32[]{:S(2)}) collective-permute-start(bf16[256,1024]{1,0:T(8,128)(2,1)} %get-tuple-element.163), channel_id=1, source_target_pairs={{0,2},{1,3},{2,0},{3,1},{4,6},{5,7},{6,4},{7,5},{8,10},{9,11},{10,... | collective-permute-start | bytes 1572872 | tf_op jit(solution)/shard_map/ppermute | solution.py:1194
  222.8 6.2 %copy-start.7 = (f32[1,2048]{1,0:T(1,128)S(1)}, f32[1,2048]{1,0:T(1,128)}, u32[]{:S(2)}) copy-start(f32[1,2048]{1,0:T(1,128)} %get-tuple-element.183) | copy-start | bytes 24580
  222.8 8.4 %copy-start.6 = (f32[8,1024]{1,0:T(8,128)S(1)}, f32[8,1024]{1,0:T(8,128)}, u32[]{:S(2)}) copy-start(f32[8,1024]{1,0:T(8,128)} %get-tuple-element.182) | copy-start | bytes 98308
  225.6 9.8 %collective-permute-start.34 = (bf16[2,128,384]{2,1,0:T(8,128)(2,1)S(1)}, bf16[2,128,384]{2,1,0:T(8,128)(2,1)S(1)}, u32[]{:S(2)}, u32[]{:S(2)}) collective-permute-start(bf16[2,128,384]{2,1,0:T(8,128)(2,1)S(1)} %get-tuple-element.191), channel_id=1, source_target_pairs={{0,8},{4,12},{8,0},{12,4},{16,24},{20,28},{24,16},{28,20},{1,9},{5... | collective-permute-start | bytes 589832 | tf_op jit(solution)/shard_map/ppermute | solution.py:1228
  229.1 13.4 %collective-permute-start.31 = (bf16[1,128,512]{2,1,0:T(8,128)(2,1)S(1)}, bf16[1,128,512]{2,1,0:T(8,128)(2,1)S(1)}, u32[]{:S(2)}, u32[]{:S(2)}) collective-permute-start(bf16[1,128,512]{2,1,0:T(8,128)(2,1)S(1)} %get-tuple-element.185), channel_id=1, source_target_pairs={{0,2},{1,3},{2,0},{3,1},{4,6},{5,7},{6,4},{7,5},{8,10},{9,11},{10,... | collective-permute-start | bytes 393224 | tf_op jit(solution)/shard_map/ppermute | solution.py:1194
  230.6 11.9 %collective-permute-start.32 = (bf16[1,128,512]{2,1,0:T(8,128)(2,1)S(1)}, bf16[1,128,512]{2,1,0:T(8,128)(2,1)S(1)}, u32[]{:S(2)}, u32[]{:S(2)}) collective-permute-start(bf16[1,128,512]{2,1,0:T(8,128)(2,1)S(1)} %get-tuple-element.187), channel_id=1, source_target_pairs={{0,4},{4,0},{8,12},{12,8},{16,20},{20,16},{24,28},{28,24},{1,5},{5... | collective-permute-start | bytes 393224 | tf_op jit(solution)/shard_map/ppermute | solution.py:1228
  231.5 11.0 %collective-permute-start.33 = (bf16[1,128,640]{2,1,0:T(8,128)(2,1)S(1)}, bf16[1,128,640]{2,1,0:T(8,128)(2,1)S(1)}, u32[]{:S(2)}, u32[]{:S(2)}) collective-permute-start(bf16[1,128,640]{2,1,0:T(8,128)(2,1)S(1)} %get-tuple-element.190), channel_id=1, source_target_pairs={{0,16},{4,20},{8,24},{12,28},{16,0},{20,4},{24,8},{28,12},{1,17},{... | collective-permute-start | bytes 491528 | tf_op jit(solution)/shard_map/ppermute | solution.py:1228
  235.5 18.9 %copy-start.1 = (bf16[4096]{0:T(1024)(128)(2,1)S(1)}, bf16[4096]{0:T(1024)(128)(2,1)}, u32[]{:S(2)}) copy-start(bf16[4096]{0:T(1024)(128)(2,1)} %param.27) | copy-start | bytes 24580
  237.6 6.0 %collective-permute-start.35 = (bf16[1,128,384]{2,1,0:T(8,128)(2,1)S(1)}, bf16[1,128,384]{2,1,0:T(8,128)(2,1)S(1)}, u32[]{:S(2)}, u32[]{:S(2)}) collective-permute-start(bf16[1,128,384]{2,1,0:T(8,128)(2,1)S(1)} %get-tuple-element.193), channel_id=1, source_target_pairs={{0,16},{4,20},{8,24},{12,28},{16,0},{20,4},{24,8},{28,12},{1,17},{... | collective-permute-start | bytes 294920 | tf_op jit(solution)/shard_map/ppermute | solution.py:1228
  239.9 9.9 %all-to-all-start = ((f32[32,1,384]{2,1,0:T(1,128)}), f32[32,1,384]{2,1,0:T(1,128)S(1)}, u32[]{:S(2)}, u32[]{:S(2)}) async-start(f32[32,1,384]{2,1,0:T(1,128)} %copy.43), calls=%async_computation | async-start | bytes 98304 | tf_op jit(solution)/shard_map/all_to_all | solution.py:1455
  246.6 5.1 %collective-permute-start.36 = (bf16[32,4096]{1,0:T(8,128)(2,1)}, bf16[32,4096]{1,0:T(8,128)(2,1)S(1)}, u32[]{:S(2)}, u32[]{:S(2)}) collective-permute-start(bf16[32,4096]{1,0:T(8,128)(2,1)} %get-tuple-element.195), channel_id=1, source_target_pairs={{0,1},{1,0},{2,3},{3,2},{4,5},{5,4},{6,7},{7,6},{8,9},{9,8},{10,11... | collective-permute-start | bytes 786440 | tf_op jit(solution)/shard_map/ppermute | solution.py:1200
  (5 other events, 18.3 us)
